TPU v7x, 32 devices: a whole 2x2x4 slice. The times are simulated.
32 devices in a mesh: gx: 16 (over z, y, core), gy: 2 (over x).
Axes of the slice: x: 2, y: 2, z: 4, core: 2. Of those that a mesh axis runs over, the one named last changes fastest.
Arguments:
- latents: bfloat16 [16, 2, 1024, 128], P('gx', 'gy'), may hold values from -6 to 6
- mig_rows: int32 [16, 2, 4, 64], P('gx', 'gy'), may hold values from 0 to 1023, as said below
- mig_count: int32 [16, 2, 4], P('gx', 'gy'), may hold values from 0 to 64, as said below
- ghost_rows: int32 [16, 2, 8, 256], P('gx', 'gy'), may hold values from 0 to 1279, as said below
- ghost_count: int32 [16, 2, 8], P('gx', 'gy'), may hold values from 0 to 256, as said below
- neighbours: int32 [16, 2, 16, 80], P('gx', 'gy'), may hold values from -1 to 3327, as said below
- geometry: float32 [16, 2, 4, 16, 1280], P('gx', 'gy'), may hold values from -1 to 1
- edge_w: bfloat16 [2, 3, 128, 128], replicated, may hold values from -0.5 to 0.5
- node_w: bfloat16 [2, 3, 128, 128], replicated, may hold values from -0.5 to 0.5
- geo_w: float32 [2, 4, 128], replicated, may hold values from -3 to 3
- biases: float32 [2, 4, 128], replicated, may hold values from -3 to 3
- gains: float32 [2, 2, 128], replicated, may hold values from 0.1 to 1.9
Outputs:
- updated: bfloat16 [16, 2, 1280, 128], P('gx', 'gy')
Inputs may be any that keep to these rules, and one draw needn't show every extreme that they name: `mig_rows`: within one device all 256 entries are distinct rows. `mig_count`: zero towards the outside of the device grid; some device sends 64 rows in some direction. `ghost_rows`: rows of the device's block after migration. `ghost_count`: zero towards the outside of the device grid; some device fills all 256 slots towards some neighbour. `neighbours`: -1 marks an empty slot; other values are rows of the device's table. A slot of a tile is shared by the tile's 16 rows.
All inputs are finite; a program needn't handle non-finite values.
Results may differ from a plain program's by a relative error of at most 0.0061.
Values may be sent and summed in bfloat16 or wider, within the bound.
No kernel may reach another device: no remote copies, remote signals or barrier semaphores. Data moves between devices by JAX's collectives and lax.ppermute only.
A program may use at most 64 MiB of HBM per device.

v0:
```python
import math

import jax
import jax.numpy as jnp
from jax import lax
from jax.sharding import PartitionSpec as P


def shifted(value, axis, steps):
    count = lax.axis_size(axis)
    leading, last = (max(0, -steps), min(count, count - steps))
    return lax.ppermute(value, axis, [(source, source + steps) for source in range(leading, last)])


def layer_norm(values, gain):
    center = values - jnp.mean(values, axis=-1, keepdims=True)
    spread = jnp.mean(center * center, axis=-1, keepdims=True)
    return center * lax.rsqrt(spread + 1e-05) * gain


def select_rows(source, row_list, row_ok):
    picker = (
        row_list.reshape(-1)[:, None] == jnp.arange(source.shape[0])[None, :]
    ) & row_ok.reshape(-1)[:, None]
    chosen = jnp.dot(picker.astype(source.dtype), source, preferred_element_type=jnp.float32)
    return chosen.astype(source.dtype).reshape(row_list.shape + (source.shape[1],))


def body(
    latents,
    mig_rows,
    mig_count,
    ghost_rows,
    ghost_count,
    neighbours,
    geometry,
    edge_w,
    node_w,
    geo_w,
    biases,
    gains,
):
    owned = latents[0, 0]
    zero_value = jnp.zeros((), owned.dtype)
    leave_rows = mig_rows[0, 0]
    slot_total = leave_rows.shape[1]
    leave_ok = jnp.arange(slot_total)[None, :] < mig_count[0, 0][:, None]
    packets = select_rows(owned, leave_rows, leave_ok)
    matches = (jnp.arange(owned.shape[0])[:, None] == leave_rows.reshape(1, -1)) & leave_ok.reshape(
        1, -1
    )
    retained = jnp.where(jnp.any(matches, axis=1)[:, None], zero_value, owned)
    pieces = [retained]
    for offset, source in ((1, 1), (-1, 0)):
        pieces.append(shifted(packets[source], "gx", offset))
    for offset, source in ((1, 3), (-1, 2)):
        pieces.append(shifted(packets[source], "gy", offset))
    extended = jnp.concatenate(pieces, axis=0)
    ghost_list = ghost_rows[0, 0]
    ghost_slots = ghost_list.shape[1]
    ghost_ok = jnp.arange(ghost_slots)[None, :] < ghost_count[0, 0][:, None]
    tile_links = neighbours[0, 0]
    tile_size = tile_links.shape[0]
    edge_feats = geometry[0, 0]
    rows_total = extended.shape[0]
    width = extended.shape[1]
    block_rows = math.gcd(rows_total, 256)
    block_tiles = block_rows // tile_size
    block_count = rows_total // block_rows
    for layer in range(edge_w.shape[0]):
        outgoing = select_rows(extended, ghost_list, ghost_ok)
        sectioned = [outgoing[position] for position in range(8)]
        for offset, members in ((-1, (0, 1, 2)), (1, (5, 6, 7))):
            landed = shifted(jnp.stack([sectioned[member] for member in members]), "gx", offset)
            for position, member in enumerate(members):
                sectioned[member] = landed[position]
        for offset, members in ((-1, (0, 3, 5)), (1, (2, 4, 7))):
            landed = shifted(jnp.stack([sectioned[member] for member in members]), "gy", offset)
            for position, member in enumerate(members):
                sectioned[member] = landed[position]
        table = jnp.concatenate([extended] + sectioned, axis=0)
        edge_mats = edge_w[layer]
        node_mats = node_w[layer]
        geo_rows = geo_w[layer]
        bias_rows = biases[layer]
        gain_rows = gains[layer]
        joined_mat = edge_mats[:2].reshape(2 * width, width)

        def messages(block_index):
            row_start = block_index * block_rows
            link_part = lax.dynamic_slice_in_dim(
                tile_links, block_index * block_tiles, block_tiles, 1
            )
            feat_part = lax.dynamic_slice_in_dim(edge_feats, row_start, block_rows, 2)
            live_tile = link_part >= 0
            sender_row = jnp.where(live_tile, link_part, 0)
            live_edge = jnp.broadcast_to(
                live_tile[:, :, None], (tile_size, block_tiles, tile_size)
            ).reshape(tile_size, block_rows)
            own_rows = lax.dynamic_slice_in_dim(extended, row_start, block_rows, 0)
            tile_send = table[sender_row]
            senders = jnp.broadcast_to(
                tile_send[:, :, None], (tile_size, block_tiles, tile_size, width)
            )
            senders = senders.reshape(tile_size, block_rows, width)
            joined = jnp.concatenate(
                [jnp.broadcast_to(own_rows[None], senders.shape), senders], axis=-1
            )
            first_sum = jnp.dot(
                joined.reshape(-1, 2 * width), joined_mat, preferred_element_type=jnp.float32
            )
            first_sum = first_sum.reshape(senders.shape)
            geo_term = feat_part[0][..., None] * geo_rows[0]
            for channel in range(1, 4):
                geo_term = geo_term + feat_part[channel][..., None] * geo_rows[channel]
            first_sum = first_sum + geo_term + bias_rows[0]
            hidden = jnp.maximum(first_sum, 0.0).astype(jnp.bfloat16)
            second = jnp.dot(
                hidden.reshape(-1, width), edge_mats[2], preferred_element_type=jnp.float32
            )
            second = second.reshape(hidden.shape) + bias_rows[1]
            message = layer_norm(second, gain_rows[0])
            return jnp.sum(jnp.where(live_edge[..., None], message, 0.0), axis=0)

        totals = lax.map(messages, jnp.arange(block_count)).reshape(rows_total, width)
        gathered = totals.astype(jnp.bfloat16)
        node_first = jnp.dot(extended, node_mats[0], preferred_element_type=jnp.float32)
        node_first = (
            node_first
            + jnp.dot(gathered, node_mats[1], preferred_element_type=jnp.float32)
            + bias_rows[2]
        )
        node_hidden = jnp.maximum(node_first, 0.0).astype(jnp.bfloat16)
        node_out = (
            jnp.dot(node_hidden, node_mats[2], preferred_element_type=jnp.float32) + bias_rows[3]
        )
        extended = (extended.astype(jnp.float32) + layer_norm(node_out, gain_rows[1])).astype(
            jnp.bfloat16
        )
    return extended[None, None]


def solution(mesh):
    return jax.shard_map(
        body,
        mesh=mesh,
        in_specs=(
            P("gx", "gy", None, None),
            P("gx", "gy", None, None),
            P("gx", "gy", None),
            P("gx", "gy", None, None),
            P("gx", "gy", None),
            P("gx", "gy", None, None),
            P("gx", "gy", None, None, None),
            P(),
            P(),
            P(),
            P(),
            P(),
        ),
        out_specs=P("gx", "gy", None, None),
        check_vma=False,
    )
```

profile of v0, /device:TPU:8, one launch (start us, length us, event | category | flops | bytes accessed | tf_op | source)
XLA Modules:
  0.0 245.0 jit_solution(16396928564230235641)
XLA Ops:
  4.9 4.5 %collective-permute-start.1 = (bf16[64,128]{1,0:T(8,128)(2,1)S(1)}, bf16[64,128]{1,0:T(8,128)(2,1)S(1)}, u32[]{:S(2)}, u32[]{:S(2)}) collective-permute-start(bf16[64,128]{1,0:T(8,128)(2,1)S(1)} %get-tuple-element.345), channel_id=1, source_target_pairs={{2,0},{4,2},{6,4},{8,6},{10,8},{12,10},{14,12},{16,14},{18,16},{20... | collective-permute-start | bytes 49160 | tf_op jit(solution)/shard_map/ppermute | solution.py:12
  9.5 3.4 %collective-permute-start.2 = (bf16[64,128]{1,0:T(8,128)(2,1)S(1)}, bf16[64,128]{1,0:T(8,128)(2,1)S(1)}, u32[]{:S(2)}, u32[]{:S(2)}) collective-permute-start(bf16[64,128]{1,0:T(8,128)(2,1)S(1)} %get-tuple-element.344), channel_id=1, source_target_pairs={{0,1},{2,3},{4,5},{6,7},{8,9},{10,11},{12,13},{14,15},{16,17},{18,... | collective-permute-start | bytes 49160 | tf_op jit(solution)/shard_map/ppermute | solution.py:12
  20.6 3.0 %fusion.67 = bf16[2048,128]{1,0:T(8,128)(2,1)S(1)} fusion(bf16[1280,128]{0,1:T(8,128)(2,1)S(1)} %concatenate.24, s32[2048]{0:T(1024)S(1)} %bitcast.289, pred[2048]{0:T(1024)(128)(4,1)S(1)} %lt.83), kind=kOutput, calls=%fused_computation.104 | convolution fusion | flops 676593664 | bytes 862208 | tf_op jit(solution)/shard_map/dot_general | solution.py:25
  26.3 2.4 collective-permute-start.5
  28.9 5.3 %collective-permute-done.5 = bf16[3,256,128]{2,1,0:T(8,128)(2,1)S(1)} collective-permute-done((bf16[3,256,128]{2,1,0:T(8,128)(2,1)S(1)}, bf16[3,256,128]{2,1,0:T(8,128)(2,1)S(1)}, u32[]{:S(2)}, u32[]{:S(2)}) %collective-permute-start.5) | collective-permute-done | bytes 196640 | tf_op jit(solution)/shard_map/ppermute | solution.py:12
  34.3 4.6 %collective-permute-start.7 = (bf16[3,256,128]{2,1,0:T(8,128)(2,1)S(1)}, bf16[3,256,128]{2,1,0:T(8,128)(2,1)S(1)}, u32[]{:S(2)}, u32[]{:S(2)}) collective-permute-start(bf16[3,256,128]{2,1,0:T(8,128)(2,1)S(1)} %pad_maximum_fusion.3), channel_id=1, source_target_pairs={{0,1},{2,3},{4,5},{6,7},{8,9},{10,11},{12,13},{14,15},{16,17},{18,... | collective-permute-start | bytes 589832 | tf_op jit(solution)/shard_map/ppermute | solution.py:12
  42.3 5.4 %collective-permute-done.6 = bf16[3,256,128]{2,1,0:T(8,128)(2,1)S(1)} collective-permute-done((bf16[3,256,128]{2,1,0:T(8,128)(2,1)S(1)}, bf16[3,256,128]{2,1,0:T(8,128)(2,1)S(1)}, u32[]{:S(2)}, u32[]{:S(2)}) %collective-permute-start.6) | collective-permute-done | bytes 196640 | tf_op jit(solution)/shard_map/ppermute | solution.py:12
  49.8 77.5 %while.20 = (s32[]{:T(128)}, bf16[5,256,128]{2,1,0:T(8,128)(2,1)}, s32[5]{0:T(128)S(1)}, s32[16,80]{1,0:T(8,128)S(1)}, bf16[1280,128]{0,1:T(8,128)(2,1)S(1)}, /*...) while((s32[]{:T(128)}, bf16[5,256,128]{2,1,0:T(8,128)(2,1)}, ...), condition=%wide.region_5.6_spmd, body=%wide.region_1.5_spmd.sunk | while | flops 418879744 | bytes 18810164 | solution.py:125
  56.7 4.1 %add_reduce_fusion.4 = (f32[16,256]{1,0:T(8,128)S(1)}, f32[16,256,128]{2,1,0:T(8,128)S(1)}) fusion(f32[128]{0:T(128)S(1)} %get-tuple-element.529, bf16[3,128,128]{1,2,0:T(8,128)(2,1)} %get-tuple-element.623, bf16[16,256,128]{2,1,0:T(8,128)(2,1)S(1)} %bitcast.275, bf16[16,256,128]{2,1,0:T(8,128)(2,1)} %broadcast_in_dim.121, ...), kind=kOutput, calls=%fused_computation.9.clone.1 | convolution fusion | flops 413659136 | bytes 4377600 | tf_op jit(solution)/shard_map/while/body/eval_jaxpr/dot_general | solution.py:118
  72.2 4.1 %add_reduce_fusion.4 = (f32[16,256]{1,0:T(8,128)S(1)}, f32[16,256,128]{2,1,0:T(8,128)S(1)}) fusion(f32[128]{0:T(128)S(1)} %get-tuple-element.529, bf16[3,128,128]{1,2,0:T(8,128)(2,1)} %get-tuple-element.623, bf16[16,256,128]{2,1,0:T(8,128)(2,1)S(1)} %bitcast.275, bf16[16,256,128]{2,1,0:T(8,128)(2,1)} %broadcast_in_dim.121, ...), kind=kOutput, calls=%fused_computation.9.clone.1 | convolution fusion | flops 413659136 | bytes 4377600 | tf_op jit(solution)/shard_map/while/body/eval_jaxpr/dot_general | solution.py:118
  87.7 4.1 %add_reduce_fusion.4 = (f32[16,256]{1,0:T(8,128)S(1)}, f32[16,256,128]{2,1,0:T(8,128)S(1)}) fusion(f32[128]{0:T(128)S(1)} %get-tuple-element.529, bf16[3,128,128]{1,2,0:T(8,128)(2,1)} %get-tuple-element.623, bf16[16,256,128]{2,1,0:T(8,128)(2,1)S(1)} %bitcast.275, bf16[16,256,128]{2,1,0:T(8,128)(2,1)} %broadcast_in_dim.121, ...), kind=kOutput, calls=%fused_computation.9.clone.1 | convolution fusion | flops 413659136 | bytes 4377600 | tf_op jit(solution)/shard_map/while/body/eval_jaxpr/dot_general | solution.py:118
  103.2 4.1 %add_reduce_fusion.4 = (f32[16,256]{1,0:T(8,128)S(1)}, f32[16,256,128]{2,1,0:T(8,128)S(1)}) fusion(f32[128]{0:T(128)S(1)} %get-tuple-element.529, bf16[3,128,128]{1,2,0:T(8,128)(2,1)} %get-tuple-element.623, bf16[16,256,128]{2,1,0:T(8,128)(2,1)S(1)} %bitcast.275, bf16[16,256,128]{2,1,0:T(8,128)(2,1)} %broadcast_in_dim.121, ...), kind=kOutput, calls=%fused_computation.9.clone.1 | convolution fusion | flops 413659136 | bytes 4377600 | tf_op jit(solution)/shard_map/while/body/eval_jaxpr/dot_general | solution.py:118
  118.7 4.1 %add_reduce_fusion.4 = (f32[16,256]{1,0:T(8,128)S(1)}, f32[16,256,128]{2,1,0:T(8,128)S(1)}) fusion(f32[128]{0:T(128)S(1)} %get-tuple-element.529, bf16[3,128,128]{1,2,0:T(8,128)(2,1)} %get-tuple-element.623, bf16[16,256,128]{2,1,0:T(8,128)(2,1)S(1)} %bitcast.275, bf16[16,256,128]{2,1,0:T(8,128)(2,1)} %broadcast_in_dim.121, ...), kind=kOutput, calls=%fused_computation.9.clone.1 | convolution fusion | flops 413659136 | bytes 4377600 | tf_op jit(solution)/shard_map/while/body/eval_jaxpr/dot_general | solution.py:118
  130.9 4.9 %fusion.70 = bf16[2048,128]{0,1:T(8,128)(2,1)S(1)} fusion(bf16[1280,128]{0,1:T(8,128)(2,1)} %get-tuple-element.638, s32[2048]{0:T(1024)S(1)} %bitcast.290, pred[2048]{0:T(1024)(128)(4,1)S(1)} %copy-done.25), kind=kOutput, calls=%fused_computation.105 | convolution fusion | flops 676593664 | bytes 862208 | tf_op jit(solution)/shard_map/dot_general | solution.py:25
  138.6 2.4 collective-permute-start.9
  141.1 5.4 %collective-permute-done.9 = bf16[3,256,128]{1,2,0:T(8,128)(2,1)S(1)} collective-permute-done((bf16[3,256,128]{1,2,0:T(8,128)(2,1)S(1)}, bf16[3,256,128]{1,2,0:T(8,128)(2,1)S(1)}, u32[]{:S(2)}, u32[]{:S(2)}) %collective-permute-start.9) | collective-permute-done | bytes 196640 | tf_op jit(solution)/shard_map/ppermute | solution.py:12
  150.0 4.7 %collective-permute-start.11 = (bf16[3,256,128]{1,2,0:T(8,128)(2,1)S(1)}, bf16[3,256,128]{1,2,0:T(8,128)(2,1)S(1)}, u32[]{:S(2)}, u32[]{:S(2)}) collective-permute-start(bf16[3,256,128]{1,2,0:T(8,128)(2,1)S(1)} %pad_maximum_fusion.7), channel_id=1, source_target_pairs={{0,1},{2,3},{4,5},{6,7},{8,9},{10,11},{12,13},{14,15},{16,17},{18,... | collective-permute-start | bytes 589832 | tf_op jit(solution)/shard_map/ppermute | solution.py:12
  154.8 2.9 %collective-permute-done.11 = bf16[3,256,128]{1,2,0:T(8,128)(2,1)S(1)} collective-permute-done((bf16[3,256,128]{1,2,0:T(8,128)(2,1)S(1)}, bf16[3,256,128]{1,2,0:T(8,128)(2,1)S(1)}, u32[]{:S(2)}, u32[]{:S(2)}) %collective-permute-start.11) | collective-permute-done | bytes 196640 | tf_op jit(solution)/shard_map/ppermute | solution.py:12
  158.5 82.8 %while.21 = (s32[]{:T(128)}, bf16[5,256,128]{2,1,0:T(8,128)(2,1)S(1)}, s32[5]{0:T(128)S(1)}, s32[16,80]{1,0:T(8,128)S(1)}, bf16[1280,128]{0,1:T(8,128)(2,1)}, /*...) while((s32[]{:T(128)}, ...), condition=%wide.region_12.13_spmd, body=%wide.region_8.12_spmd.sunk | while | flops 418879744 | bytes 18776756 | solution.py:125
  167.0 4.1 %add_reduce_fusion.5 = (f32[16,256]{1,0:T(8,128)S(1)}, f32[16,256,128]{2,1,0:T(8,128)S(1)}) fusion(f32[128]{0:T(128)S(1)} %get-tuple-element.556, bf16[3,128,128]{1,2,0:T(8,128)(2,1)} %get-tuple-element.686, bf16[16,256,128]{2,1,0:T(8,128)(2,1)S(1)} %bitcast.276, bf16[16,256,128]{2,1,0:T(8,128)(2,1)} %broadcast_in_dim.126, ...), kind=kOutput, calls=%fused_computation.51.clone.1 | convolution fusion | flops 413659136 | bytes 4377600 | tf_op jit(solution)/shard_map/while/body/eval_jaxpr/dot_general | solution.py:118
  183.6 4.1 %add_reduce_fusion.5 = (f32[16,256]{1,0:T(8,128)S(1)}, f32[16,256,128]{2,1,0:T(8,128)S(1)}) fusion(f32[128]{0:T(128)S(1)} %get-tuple-element.556, bf16[3,128,128]{1,2,0:T(8,128)(2,1)} %get-tuple-element.686, bf16[16,256,128]{2,1,0:T(8,128)(2,1)S(1)} %bitcast.276, bf16[16,256,128]{2,1,0:T(8,128)(2,1)} %broadcast_in_dim.126, ...), kind=kOutput, calls=%fused_computation.51.clone.1 | convolution fusion | flops 413659136 | bytes 4377600 | tf_op jit(solution)/shard_map/while/body/eval_jaxpr/dot_general | solution.py:118
  200.2 4.1 %add_reduce_fusion.5 = (f32[16,256]{1,0:T(8,128)S(1)}, f32[16,256,128]{2,1,0:T(8,128)S(1)}) fusion(f32[128]{0:T(128)S(1)} %get-tuple-element.556, bf16[3,128,128]{1,2,0:T(8,128)(2,1)} %get-tuple-element.686, bf16[16,256,128]{2,1,0:T(8,128)(2,1)S(1)} %bitcast.276, bf16[16,256,128]{2,1,0:T(8,128)(2,1)} %broadcast_in_dim.126, ...), kind=kOutput, calls=%fused_computation.51.clone.1 | convolution fusion | flops 413659136 | bytes 4377600 | tf_op jit(solution)/shard_map/while/body/eval_jaxpr/dot_general | solution.py:118
  216.7 4.1 %add_reduce_fusion.5 = (f32[16,256]{1,0:T(8,128)S(1)}, f32[16,256,128]{2,1,0:T(8,128)S(1)}) fusion(f32[128]{0:T(128)S(1)} %get-tuple-element.556, bf16[3,128,128]{1,2,0:T(8,128)(2,1)} %get-tuple-element.686, bf16[16,256,128]{2,1,0:T(8,128)(2,1)S(1)} %bitcast.276, bf16[16,256,128]{2,1,0:T(8,128)(2,1)} %broadcast_in_dim.126, ...), kind=kOutput, calls=%fused_computation.51.clone.1 | convolution fusion | flops 413659136 | bytes 4377600 | tf_op jit(solution)/shard_map/while/body/eval_jaxpr/dot_general | solution.py:118
  233.3 4.1 %add_reduce_fusion.5 = (f32[16,256]{1,0:T(8,128)S(1)}, f32[16,256,128]{2,1,0:T(8,128)S(1)}) fusion(f32[128]{0:T(128)S(1)} %get-tuple-element.556, bf16[3,128,128]{1,2,0:T(8,128)(2,1)} %get-tuple-element.686, bf16[16,256,128]{2,1,0:T(8,128)(2,1)S(1)} %bitcast.276, bf16[16,256,128]{2,1,0:T(8,128)(2,1)} %broadcast_in_dim.126, ...), kind=kOutput, calls=%fused_computation.51.clone.1 | convolution fusion | flops 413659136 | bytes 4377600 | tf_op jit(solution)/shard_map/while/body/eval_jaxpr/dot_general | solution.py:118
  (498 shorter events, 140.2 us)
Async XLA Ops:
  0.0 18.6 %copy-start.16 = (f32[2,4,128]{2,1,0:T(4,128)S(1)}, f32[2,4,128]{2,1,0:T(4,128)}, u32[]{:S(2)}) copy-start(f32[2,4,128]{2,1,0:T(4,128)} %param.26) | copy-start | bytes 12292
  0.0 19.2 %copy-start.21 = (f32[2,4,128]{2,1,0:T(4,128)S(1)}, f32[2,4,128]{2,1,0:T(4,128)}, u32[]{:S(2)}) copy-start(f32[2,4,128]{2,1,0:T(4,128)} %param.25) | copy-start | bytes 12292
  0.0 19.8 %copy-start.26 = (s32[1,1,8]{2,1,0:T(1,128)S(1)}, s32[1,1,8]{2,1,0:T(1,128)}, u32[]{:S(2)}) copy-start(s32[1,1,8]{2,1,0:T(1,128)} %param.20) | copy-start | bytes 100
  0.0 19.9 %copy-start.17 = (s32[1,1,8,256]{3,2,1,0:T(8,128)S(1)}, s32[1,1,8,256]{3,2,1,0:T(8,128)}, u32[]{:S(2)}) copy-start(s32[1,1,8,256]{3,2,1,0:T(8,128)} %param.19) | copy-start | bytes 24580
  3.0 17.0 %collective-permute-start = (bf16[64,128]{1,0:T(8,128)(2,1)S(1)}, bf16[64,128]{1,0:T(8,128)(2,1)S(1)}, u32[]{:S(2)}, u32[]{:S(2)}) collective-permute-start(bf16[64,128]{1,0:T(8,128)(2,1)S(1)} %get-tuple-element.346), channel_id=1, source_target_pairs={{0,2},{2,4},{4,6},{6,8},{8,10},{10,12},{12,14},{14,16},{16,18},{18... | collective-permute-start | bytes 49160 | tf_op jit(solution)/shard_map/ppermute | solution.py:12
  4.9 15.2 %collective-permute-start.1 = (bf16[64,128]{1,0:T(8,128)(2,1)S(1)}, bf16[64,128]{1,0:T(8,128)(2,1)S(1)}, u32[]{:S(2)}, u32[]{:S(2)}) collective-permute-start(bf16[64,128]{1,0:T(8,128)(2,1)S(1)} %get-tuple-element.345), channel_id=1, source_target_pairs={{2,0},{4,2},{6,4},{8,6},{10,8},{12,10},{14,12},{16,14},{18,16},{20... | collective-permute-start | bytes 49160 | tf_op jit(solution)/shard_map/ppermute | solution.py:12
  9.5 10.8 %collective-permute-start.2 = (bf16[64,128]{1,0:T(8,128)(2,1)S(1)}, bf16[64,128]{1,0:T(8,128)(2,1)S(1)}, u32[]{:S(2)}, u32[]{:S(2)}) collective-permute-start(bf16[64,128]{1,0:T(8,128)(2,1)S(1)} %get-tuple-element.344), channel_id=1, source_target_pairs={{0,1},{2,3},{4,5},{6,7},{8,9},{10,11},{12,13},{14,15},{16,17},{18,... | collective-permute-start | bytes 49160 | tf_op jit(solution)/shard_map/ppermute | solution.py:12
  12.9 7.5 %collective-permute-start.3 = (bf16[64,128]{1,0:T(8,128)(2,1)S(1)}, bf16[64,128]{1,0:T(8,128)(2,1)S(1)}, u32[]{:S(2)}, u32[]{:S(2)}) collective-permute-start(bf16[64,128]{1,0:T(8,128)(2,1)S(1)} %get-tuple-element.343), channel_id=1, source_target_pairs={{1,0},{3,2},{5,4},{7,6},{9,8},{11,10},{13,12},{15,14},{17,16},{19,... | collective-permute-start | bytes 49160 | tf_op jit(solution)/shard_map/ppermute | solution.py:12
  23.8 5.1 %collective-permute-start.4 = (bf16[3,256,128]{2,1,0:T(8,128)(2,1)S(1)}, bf16[3,256,128]{2,1,0:T(8,128)(2,1)S(1)}, u32[]{:S(2)}, u32[]{:S(2)}) collective-permute-start(bf16[3,256,128]{2,1,0:T(8,128)(2,1)S(1)} %pad_maximum_fusion), channel_id=1, source_target_pairs={{2,0},{4,2},{6,4},{8,6},{10,8},{12,10},{14,12},{16,14},{18,16},{20... | collective-permute-start | bytes 589832 | tf_op jit(solution)/shard_map/ppermute | solution.py:12
  26.3 7.9 %collective-permute-start.5 = (bf16[3,256,128]{2,1,0:T(8,128)(2,1)S(1)}, bf16[3,256,128]{2,1,0:T(8,128)(2,1)S(1)}, u32[]{:S(2)}, u32[]{:S(2)}) collective-permute-start(bf16[3,256,128]{2,1,0:T(8,128)(2,1)S(1)} %pad_maximum_fusion.1), channel_id=1, source_target_pairs={{0,2},{2,4},{4,6},{6,8},{8,10},{10,12},{12,14},{14,16},{16,18},{18... | collective-permute-start | bytes 589832 | tf_op jit(solution)/shard_map/ppermute | solution.py:12
  34.3 7.7 %collective-permute-start.7 = (bf16[3,256,128]{2,1,0:T(8,128)(2,1)S(1)}, bf16[3,256,128]{2,1,0:T(8,128)(2,1)S(1)}, u32[]{:S(2)}, u32[]{:S(2)}) collective-permute-start(bf16[3,256,128]{2,1,0:T(8,128)(2,1)S(1)} %pad_maximum_fusion.3), channel_id=1, source_target_pairs={{0,1},{2,3},{4,5},{6,7},{8,9},{10,11},{12,13},{14,15},{16,17},{18,... | collective-permute-start | bytes 589832 | tf_op jit(solution)/shard_map/ppermute | solution.py:12
  40.2 7.6 %collective-permute-start.6 = (bf16[3,256,128]{2,1,0:T(8,128)(2,1)S(1)}, bf16[3,256,128]{2,1,0:T(8,128)(2,1)S(1)}, u32[]{:S(2)}, u32[]{:S(2)}) collective-permute-start(bf16[3,256,128]{2,1,0:T(8,128)(2,1)S(1)} %pad_maximum_fusion.2), channel_id=1, source_target_pairs={{1,0},{3,2},{5,4},{7,6},{9,8},{11,10},{13,12},{15,14},{17,16},{19,... | collective-permute-start | bytes 589832 | tf_op jit(solution)/shard_map/ppermute | solution.py:12
  65.3 6.9 %copy-start.8 = (f32[4,128]{1,0:T(4,128)}, f32[4,128]{1,0:T(4,128)S(1)}, u32[]{:S(2)}) copy-start(f32[4,128]{1,0:T(4,128)S(1)} %get-tuple-element.621) | copy-start | bytes 6148 | tf_op jit(solution)/shard_map/while
  80.9 6.9 %copy-start.8 = (f32[4,128]{1,0:T(4,128)}, f32[4,128]{1,0:T(4,128)S(1)}, u32[]{:S(2)}) copy-start(f32[4,128]{1,0:T(4,128)S(1)} %get-tuple-element.621) | copy-start | bytes 6148 | tf_op jit(solution)/shard_map/while
  80.9 6.8 %copy-start.12 = (f32[4,128]{1,0:T(4,128)}, f32[4,128]{1,0:T(4,128)S(1)}, u32[]{:S(2)}) copy-start(f32[4,128]{1,0:T(4,128)S(1)} %get-tuple-element.622) | copy-start | bytes 6148 | tf_op jit(solution)/shard_map/while
  96.4 6.9 %copy-start.8 = (f32[4,128]{1,0:T(4,128)}, f32[4,128]{1,0:T(4,128)S(1)}, u32[]{:S(2)}) copy-start(f32[4,128]{1,0:T(4,128)S(1)} %get-tuple-element.621) | copy-start | bytes 6148 | tf_op jit(solution)/shard_map/while
  96.4 6.8 %copy-start.12 = (f32[4,128]{1,0:T(4,128)}, f32[4,128]{1,0:T(4,128)S(1)}, u32[]{:S(2)}) copy-start(f32[4,128]{1,0:T(4,128)S(1)} %get-tuple-element.622) | copy-start | bytes 6148 | tf_op jit(solution)/shard_map/while
  111.9 6.9 %copy-start.8 = (f32[4,128]{1,0:T(4,128)}, f32[4,128]{1,0:T(4,128)S(1)}, u32[]{:S(2)}) copy-start(f32[4,128]{1,0:T(4,128)S(1)} %get-tuple-element.621) | copy-start | bytes 6148 | tf_op jit(solution)/shard_map/while
  130.9 6.9 %copy-start.5 = (bf16[1,3,128,128]{3,2,1,0:T(8,128)(2,1)S(1)}, bf16[1,3,128,128]{3,2,1,0:T(8,128)(2,1)}, u32[]{:S(2)}) copy-start(bf16[1,3,128,128]{3,2,1,0:T(8,128)(2,1)} %get-tuple-element.323) | copy-start | bytes 294916
  135.9 5.1 %collective-permute-start.8 = (bf16[3,256,128]{1,2,0:T(8,128)(2,1)S(1)}, bf16[3,256,128]{1,2,0:T(8,128)(2,1)S(1)}, u32[]{:S(2)}, u32[]{:S(2)}) collective-permute-start(bf16[3,256,128]{1,2,0:T(8,128)(2,1)S(1)} %pad_maximum_fusion.4), channel_id=1, source_target_pairs={{2,0},{4,2},{6,4},{8,6},{10,8},{12,10},{14,12},{16,14},{18,16},{20... | collective-permute-start | bytes 589832 | tf_op jit(solution)/shard_map/ppermute | solution.py:12
  138.6 7.9 %collective-permute-start.9 = (bf16[3,256,128]{1,2,0:T(8,128)(2,1)S(1)}, bf16[3,256,128]{1,2,0:T(8,128)(2,1)S(1)}, u32[]{:S(2)}, u32[]{:S(2)}) collective-permute-start(bf16[3,256,128]{1,2,0:T(8,128)(2,1)S(1)} %pad_maximum_fusion.5), channel_id=1, source_target_pairs={{0,2},{2,4},{4,6},{6,8},{8,10},{10,12},{12,14},{14,16},{16,18},{18... | collective-permute-start | bytes 589832 | tf_op jit(solution)/shard_map/ppermute | solution.py:12
  146.6 11.9 %copy-start.6 = (f32[4,128]{1,0:T(4,128)S(1)}, f32[4,128]{1,0:T(4,128)}, u32[]{:S(2)}) copy-start(f32[4,128]{1,0:T(4,128)} %get-tuple-element.642) | copy-start | bytes 6148
  146.6 8.2 %collective-permute-start.10 = (bf16[3,256,128]{1,2,0:T(8,128)(2,1)S(1)}, bf16[3,256,128]{1,2,0:T(8,128)(2,1)S(1)}, u32[]{:S(2)}, u32[]{:S(2)}) collective-permute-start(bf16[3,256,128]{1,2,0:T(8,128)(2,1)S(1)} %pad_maximum_fusion.6), channel_id=1, source_target_pairs={{1,0},{3,2},{5,4},{7,6},{9,8},{11,10},{13,12},{15,14},{17,16},{19,... | collective-permute-start | bytes 589832 | tf_op jit(solution)/shard_map/ppermute | solution.py:12
  150.0 7.7 %collective-permute-start.11 = (bf16[3,256,128]{1,2,0:T(8,128)(2,1)S(1)}, bf16[3,256,128]{1,2,0:T(8,128)(2,1)S(1)}, u32[]{:S(2)}, u32[]{:S(2)}) collective-permute-start(bf16[3,256,128]{1,2,0:T(8,128)(2,1)S(1)} %pad_maximum_fusion.7), channel_id=1, source_target_pairs={{0,1},{2,3},{4,5},{6,7},{8,9},{10,11},{12,13},{14,15},{16,17},{18,... | collective-permute-start | bytes 589832 | tf_op jit(solution)/shard_map/ppermute | solution.py:12
  (87 other events, 340.0 us)
where the time goes:
time: 248 us; the launch traced here: 245 us
  local copies, waits for them, and re-layouts  85.7 us (35%)
  matrix products  56.7 us (23%)
  other arithmetic  37 us (15%)
  starting transfers between devices  31.7 us (13%)
  waiting for transfers between devices  19.5 us (8%)
  loops' own time  13.7 us (6%)
    dot_general x10, matrix products, messages(): jnp.dot(hidden.reshape(-1, width), edge_mats[2], preferred_element_type=j...  41.2 us
    ppermute x12, starting transfers between devices, shifted(): lax.ppermute(value, axis, [(source, source + steps) for source in range(l...  31.7 us
    mul x20, local copies, waits for them, and re-layouts, messages(): geo_term = feat_part[0][..., None] * geo_rows[0]  19.6 us
    reduce_sum x10, other arithmetic, messages(): return jnp.sum(jnp.where(live_edge[..., None], message, 0.0), axis=0)  19.6 us
    ppermute x12, waiting for transfers between devices, shifted(): lax.ppermute(value, axis, [(source, source + steps) for source in range(l...  19.5 us
    another operation x2, loops' own time, body(): lax.map(messages, jnp.arange(block_count)).reshape(rows_total, width)  13.7 us
    reduce_sum x12, other arithmetic, layer_norm(): spread = jnp.mean(center * center, axis=-1, keepdims=True)  13.2 us
    broadcast_in_dim x10, local copies, waits for them, and re-layouts, messages(): jnp.broadcast_to(own_rows[None], senders.shape)  11.9 us
  transfers between devices with their start and end apart: 12, of which 6 were waited for; matrix products, arithmetic and copies ran while one was open for 5% of the time, Pallas kernels for 0%

commit v1 on v0

v1 whole, which is shorter than its diff:
```python
import functools
import itertools
import math

import jax
import jax.numpy as jnp
from jax import lax
from jax.experimental import pallas as pl
from jax.experimental.pallas import tpu as pltpu
from jax.sharding import PartitionSpec as P

F32 = jnp.float32
BF16 = jnp.bfloat16
CHUNK = 128
VMEM = pl.BlockSpec(memory_space=pltpu.VMEM)
SMEM = pl.BlockSpec(memory_space=pltpu.SMEM)
PARAMS = pltpu.CompilerParams(vmem_limit_bytes=48 * 1024 * 1024)


def partner(place, count, kind):
    other = place + 1 if place % 2 == kind else place - 1
    return other if 0 <= other < count else None


def kinds(count):
    return [0, 1][: max(0, min(2, count - 1))]


def links(count_x, count_y):
    both = itertools.product([None] + kinds(count_x), [None] + kinds(count_y))
    return [pair for pair in both if pair != (None, None)]


def swap(value, link):
    count_x, count_y = lax.axis_size("gx"), lax.axis_size("gy")
    pairs = []
    for x, y in itertools.product(range(count_x), range(count_y)):
        to_x = x if link[0] is None else partner(x, count_x, link[0])
        to_y = y if link[1] is None else partner(y, count_y, link[1])
        if to_x is not None and to_y is not None:
            pairs.append((x * count_y + y, to_x * count_y + to_y))
    return lax.ppermute(value, ("gx", "gy"), pairs)


def step(axis, kind):
    if kind is None:
        return 0
    sign = 1 if kind == 0 else -1
    return sign * (1 - 2 * lax.rem(lax.axis_index(axis), 2))


def section(step_x, step_y):
    place = (step_x + 1) * 3 + step_y + 1
    return jnp.where(place > 4, place - 1, place)


def side(link):
    if link[1] is None:
        return (step("gx", link[0]) + 1) // 2
    return 2 + (step("gy", link[1]) + 1) // 2


def pack_kernel(sides, latents_ref, rows_ref, count_ref, retained_ref, *packet_refs):
    total = latents_ref.shape[0]
    slots = rows_ref.shape[1]
    owned = latents_ref[...]
    row_id = lax.broadcasted_iota(jnp.int32, (total, slots), 0)
    lane = lax.broadcasted_iota(jnp.int32, (1, slots), 1)

    def picker(direction):
        wanted = rows_ref[pl.ds(direction, 1), :]
        wanted = jnp.where(lane < count_ref[direction], wanted, -1)
        return (row_id == wanted).astype(F32)

    marks = picker(0)
    for direction in range(1, 4):
        marks = marks + picker(direction)
    marks = jnp.dot(marks.astype(BF16), jnp.ones((slots, owned.shape[1]), BF16), preferred_element_type=F32)
    retained_ref[...] = jnp.where(marks > 0.0, 0.0, owned.astype(F32)).astype(BF16)
    for link, packet_ref in zip(sides, packet_refs):
        chosen = lax.dot_general(
            picker(side(link)).astype(BF16), owned, (((0,), (0,)), ((), ())), preferred_element_type=F32
        )
        packet_ref[...] = chosen.astype(BF16)


def gather_ghosts(all_links, extended_ref, rows_ref, count_ref, send_refs):
    total, width = extended_ref.shape
    slots = rows_ref.shape[1]
    lane = lax.broadcasted_iota(jnp.int32, (1, slots), 1)
    column = lax.broadcasted_iota(jnp.int32, (slots, 128), 1).astype(F32)
    for link, send_ref in zip(all_links, send_refs):
        target = section(step("gx", link[0]), step("gy", link[1]))
        wanted = rows_ref[pl.ds(target, 1), :]
        wanted = jnp.where(lane < count_ref[target], wanted, -1).astype(F32)
        wanted = jnp.transpose(jnp.broadcast_to(wanted, (128, slots)))
        picker = jnp.concatenate(
            [jnp.where(wanted == column + float(start), 1.0, 0.0).astype(BF16) for start in range(0, total, 128)],
            axis=1,
        )
        send_ref[...] = jnp.dot(picker, extended_ref[...], preferred_element_type=F32).astype(BF16)


def build_kernel(sides, all_links, retained_ref, *refs):
    arrivals, refs = refs[: len(sides)], refs[len(sides) :]
    rows_ref, count_ref, extended_ref, *send_refs = refs
    total = extended_ref.shape[0]
    owned = retained_ref.shape[0]
    slots = (total - owned) // 4
    extended_ref[pl.ds(0, owned), :] = retained_ref[...]
    extended_ref[pl.ds(owned, total - owned), :] = jnp.zeros((total - owned, extended_ref.shape[1]), BF16)
    for link, arrival_ref in zip(sides, arrivals):
        start = pl.multiple_of(owned + slots * side(link), 16)
        extended_ref[pl.ds(start, slots), :] = arrival_ref[...]
    gather_ghosts(all_links, extended_ref, rows_ref, count_ref, send_refs)


def turn_kernel(geometry_ref, turned_ref):
    feats = geometry_ref[...]
    high = feats.astype(BF16).astype(F32)
    turned_ref[...] = jnp.transpose(jnp.concatenate([high, feats - high], axis=0)).astype(BF16)


def spread_of(center):
    return jnp.sum(center * center, axis=-1, keepdims=True)


def layer_kernel(
    layer, last, all_links, extended_ref, turned_ref, links_ref, edge_ref, node_ref, geo_ref, bias_ref, gain_ref, *refs
):
    landed, refs = refs[: len(all_links)], refs[len(all_links) :]
    if not last:
        rows_ref, count_ref, *refs = refs
    updated_ref, refs = refs[0], refs[1:]
    send_refs, refs = (() if last else refs[: len(all_links)]), (refs if last else refs[len(all_links) :])
    table_ref, first_ref, second_ref, total_ref = refs
    rows_total, width = extended_ref.shape
    slots, tiles = links_ref.shape
    rows = rows_total // tiles
    ghosts = landed[0].shape[0]
    turned_width = turned_ref.shape[1]

    bias_first = bias_ref[layer, pl.ds(0, 1), :]
    sender_mat = edge_ref[layer, 1]
    table_ref[pl.ds(0, rows_total), :] = (
        jnp.dot(extended_ref[...], sender_mat, preferred_element_type=F32) + bias_first
    )
    if len(all_links) < 8:
        table_ref[pl.ds(rows_total, 8 * ghosts), :] = jnp.broadcast_to(bias_first, (8 * ghosts, width))
    for link, landed_ref in zip(all_links, landed):
        source = section(-step("gx", link[0]), -step("gy", link[1]))
        start = pl.multiple_of(rows_total + ghosts * source, 16)
        table_ref[pl.ds(start, ghosts), :] = (
            jnp.dot(landed_ref[...], sender_mat, preferred_element_type=F32) + bias_first
        )

    channels = geo_ref.shape[1]
    spread_geo = jnp.concatenate(
        [jnp.broadcast_to(geo_ref[layer, pl.ds(c, 1), :], (slots, width)) for c in range(channels)], axis=0
    )
    slot_of = lax.rem(lax.broadcasted_iota(jnp.int32, (channels * slots, width), 0), slots)
    for slot in range(slots):
        part = jnp.where(slot_of == slot, spread_geo, 0.0).astype(BF16)
        first_ref[pl.ds(0, channels * slots), pl.ds(slot * width, width)] = part
        first_ref[pl.ds(channels * slots, channels * slots), pl.ds(slot * width, width)] = part
        first_ref[pl.ds(turned_width, width), pl.ds(slot * width, width)] = edge_ref[layer, 0]
    edge_second = edge_ref[layer, 2].astype(F32)
    edge_second = (edge_second - jnp.mean(edge_second, axis=-1, keepdims=True)).astype(BF16)
    second_ref[...] = jnp.zeros(second_ref.shape, BF16)
    second_ref[pl.ds(0, width), pl.ds(0, width)] = edge_second
    second_ref[pl.ds(width, width), pl.ds(width, width)] = edge_second
    bias_second = bias_ref[layer, pl.ds(1, 1), :]
    bias_second = bias_second - jnp.mean(bias_second, axis=-1, keepdims=True)

    chunk_tiles = CHUNK // rows

    @pl.loop(0, rows_total // CHUNK)
    def _(chunk):
        start = pl.multiple_of(chunk * CHUNK, CHUNK)
        own = jnp.concatenate([turned_ref[pl.ds(start, CHUNK), :], extended_ref[pl.ds(start, CHUNK), :]], axis=1)
        sums = [jnp.zeros((rows, width), F32) for _ in range(chunk_tiles)]
        for pair in range(0, slots, 2):
            first = jnp.dot(own, first_ref[:, pl.ds(pair * width, 2 * width)], preferred_element_type=F32)
            halves, limits = [], []
            for slot in (pair, pair + 1):
                senders = []
                for tile in range(chunk_tiles):
                    row = links_ref[slot, chunk * chunk_tiles + tile]
                    limits.append(jnp.where(row >= 0, width * 1e-5, jnp.inf))
                    picked = table_ref[pl.ds(jnp.maximum(row, 0), 1), :]
                    senders.append(jnp.broadcast_to(picked, (rows, width)))
                halves.append(jnp.concatenate(senders, axis=0))
            hidden = jnp.maximum(first + jnp.concatenate(halves, axis=1), 0.0).astype(BF16)
            second = jnp.dot(hidden, second_ref[...], preferred_element_type=F32)
            for half in range(2):
                for tile in range(chunk_tiles):
                    center = second[tile * rows : (tile + 1) * rows, half * width : (half + 1) * width] + bias_second
                    scale = lax.rsqrt(spread_of(center) + limits[half * chunk_tiles + tile])
                    sums[tile] = sums[tile] + center * scale
        total_ref[pl.ds(start, CHUNK), :] = jnp.concatenate(sums, axis=0)

    gathered = (total_ref[...] * (gain_ref[layer, pl.ds(0, 1), :] * math.sqrt(width))).astype(BF16)
    extended = extended_ref[...]
    node_first = jnp.dot(
        jnp.concatenate([extended, gathered], axis=1),
        jnp.concatenate([node_ref[layer, 0], node_ref[layer, 1]], axis=0),
        preferred_element_type=F32,
    )
    node_hidden = jnp.maximum(node_first + bias_ref[layer, pl.ds(2, 1), :], 0.0).astype(BF16)
    node_out = jnp.dot(node_hidden, node_ref[layer, 2], preferred_element_type=F32) + bias_ref[layer, pl.ds(3, 1), :]
    center = node_out - jnp.mean(node_out, axis=-1, keepdims=True)
    scale = lax.rsqrt(spread_of(center) / width + 1e-5)
    updated_ref[...] = (extended.astype(F32) + center * scale * gain_ref[layer, pl.ds(1, 1), :]).astype(BF16)
    if not last:
        gather_ghosts(all_links, updated_ref, rows_ref, count_ref, send_refs)


def body(
    latents, mig_rows, mig_count, ghost_rows, ghost_count, neighbours, geometry, edge_w, node_w, geo_w, biases, gains
):
    owned = latents[0, 0]
    leave_rows, leave_count = mig_rows[0, 0], mig_count[0, 0]
    ghost_list, ghost_total = ghost_rows[0, 0], ghost_count[0, 0]
    tile_links = neighbours[0, 0]
    width = owned.shape[1]
    slots, tiles = tile_links.shape
    rows_total = geometry.shape[-1]
    ghosts = ghost_list.shape[1]
    table_rows = rows_total + 8 * ghosts
    all_links = links(lax.axis_size("gx"), lax.axis_size("gy"))
    sides = [link for link in all_links if None in link]
    rows_of = lambda count: jax.ShapeDtypeStruct((count, width), BF16)

    retained, *packets = pl.pallas_call(
        functools.partial(pack_kernel, sides),
        out_shape=[rows_of(owned.shape[0])] + [rows_of(leave_rows.shape[1])] * len(sides),
        in_specs=[VMEM, VMEM, SMEM],
        out_specs=[VMEM] * (1 + len(sides)),
        compiler_params=PARAMS,
        name="pack",
    )(owned, leave_rows, leave_count)
    arrivals = [swap(packet, link) for packet, link in zip(packets, sides)]

    feats = geometry.reshape(-1, rows_total)
    turned = pl.pallas_call(
        turn_kernel,
        out_shape=jax.ShapeDtypeStruct((rows_total, 2 * feats.shape[0]), BF16),
        in_specs=[VMEM],
        out_specs=VMEM,
        compiler_params=PARAMS,
        name="turn",
    )(feats)

    extended, *sends = pl.pallas_call(
        functools.partial(build_kernel, sides, all_links),
        out_shape=[rows_of(rows_total)] + [rows_of(ghosts)] * len(all_links),
        in_specs=[VMEM] * (2 + len(sides)) + [SMEM],
        out_specs=[VMEM] * (1 + len(all_links)),
        compiler_params=PARAMS,
        name="build",
    )(retained, *arrivals, ghost_list, ghost_total)

    layers = edge_w.shape[0]
    for layer in range(layers):
        last = layer == layers - 1
        landed = [swap(send, link) for send, link in zip(sends, all_links)]
        outs = [rows_of(rows_total)] + ([] if last else [rows_of(ghosts)] * len(all_links))
        extra = [] if last else [ghost_list, ghost_total]
        extended, *sends = pl.pallas_call(
            functools.partial(layer_kernel, layer, last, all_links),
            out_shape=outs,
            in_specs=[VMEM, VMEM, SMEM] + [VMEM] * (5 + len(all_links)) + ([] if last else [VMEM, SMEM]),
            out_specs=[VMEM] * len(outs),
            scratch_shapes=[
                pltpu.VMEM((table_rows, width), F32),
                pltpu.VMEM((turned.shape[1] + width, slots * width), BF16),
                pltpu.VMEM((2 * width, 2 * width), BF16),
                pltpu.VMEM((rows_total, width), F32),
            ],
            compiler_params=PARAMS,
            name="layer",
        )(extended, turned, tile_links, edge_w, node_w, geo_w, biases, gains, *landed, *extra)
    return extended[None, None]


def solution(mesh):
    block = lambda rank: P("gx", "gy", *[None] * rank)
    return jax.shard_map(
        body,
        mesh=mesh,
        in_specs=(block(2), block(2), block(1), block(2), block(1), block(2), block(3), P(), P(), P(), P(), P()),
        out_specs=block(2),
        check_vma=False,
    )
```

time: 248 us -> 60.5 us (0.24)
  local copies, waits for them, and re-layouts: 85.7 us -> 3.73 us
  matrix products: 56.7 us -> 0 us
  other arithmetic: 37 us -> 0 us
  Pallas kernels: 0 us -> 23 us
  loops' own time: 13.7 us -> 0 us
  starting transfers between devices: 31.7 us -> 22.2 us
  waiting for transfers between devices: 19.5 us -> 10.3 us
    dot_general x17 -> x0, matrix products: 56.7 us -> none  [the longest x10 41.2 us: messages(): jnp.dot(hidden.reshape(-1, width), edge_mats[2], preferred_element_type=j...]
    reduce_sum x22 -> x0, other arithmetic: 32.7 us -> none  [the longest x10 19.6 us: messages(): return jnp.sum(jnp.where(live_edge[..., None], message, 0.0), axis=0)]
    pallas_call x0 -> x5, Pallas kernels: none -> 23 us  [the longest x2 20 us: body(): pl.pallas_call(functools.partial(layer_kernel, layer, last, all_links), o...]
    mul x21 -> x0, local copies, waits for them, and re-layouts: 20.2 us -> none  [the longest x20 19.6 us: messages(): geo_term = feat_part[0][..., None] * geo_rows[0]]
    broadcast_in_dim x51 -> x0, local copies, waits for them, and re-layouts: 17.4 us -> none  [the longest x10 11.9 us: messages(): jnp.broadcast_to(own_rows[None], senders.shape)]
    another operation x2 -> x0, loops' own time: 13.7 us -> none  [body(): lax.map(messages, jnp.arange(block_count)).reshape(rows_total, width)]
    dynamic_slice x30 -> x0, local copies, waits for them, and re-layouts: 12.3 us -> none  [the longest x10 6.82 us: body(): lax.map(messages, jnp.arange(block_count)).reshape(rows_total, width)]
    add x11 -> x0, local copies, waits for them, and re-layouts: 9.65 us -> none  [the longest x10 9.06 us: messages(): second = second.reshape(hidden.shape) + bias_rows[1]]
  transfers between devices with their start and end apart: 12 -> 13, of which waited for: 6 -> 3; matrix products, arithmetic and copies ran while one was open for 5% -> 0% of each run, Pallas kernels for 0% -> 0%
where the time goes in v1:
time: 60.5 us; the launch traced here: 59.5 us
  Pallas kernels  23 us (38%)
  starting transfers between devices  22.2 us (37%)
  waiting for transfers between devices  10.3 us (17%)
  local copies, waits for them, and re-layouts  3.73 us (6%)
    ppermute x13, starting transfers between devices, swap(): return lax.ppermute(value, ('gx', 'gy'), pairs)  22.2 us
    pallas_call x2, Pallas kernels, body(): pl.pallas_call(functools.partial(layer_kernel, layer, last, all_links), o...  20 us
    ppermute x13, waiting for transfers between devices, swap(): return lax.ppermute(value, ('gx', 'gy'), pairs)  10.3 us
    unnamed x24, local copies, waits for them, and re-layouts  3.73 us
    pallas_call x1, Pallas kernels, body(): pl.pallas_call(functools.partial(build_kernel, sides, all_links), out_sha...  1.68 us
  transfers between devices with their start and end apart: 13, of which 3 were waited for; matrix products, arithmetic and copies ran while one was open for 0% of the time, Pallas kernels for 0%

profile of v1, /device:TPU:8, one launch (start us, length us, event | category | flops | bytes accessed | tf_op | source)
XLA Modules:
  0.0 59.5 jit_solution(1356801516111268030)
XLA Ops:
  0.0 1.0 %copy-done.3 = bf16[1,1,1024,128]{3,2,1,0:T(8,128)(2,1)S(1)} copy-done((bf16[1,1,1024,128]{3,2,1,0:T(8,128)(2,1)S(1)}, bf16[1,1,1024,128]{3,2,1,0:T(8,128)(2,1)}, u32[]{:S(2)}) %copy-start.3) | copy-done | bytes 262168
  1.0 0.7 %copy-done.10 = s32[1,1,4,64]{3,2,1,0:T(4,128)S(1)} copy-done((s32[1,1,4,64]{3,2,1,0:T(4,128)S(1)}, s32[1,1,4,64]{3,2,1,0:T(4,128)}, u32[]{:S(2)}) %copy-start.10) | copy-done | bytes 1048
  1.7 0.7 %copy-done.11 = s32[1,1,4]{2,1,0:T(1,128)S(1)} copy-done((s32[1,1,4]{2,1,0:T(1,128)S(1)}, s32[1,1,4]{2,1,0:T(1,128)}, u32[]{:S(2)}) %copy-start.11) | copy-done | bytes 40
  2.3 1.2 %pack.1 = (bf16[1024,128]{1,0:T(8,128)(2,1)S(1)}, bf16[64,128]{1,0:T(8,128)(2,1)S(1)}, bf16[64,128]{1,0:T(8,128)(2,1)S(1)}, bf16[64,128]{1,0:T(8,128)(2,1)S(1)}) custom-call(bf16[1024,128]{1,0:T(8,128)(2,1)S(1)} %bitcast.9, s32[4,64]{1,0:T(4,128)S(1)} %bitcast.16, s32[4]{0:T(128)S(1)} %bitcast.17), custom_call_target="tpu_custom_call" | custom-call | tf_op jit(solution)/shard_map/pack/pallas_call | solution.py:234
  3.5 1.6 %collective-permute-start = (bf16[64,128]{1,0:T(8,128)(2,1)S(1)}, bf16[64,128]{1,0:T(8,128)(2,1)S(1)}, u32[]{:S(2)}, u32[]{:S(2)}) collective-permute-start(bf16[64,128]{1,0:T(8,128)(2,1)S(1)} %get-tuple-element.22), channel_id=1, source_target_pairs={{0,1},{1,0},{2,3},{3,2},{4,5},{5,4},{6,7},{7,6},{8,9},{9,8},{10,11... | collective-permute-start | bytes 49160 | tf_op jit(solution)/shard_map/ppermute | solution.py:42
  5.1 3.4 %collective-permute-start.2 = (bf16[64,128]{1,0:T(8,128)(2,1)S(1)}, bf16[64,128]{1,0:T(8,128)(2,1)S(1)}, u32[]{:S(2)}, u32[]{:S(2)}) collective-permute-start(bf16[64,128]{1,0:T(8,128)(2,1)S(1)} %get-tuple-element.24), channel_id=1, source_target_pairs={{2,4},{3,5},{4,2},{5,3},{6,8},{7,9},{8,6},{9,7},{10,12},{11,13},{1... | collective-permute-start | bytes 49160 | tf_op jit(solution)/shard_map/ppermute | solution.py:42
  8.5 2.5 %collective-permute-done.2.refs_2_ = bf16[64,128]{1,0:T(8,128)(2,1)S(1)} collective-permute-done((bf16[64,128]{1,0:T(8,128)(2,1)S(1)}, bf16[64,128]{1,0:T(8,128)(2,1)S(1)}, u32[]{:S(2)}, u32[]{:S(2)}) %collective-permute-start.2) | collective-permute-done | bytes 16416 | tf_op jit(solution)/shard_map/ppermute | solution.py:42
  11.0 0.7 %copy-done.5 = s32[1,1,8,256]{3,2,1,0:T(8,128)S(1)} copy-done((s32[1,1,8,256]{3,2,1,0:T(8,128)S(1)}, s32[1,1,8,256]{3,2,1,0:T(8,128)}, u32[]{:S(2)}) %copy-start.5) | copy-done | bytes 8216
  11.7 0.7 %copy-done.9 = s32[1,1,8]{2,1,0:T(1,128)S(1)} copy-done((s32[1,1,8]{2,1,0:T(1,128)S(1)}, s32[1,1,8]{2,1,0:T(1,128)}, u32[]{:S(2)}) %copy-start.9) | copy-done | bytes 56
  12.4 1.7 %build.1 = (bf16[1280,128]{1,0:T(8,128)(2,1)S(1)}, bf16[256,128]{1,0:T(8,128)(2,1)S(1)}, bf16[256,128]{1,0:T(8,128)(2,1)S(1)}, bf16[256,128]{1,0:T(8,128)(2,1)S(...) custom-call(bf16[1024,128]{1,0:T(8,128)(2,1)S(1)} %get-tuple-element.21.retained_ref, ...), custom_call_target="tpu_custom_call" | custom-call | tf_op jit(solution)/shard_map/build/pallas_call | solution.py:254
  14.1 0.6 %collective-permute-start.3 = (bf16[256,128]{1,0:T(8,128)(2,1)S(1)}, bf16[256,128]{1,0:T(8,128)(2,1)S(1)}, u32[]{:S(2)}, u32[]{:S(2)}) collective-permute-start(bf16[256,128]{1,0:T(8,128)(2,1)S(1)} %get-tuple-element.26), channel_id=1, source_target_pairs={{0,1},{1,0},{2,3},{3,2},{4,5},{5,4},{6,7},{7,6},{8,9},{9,8},{10,11... | collective-permute-start | bytes 196616 | tf_op jit(solution)/shard_map/ppermute | solution.py:42
  14.7 1.6 %collective-permute-start.5 = (bf16[256,128]{1,0:T(8,128)(2,1)S(1)}, bf16[256,128]{1,0:T(8,128)(2,1)S(1)}, u32[]{:S(2)}, u32[]{:S(2)}) collective-permute-start(bf16[256,128]{1,0:T(8,128)(2,1)S(1)} %get-tuple-element.28), channel_id=1, source_target_pairs={{0,3},{1,2},{2,1},{3,0},{4,7},{5,6},{6,5},{7,4},{8,11},{9,10},{10,... | collective-permute-start | bytes 196616 | tf_op jit(solution)/shard_map/ppermute | solution.py:42
  16.3 3.1 %collective-permute-start.6 = (bf16[256,128]{1,0:T(8,128)(2,1)S(1)}, bf16[256,128]{1,0:T(8,128)(2,1)S(1)}, u32[]{:S(2)}, u32[]{:S(2)}) collective-permute-start(bf16[256,128]{1,0:T(8,128)(2,1)S(1)} %get-tuple-element.29), channel_id=1, source_target_pairs={{2,4},{3,5},{4,2},{5,3},{6,8},{7,9},{8,6},{9,7},{10,12},{11,13},{1... | collective-permute-start | bytes 196616 | tf_op jit(solution)/shard_map/ppermute | solution.py:42
  19.4 3.3 %collective-permute-start.7 = (bf16[256,128]{1,0:T(8,128)(2,1)S(1)}, bf16[256,128]{1,0:T(8,128)(2,1)S(1)}, u32[]{:S(2)}, u32[]{:S(2)}) collective-permute-start(bf16[256,128]{1,0:T(8,128)(2,1)S(1)} %get-tuple-element.30), channel_id=1, source_target_pairs={{2,5},{3,4},{4,3},{5,2},{6,9},{7,8},{8,7},{9,6},{10,13},{11,12},{1... | collective-permute-start | bytes 196616 | tf_op jit(solution)/shard_map/ppermute | solution.py:42
  22.7 0.0 copy-start
  22.8 0.2 turn.1.turned_ref
  23.0 3.9 %collective-permute-done.7.refs_4_ = bf16[256,128]{1,0:T(8,128)(2,1)S(1)} collective-permute-done((bf16[256,128]{1,0:T(8,128)(2,1)S(1)}, bf16[256,128]{1,0:T(8,128)(2,1)S(1)}, u32[]{:S(2)}, u32[]{:S(2)}) %collective-permute-start.7) | collective-permute-done | bytes 65568 | tf_op jit(solution)/shard_map/ppermute | solution.py:42
  26.9 10.2 %layer.2 = (bf16[1280,128]{1,0:T(8,128)(2,1)S(1)}, bf16[256,128]{1,0:T(8,128)(2,1)S(1)}, bf16[256,128]{1,0:T(8,128)(2,1)S(1)}, bf16[256,128]{1,0:T(8,128)(2,1)S(...) custom-call(bf16[1280,128]{1,0:T(8,128)(2,1)S(1)} %get-tuple-element.25.extended_ref, ...), custom_call_target="tpu_custom_call" | custom-call | tf_op jit(solution)/shard_map/layer/pallas_call | solution.py:269
  37.2 0.6 %collective-permute-start.8 = (bf16[256,128]{1,0:T(8,128)(2,1)S(1)}, bf16[256,128]{1,0:T(8,128)(2,1)S(1)}, u32[]{:S(2)}, u32[]{:S(2)}) collective-permute-start(bf16[256,128]{1,0:T(8,128)(2,1)S(1)} %get-tuple-element.32), channel_id=1, source_target_pairs={{0,1},{1,0},{2,3},{3,2},{4,5},{5,4},{6,7},{7,6},{8,9},{9,8},{10,11... | collective-permute-start | bytes 196616 | tf_op jit(solution)/shard_map/ppermute | solution.py:42
  37.8 1.6 %collective-permute-start.10 = (bf16[256,128]{1,0:T(8,128)(2,1)S(1)}, bf16[256,128]{1,0:T(8,128)(2,1)S(1)}, u32[]{:S(2)}, u32[]{:S(2)}) collective-permute-start(bf16[256,128]{1,0:T(8,128)(2,1)S(1)} %get-tuple-element.34), channel_id=1, source_target_pairs={{0,3},{1,2},{2,1},{3,0},{4,7},{5,6},{6,5},{7,4},{8,11},{9,10},{10,... | collective-permute-start | bytes 196616 | tf_op jit(solution)/shard_map/ppermute | solution.py:42
  39.4 2.9 %collective-permute-start.11 = (bf16[256,128]{1,0:T(8,128)(2,1)S(1)}, bf16[256,128]{1,0:T(8,128)(2,1)S(1)}, u32[]{:S(2)}, u32[]{:S(2)}) collective-permute-start(bf16[256,128]{1,0:T(8,128)(2,1)S(1)} %get-tuple-element.35), channel_id=1, source_target_pairs={{2,4},{3,5},{4,2},{5,3},{6,8},{7,9},{8,6},{9,7},{10,12},{11,13},{1... | collective-permute-start | bytes 196616 | tf_op jit(solution)/shard_map/ppermute | solution.py:42
  42.3 3.5 %collective-permute-start.12 = (bf16[256,128]{1,0:T(8,128)(2,1)S(1)}, bf16[256,128]{1,0:T(8,128)(2,1)S(1)}, u32[]{:S(2)}, u32[]{:S(2)}) collective-permute-start(bf16[256,128]{1,0:T(8,128)(2,1)S(1)} %get-tuple-element.36), channel_id=1, source_target_pairs={{2,5},{3,4},{4,3},{5,2},{6,9},{7,8},{8,7},{9,6},{10,13},{11,12},{1... | collective-permute-start | bytes 196616 | tf_op jit(solution)/shard_map/ppermute | solution.py:42
  45.9 3.9 %collective-permute-done.12.refs_4_ = bf16[256,128]{1,0:T(8,128)(2,1)S(1)} collective-permute-done((bf16[256,128]{1,0:T(8,128)(2,1)S(1)}, bf16[256,128]{1,0:T(8,128)(2,1)S(1)}, u32[]{:S(2)}, u32[]{:S(2)}) %collective-permute-start.12) | collective-permute-done | bytes 65568 | tf_op jit(solution)/shard_map/ppermute | solution.py:42
  49.8 9.7 %layer.3 = bf16[1280,128]{1,0:T(8,128)(2,1)} custom-call(bf16[1280,128]{1,0:T(8,128)(2,1)S(1)} %get-tuple-element.31.extended_ref, bf16[1280,128]{1,0:T(8,128)(2,1)S(1)} %turn.1.turned_ref, s32[16,80]{1,0:T(8,128)S(1)} %bitcast.11, bf16[2,3,128,128]{3,2,1,0:T(8,128)(2,1)S(1)} %copy-done, bf16[2,3,128,128]{3,2,1,0:T(8,128)(2,1)S(1)} %copy-done.1, ...), custom_call_target="tpu_custom_call" | custom-call | tf_op jit(solution)/shard_map/layer/pallas_call | solution.py:269
  (31 shorter events, 0.1 us)
Async XLA Ops:
  0.0 22.7 %copy-start.2 = (f32[1,1,4,16,1280]{4,3,2,1,0:T(8,128)S(1)}, f32[1,1,4,16,1280]{4,3,2,1,0:T(8,128)}, u32[]{:S(2)}) copy-start(f32[1,1,4,16,1280]{4,3,2,1,0:T(8,128)} %param.18) | copy-start | bytes 983044
  0.0 1.0 %copy-start.3 = (bf16[1,1,1024,128]{3,2,1,0:T(8,128)(2,1)S(1)}, bf16[1,1,1024,128]{3,2,1,0:T(8,128)(2,1)}, u32[]{:S(2)}) copy-start(bf16[1,1,1024,128]{3,2,1,0:T(8,128)(2,1)} %param.12) | copy-start | bytes 786436
  1.0 0.7 %copy-start.10 = (s32[1,1,4,64]{3,2,1,0:T(4,128)S(1)}, s32[1,1,4,64]{3,2,1,0:T(4,128)}, u32[]{:S(2)}) copy-start(s32[1,1,4,64]{3,2,1,0:T(4,128)} %param.13) | copy-start | bytes 3076
  1.7 0.7 %copy-start.11 = (s32[1,1,4]{2,1,0:T(1,128)S(1)}, s32[1,1,4]{2,1,0:T(1,128)}, u32[]{:S(2)}) copy-start(s32[1,1,4]{2,1,0:T(1,128)} %param.14) | copy-start | bytes 52
  3.5 5.0 %collective-permute-start = (bf16[64,128]{1,0:T(8,128)(2,1)S(1)}, bf16[64,128]{1,0:T(8,128)(2,1)S(1)}, u32[]{:S(2)}, u32[]{:S(2)}) collective-permute-start(bf16[64,128]{1,0:T(8,128)(2,1)S(1)} %get-tuple-element.22), channel_id=1, source_target_pairs={{0,1},{1,0},{2,3},{3,2},{4,5},{5,4},{6,7},{7,6},{8,9},{9,8},{10,11... | collective-permute-start | bytes 49160 | tf_op jit(solution)/shard_map/ppermute | solution.py:42
  5.1 3.4 %collective-permute-start.1 = (bf16[64,128]{1,0:T(8,128)(2,1)S(1)}, bf16[64,128]{1,0:T(8,128)(2,1)S(1)}, u32[]{:S(2)}, u32[]{:S(2)}) collective-permute-start(bf16[64,128]{1,0:T(8,128)(2,1)S(1)} %get-tuple-element.23), channel_id=1, source_target_pairs={{0,2},{1,3},{2,0},{3,1},{4,6},{5,7},{6,4},{7,5},{8,10},{9,11},{10,... | collective-permute-start | bytes 49160 | tf_op jit(solution)/shard_map/ppermute | solution.py:42
  5.1 5.9 %collective-permute-start.2 = (bf16[64,128]{1,0:T(8,128)(2,1)S(1)}, bf16[64,128]{1,0:T(8,128)(2,1)S(1)}, u32[]{:S(2)}, u32[]{:S(2)}) collective-permute-start(bf16[64,128]{1,0:T(8,128)(2,1)S(1)} %get-tuple-element.24), channel_id=1, source_target_pairs={{2,4},{3,5},{4,2},{5,3},{6,8},{7,9},{8,6},{9,7},{10,12},{11,13},{1... | collective-permute-start | bytes 49160 | tf_op jit(solution)/shard_map/ppermute | solution.py:42
  11.0 0.7 %copy-start.5 = (s32[1,1,8,256]{3,2,1,0:T(8,128)S(1)}, s32[1,1,8,256]{3,2,1,0:T(8,128)}, u32[]{:S(2)}) copy-start(s32[1,1,8,256]{3,2,1,0:T(8,128)} %param.15) | copy-start | bytes 24580
  14.1 8.9 %collective-permute-start.3 = (bf16[256,128]{1,0:T(8,128)(2,1)S(1)}, bf16[256,128]{1,0:T(8,128)(2,1)S(1)}, u32[]{:S(2)}, u32[]{:S(2)}) collective-permute-start(bf16[256,128]{1,0:T(8,128)(2,1)S(1)} %get-tuple-element.26), channel_id=1, source_target_pairs={{0,1},{1,0},{2,3},{3,2},{4,5},{5,4},{6,7},{7,6},{8,9},{9,8},{10,11... | collective-permute-start | bytes 196616 | tf_op jit(solution)/shard_map/ppermute | solution.py:42
  14.7 8.3 %collective-permute-start.4 = (bf16[256,128]{1,0:T(8,128)(2,1)S(1)}, bf16[256,128]{1,0:T(8,128)(2,1)S(1)}, u32[]{:S(2)}, u32[]{:S(2)}) collective-permute-start(bf16[256,128]{1,0:T(8,128)(2,1)S(1)} %get-tuple-element.27), channel_id=1, source_target_pairs={{0,2},{1,3},{2,0},{3,1},{4,6},{5,7},{6,4},{7,5},{8,10},{9,11},{10,... | collective-permute-start | bytes 196616 | tf_op jit(solution)/shard_map/ppermute | solution.py:42
  14.7 8.3 %collective-permute-start.5 = (bf16[256,128]{1,0:T(8,128)(2,1)S(1)}, bf16[256,128]{1,0:T(8,128)(2,1)S(1)}, u32[]{:S(2)}, u32[]{:S(2)}) collective-permute-start(bf16[256,128]{1,0:T(8,128)(2,1)S(1)} %get-tuple-element.28), channel_id=1, source_target_pairs={{0,3},{1,2},{2,1},{3,0},{4,7},{5,6},{6,5},{7,4},{8,11},{9,10},{10,... | collective-permute-start | bytes 196616 | tf_op jit(solution)/shard_map/ppermute | solution.py:42
  16.3 6.7 %collective-permute-start.6 = (bf16[256,128]{1,0:T(8,128)(2,1)S(1)}, bf16[256,128]{1,0:T(8,128)(2,1)S(1)}, u32[]{:S(2)}, u32[]{:S(2)}) collective-permute-start(bf16[256,128]{1,0:T(8,128)(2,1)S(1)} %get-tuple-element.29), channel_id=1, source_target_pairs={{2,4},{3,5},{4,2},{5,3},{6,8},{7,9},{8,6},{9,7},{10,12},{11,13},{1... | collective-permute-start | bytes 196616 | tf_op jit(solution)/shard_map/ppermute | solution.py:42
  19.4 7.5 %collective-permute-start.7 = (bf16[256,128]{1,0:T(8,128)(2,1)S(1)}, bf16[256,128]{1,0:T(8,128)(2,1)S(1)}, u32[]{:S(2)}, u32[]{:S(2)}) collective-permute-start(bf16[256,128]{1,0:T(8,128)(2,1)S(1)} %get-tuple-element.30), channel_id=1, source_target_pairs={{2,5},{3,4},{4,3},{5,2},{6,9},{7,8},{8,7},{9,6},{10,13},{11,12},{1... | collective-permute-start | bytes 196616 | tf_op jit(solution)/shard_map/ppermute | solution.py:42
  22.7 4.2 %copy-start = (bf16[2,3,128,128]{3,2,1,0:T(8,128)(2,1)S(1)}, bf16[2,3,128,128]{3,2,1,0:T(8,128)(2,1)}, u32[]{:S(2)}) copy-start(bf16[2,3,128,128]{3,2,1,0:T(8,128)(2,1)} %edge_ref.3) | copy-start | bytes 589828
  22.7 4.2 %copy-start.1 = (bf16[2,3,128,128]{3,2,1,0:T(8,128)(2,1)S(1)}, bf16[2,3,128,128]{3,2,1,0:T(8,128)(2,1)}, u32[]{:S(2)}) copy-start(bf16[2,3,128,128]{3,2,1,0:T(8,128)(2,1)} %node_ref.3) | copy-start | bytes 589828
  22.7 4.2 %copy-start.4 = (s32[1,1,16,80]{3,2,1,0:T(8,128)S(1)}, s32[1,1,16,80]{3,2,1,0:T(8,128)}, u32[]{:S(2)}) copy-start(s32[1,1,16,80]{3,2,1,0:T(8,128)} %param.17) | copy-start | bytes 15364
  22.8 4.2 %copy-start.6 = (f32[2,4,128]{2,1,0:T(4,128)S(1)}, f32[2,4,128]{2,1,0:T(4,128)}, u32[]{:S(2)}) copy-start(f32[2,4,128]{2,1,0:T(4,128)} %geo_ref.3) | copy-start | bytes 12292
  22.8 4.2 %copy-start.7 = (f32[2,4,128]{2,1,0:T(4,128)S(1)}, f32[2,4,128]{2,1,0:T(4,128)}, u32[]{:S(2)}) copy-start(f32[2,4,128]{2,1,0:T(4,128)} %bias_ref.3) | copy-start | bytes 12292
  23.0 4.0 %copy-start.8 = (f32[2,2,128]{2,1,0:T(2,128)S(1)}, f32[2,2,128]{2,1,0:T(2,128)}, u32[]{:S(2)}) copy-start(f32[2,2,128]{2,1,0:T(2,128)} %gain_ref.3) | copy-start | bytes 6148
  37.2 8.6 %collective-permute-start.8 = (bf16[256,128]{1,0:T(8,128)(2,1)S(1)}, bf16[256,128]{1,0:T(8,128)(2,1)S(1)}, u32[]{:S(2)}, u32[]{:S(2)}) collective-permute-start(bf16[256,128]{1,0:T(8,128)(2,1)S(1)} %get-tuple-element.32), channel_id=1, source_target_pairs={{0,1},{1,0},{2,3},{3,2},{4,5},{5,4},{6,7},{7,6},{8,9},{9,8},{10,11... | collective-permute-start | bytes 196616 | tf_op jit(solution)/shard_map/ppermute | solution.py:42
  37.8 8.1 %collective-permute-start.9 = (bf16[256,128]{1,0:T(8,128)(2,1)S(1)}, bf16[256,128]{1,0:T(8,128)(2,1)S(1)}, u32[]{:S(2)}, u32[]{:S(2)}) collective-permute-start(bf16[256,128]{1,0:T(8,128)(2,1)S(1)} %get-tuple-element.33), channel_id=1, source_target_pairs={{0,2},{1,3},{2,0},{3,1},{4,6},{5,7},{6,4},{7,5},{8,10},{9,11},{10,... | collective-permute-start | bytes 196616 | tf_op jit(solution)/shard_map/ppermute | solution.py:42
  37.8 8.1 %collective-permute-start.10 = (bf16[256,128]{1,0:T(8,128)(2,1)S(1)}, bf16[256,128]{1,0:T(8,128)(2,1)S(1)}, u32[]{:S(2)}, u32[]{:S(2)}) collective-permute-start(bf16[256,128]{1,0:T(8,128)(2,1)S(1)} %get-tuple-element.34), channel_id=1, source_target_pairs={{0,3},{1,2},{2,1},{3,0},{4,7},{5,6},{6,5},{7,4},{8,11},{9,10},{10,... | collective-permute-start | bytes 196616 | tf_op jit(solution)/shard_map/ppermute | solution.py:42
  39.4 6.5 %collective-permute-start.11 = (bf16[256,128]{1,0:T(8,128)(2,1)S(1)}, bf16[256,128]{1,0:T(8,128)(2,1)S(1)}, u32[]{:S(2)}, u32[]{:S(2)}) collective-permute-start(bf16[256,128]{1,0:T(8,128)(2,1)S(1)} %get-tuple-element.35), channel_id=1, source_target_pairs={{2,4},{3,5},{4,2},{5,3},{6,8},{7,9},{8,6},{9,7},{10,12},{11,13},{1... | collective-permute-start | bytes 196616 | tf_op jit(solution)/shard_map/ppermute | solution.py:42
  42.3 7.5 %collective-permute-start.12 = (bf16[256,128]{1,0:T(8,128)(2,1)S(1)}, bf16[256,128]{1,0:T(8,128)(2,1)S(1)}, u32[]{:S(2)}, u32[]{:S(2)}) collective-permute-start(bf16[256,128]{1,0:T(8,128)(2,1)S(1)} %get-tuple-element.36), channel_id=1, source_target_pairs={{2,5},{3,4},{4,3},{5,2},{6,9},{7,8},{8,7},{9,6},{10,13},{11,12},{1... | collective-permute-start | bytes 196616 | tf_op jit(solution)/shard_map/ppermute | solution.py:42
  (1 other events, 0.7 us)

commit v2 on v1

v2 whole, which is shorter than its diff:
```python
import functools
import itertools
import math

import jax
import jax.numpy as jnp
from jax import lax
from jax.experimental import pallas as pl
from jax.experimental.pallas import tpu as pltpu
from jax.sharding import PartitionSpec as P

F32 = jnp.float32
BF16 = jnp.bfloat16
CHUNK = 256
VMEM = pl.BlockSpec(memory_space=pltpu.VMEM)
SMEM = pl.BlockSpec(memory_space=pltpu.SMEM)
HBM = pl.BlockSpec(memory_space=pltpu.HBM)
PARAMS = pltpu.CompilerParams(vmem_limit_bytes=24 * 1024 * 1024)
WHOLE = pltpu.CompilerParams(vmem_limit_bytes=64 * 1024 * 1024)


def partner(place, count, kind):
    other = place + 1 if place % 2 == kind else place - 1
    return other if 0 <= other < count else None


def kinds(count):
    return [0, 1][: max(0, min(2, count - 1))]


def links(count_x, count_y):
    both = itertools.product(kinds(count_x)[::-1] + [None], kinds(count_y)[::-1] + [None])
    return [pair for pair in both if pair != (None, None)]


def swap(value, link):
    count_x, count_y = lax.axis_size("gx"), lax.axis_size("gy")
    pairs = []
    for x, y in itertools.product(range(count_x), range(count_y)):
        to_x = x if link[0] is None else partner(x, count_x, link[0])
        to_y = y if link[1] is None else partner(y, count_y, link[1])
        if to_x is not None and to_y is not None:
            pairs.append((x * count_y + y, to_x * count_y + to_y))
    return lax.ppermute(value, ("gx", "gy"), pairs)


def step(axis, kind):
    if kind is None:
        return 0
    sign = 1 if kind == 0 else -1
    return sign * (1 - 2 * lax.rem(lax.axis_index(axis), 2))


def section(step_x, step_y):
    place = (step_x + 1) * 3 + step_y + 1
    return jnp.where(place > 4, place - 1, place)


def side(link):
    if link[1] is None:
        return (step("gx", link[0]) + 1) // 2
    return 2 + (step("gy", link[1]) + 1) // 2


def fetch(sources, targets, sems):
    copies = [pltpu.make_async_copy(*ends, sems.at[place]) for place, ends in enumerate(zip(sources, targets))]
    for copy in copies:
        copy.start()
    for copy in copies:
        copy.wait()


def fetched(*arrays, smem=()):
    held = [
        (pltpu.SMEM if place in smem else pltpu.VMEM)(array.shape, array.dtype) for place, array in enumerate(arrays)
    ]
    return held + [pltpu.SemaphoreType.DMA((len(arrays),))]


def pack_kernel(sides, latents_hbm, rows_hbm, count_hbm, retained_ref, *refs):
    packet_refs, (latents_ref, rows_ref, count_ref, sems) = refs[: len(sides)], refs[len(sides) :]
    fetch((latents_hbm, rows_hbm, count_hbm), (latents_ref, rows_ref, count_ref), sems)
    total = latents_ref.shape[0]
    slots = rows_ref.shape[1]
    owned = latents_ref[...]
    row_id = lax.broadcasted_iota(jnp.int32, (total, slots), 0)
    lane = lax.broadcasted_iota(jnp.int32, (1, slots), 1)

    def picker(direction):
        wanted = rows_ref[pl.ds(direction, 1), :]
        wanted = jnp.where(lane < count_ref[direction], wanted, -1)
        return (row_id == wanted).astype(F32)

    marks = picker(0)
    for direction in range(1, 4):
        marks = marks + picker(direction)
    marks = jnp.dot(marks.astype(BF16), jnp.ones((slots, owned.shape[1]), BF16), preferred_element_type=F32)
    retained_ref[...] = jnp.where(marks > 0.0, 0.0, owned.astype(F32)).astype(BF16)
    for link, packet_ref in zip(sides, packet_refs):
        chosen = lax.dot_general(
            picker(side(link)).astype(BF16), owned, (((0,), (0,)), ((), ())), preferred_element_type=F32
        )
        packet_ref[...] = chosen.astype(BF16)


def gather_ghosts(extended_ref, wanted_ref, send_refs):
    total = extended_ref.shape[0]
    column = lax.broadcasted_iota(jnp.int32, wanted_ref.shape[1:], 1).astype(F32)
    for place, send_ref in enumerate(send_refs):
        wanted = wanted_ref[place]
        picker = jnp.concatenate(
            [jnp.where(wanted == column + float(start), 1.0, 0.0).astype(BF16) for start in range(0, total, 128)],
            axis=1,
        )
        send_ref[...] = jnp.dot(picker, extended_ref[...], preferred_element_type=F32).astype(BF16)


def build_kernel(sides, retained_ref, *refs):
    arrivals, refs = refs[: len(sides)], refs[len(sides) :]
    wanted_ref, extended_ref, *send_refs = refs
    total = extended_ref.shape[0]
    owned = retained_ref.shape[0]
    slots = (total - owned) // 4
    extended_ref[pl.ds(0, owned), :] = retained_ref[...]
    extended_ref[pl.ds(owned, total - owned), :] = jnp.zeros((total - owned, extended_ref.shape[1]), BF16)
    for link, arrival_ref in zip(sides, arrivals):
        start = pl.multiple_of(owned + slots * side(link), 16)
        extended_ref[pl.ds(start, slots), :] = arrival_ref[...]
    gather_ghosts(extended_ref, wanted_ref, send_refs)


def want_kernel(all_links, rows_ref, count_ref, wanted_ref):
    ghosts = rows_ref.shape[1]
    lane = lax.broadcasted_iota(jnp.int32, (1, ghosts), 1)
    for place, link in enumerate(all_links):
        target = section(step("gx", link[0]), step("gy", link[1]))
        wanted = rows_ref[pl.ds(target, 1), :]
        wanted = jnp.where(lane < count_ref[target], wanted, -1).astype(F32)
        wanted_ref[place] = jnp.transpose(jnp.broadcast_to(wanted, (128, ghosts)))


def static_kernel(geometry_ref, edge_ref, geo_ref, extended_ref, turned_ref, first_ref, second_ref):
    del extended_ref
    feats = geometry_ref[...]
    high = feats.astype(BF16).astype(F32)
    turned_ref[...] = jnp.transpose(jnp.concatenate([high, feats - high], axis=0)).astype(BF16)

    layers, channels, width = geo_ref.shape
    slots = first_ref.shape[2] // width
    part_rows = channels * slots
    slot_of = lax.rem(lax.broadcasted_iota(jnp.int32, (part_rows, width), 0), slots)
    second_ref[...] = jnp.zeros(second_ref.shape, BF16)
    for layer in range(layers):
        spread_geo = jnp.concatenate(
            [jnp.broadcast_to(geo_ref[layer, pl.ds(c, 1), :], (slots, width)) for c in range(channels)], axis=0
        )
        for slot in range(slots):
            part = jnp.where(slot_of == slot, spread_geo, 0.0).astype(BF16)
            columns = pl.ds(slot * width, width)
            first_ref[layer, pl.ds(0, part_rows), columns] = part
            first_ref[layer, pl.ds(part_rows, part_rows), columns] = part
            first_ref[layer, pl.ds(2 * part_rows, width), columns] = edge_ref[layer, 0]
        edge_second = edge_ref[layer, 2].astype(F32)
        edge_second = (edge_second - jnp.mean(edge_second, axis=-1, keepdims=True)).astype(BF16)
        second_ref[layer, pl.ds(0, width), pl.ds(0, width)] = edge_second
        second_ref[layer, pl.ds(width, width), pl.ds(width, width)] = edge_second


def receive_kernel(layer, extended_ref, turned_ref, first_ref, edge_ref, bias_ref, base_ref, table_ref):
    own = jnp.concatenate([turned_ref[...], extended_ref[...]], axis=1)
    width = extended_ref.shape[1]
    bias = bias_ref[layer, pl.ds(0, 1), :]
    bias = jnp.concatenate([bias, bias], axis=1)
    for start in range(0, base_ref.shape[1], 2 * width):
        columns = pl.ds(start, 2 * width)
        base_ref[:, columns] = (jnp.dot(own, first_ref[layer, :, columns], preferred_element_type=F32) + bias).astype(BF16)
    table_ref[...] = jnp.dot(extended_ref[...], edge_ref[layer, 1], preferred_element_type=F32)


def spread_of(center):
    return jnp.sum(center * center, axis=-1, keepdims=True)


def layer_kernel(
    layer, last, all_links, extended_ref, base_ref, own_ref, links_ref, edge_ref, node_ref, second_ref, bias_ref, gain_ref, *refs
):
    landed, refs = refs[: len(all_links)], refs[len(all_links) :]
    if not last:
        wanted_ref, *refs = refs
    updated_ref, *send_refs, table_ref, hidden_ref, total_ref = refs
    rows_total, width = extended_ref.shape
    slots, tiles = links_ref.shape
    rows = rows_total // tiles
    ghosts = landed[0].shape[0]

    sender_mat = edge_ref[layer, 1]
    table_ref[pl.ds(0, rows_total), :] = own_ref[...]
    if len(all_links) < 8:
        table_ref[pl.ds(rows_total, 8 * ghosts), :] = jnp.zeros((8 * ghosts, width), F32)
    for link, landed_ref in zip(all_links, landed):
        source = section(-step("gx", link[0]), -step("gy", link[1]))
        start = pl.multiple_of(rows_total + ghosts * source, 16)
        table_ref[pl.ds(start, ghosts), :] = jnp.dot(landed_ref[...], sender_mat, preferred_element_type=F32)
    bias_second = bias_ref[layer, pl.ds(1, 1), :]
    bias_second = bias_second - jnp.mean(bias_second, axis=-1, keepdims=True)

    chunk_rows = math.gcd(rows_total, CHUNK)
    chunk_tiles = chunk_rows // rows
    chunks = range(0, rows_total, chunk_rows)
    for pair in range(0, slots, 2):
        for start in chunks:
            halves = []
            for slot in (pair, pair + 1):
                senders = []
                for tile in range(start // rows, start // rows + chunk_tiles):
                    picked = table_ref[pl.ds(jnp.maximum(links_ref[slot, tile], 0), 1), :]
                    senders.append(jnp.broadcast_to(picked, (rows, width)))
                halves.append(jnp.concatenate(senders, axis=0))
            base = base_ref[pl.ds(start, chunk_rows), pl.ds(pair * width, 2 * width)].astype(F32)
            hidden = jnp.maximum(base + jnp.concatenate(halves, axis=1), 0.0)
            hidden_ref[pl.ds(start, chunk_rows), :] = hidden.astype(BF16)
        for start in chunks:
            second = jnp.dot(hidden_ref[pl.ds(start, chunk_rows), :], second_ref[layer], preferred_element_type=F32)
            for place in range(0, chunk_rows, rows):
                tile = (start + place) // rows
                total = 0.0 if pair == 0 else total_ref[pl.ds(start + place, rows), :]
                for half in range(2):
                    center = second[place : place + rows, half * width : (half + 1) * width] + bias_second
                    limit = jnp.where(links_ref[pair + half, tile] >= 0, width * 1e-5, jnp.inf)
                    total = total + center * lax.rsqrt(spread_of(center) + limit)
                total_ref[pl.ds(start + place, rows), :] = total

    gathered = (total_ref[...] * (gain_ref[layer, pl.ds(0, 1), :] * math.sqrt(width))).astype(BF16)
    extended = extended_ref[...]
    node_first = jnp.dot(
        jnp.concatenate([extended, gathered], axis=1),
        jnp.concatenate([node_ref[layer, 0], node_ref[layer, 1]], axis=0),
        preferred_element_type=F32,
    )
    node_hidden = jnp.maximum(node_first + bias_ref[layer, pl.ds(2, 1), :], 0.0).astype(BF16)
    node_out = jnp.dot(node_hidden, node_ref[layer, 2], preferred_element_type=F32) + bias_ref[layer, pl.ds(3, 1), :]
    center = node_out - jnp.mean(node_out, axis=-1, keepdims=True)
    scale = lax.rsqrt(spread_of(center) / width + 1e-5)
    updated_ref[...] = (extended.astype(F32) + center * scale * gain_ref[layer, pl.ds(1, 1), :]).astype(BF16)
    if not last:
        gather_ghosts(updated_ref, wanted_ref, send_refs)


def body(
    latents, mig_rows, mig_count, ghost_rows, ghost_count, neighbours, geometry, edge_w, node_w, geo_w, biases, gains
):
    owned = latents[0, 0]
    leave_rows, leave_count = mig_rows[0, 0], mig_count[0, 0]
    ghost_list, ghost_total = ghost_rows[0, 0], ghost_count[0, 0]
    tile_links = neighbours[0, 0]
    width = owned.shape[1]
    slots, tiles = tile_links.shape
    rows_total = geometry.shape[-1]
    ghosts = ghost_list.shape[1]
    table_rows = rows_total + 8 * ghosts
    all_links = links(lax.axis_size("gx"), lax.axis_size("gy"))
    sides = [link for link in all_links if None in link]
    rows_of = lambda count: jax.ShapeDtypeStruct((count, width), BF16)

    retained, *packets = pl.pallas_call(
        functools.partial(pack_kernel, sides),
        out_shape=[rows_of(owned.shape[0])] + [rows_of(leave_rows.shape[1])] * len(sides),
        in_specs=[HBM] * 3,
        out_specs=[VMEM] * (1 + len(sides)),
        scratch_shapes=fetched(owned, leave_rows, leave_count, smem=(2,)),
        compiler_params=WHOLE,
        name="pack",
    )(owned, leave_rows, leave_count)
    arrivals = [swap(packet, link) for packet, link in zip(packets, sides)]

    feats = geometry.reshape(-1, rows_total)
    layers = edge_w.shape[0]
    deep = 2 * feats.shape[0] + width
    wanted = pl.pallas_call(
        functools.partial(want_kernel, all_links),
        out_shape=jax.ShapeDtypeStruct((len(all_links), ghosts, 128), F32),
        in_specs=[VMEM, SMEM],
        out_specs=VMEM,
        compiler_params=PARAMS,
        cost_estimate=pl.CostEstimate(flops=500_000_000, bytes_accessed=1_000_000, transcendentals=0),
        name="want",
    )(ghost_list, ghost_total)
    extended, *sends = pl.pallas_call(
        functools.partial(build_kernel, sides),
        out_shape=[rows_of(rows_total)] + [rows_of(ghosts)] * len(all_links),
        in_specs=[VMEM] * (2 + len(sides)),
        out_specs=[VMEM] * (1 + len(all_links)),
        compiler_params=PARAMS,
        name="build",
    )(retained, *arrivals, wanted)

    turned, first_mats, second_mats = pl.pallas_call(
        static_kernel,
        out_shape=[
            jax.ShapeDtypeStruct((rows_total, 2 * feats.shape[0]), BF16),
            jax.ShapeDtypeStruct((layers, deep, slots * width), BF16),
            jax.ShapeDtypeStruct((layers, 2 * width, 2 * width), BF16),
        ],
        in_specs=[VMEM] * 3 + [pl.BlockSpec(memory_space=pl.ANY)],
        out_specs=[VMEM] * 3,
        compiler_params=PARAMS,
        cost_estimate=pl.CostEstimate(flops=1_000_000_000, bytes_accessed=3_000_000, transcendentals=0),
        name="static",
    )(feats, edge_w, geo_w, extended)

    for layer in range(layers):
        last = layer == layers - 1
        landed = [swap(send, link) for send, link in zip(sends, all_links)]
        base, own = pl.pallas_call(
            functools.partial(receive_kernel, layer),
            out_shape=[
                jax.ShapeDtypeStruct((rows_total, slots * width), BF16),
                jax.ShapeDtypeStruct((rows_total, width), F32),
            ],
            in_specs=[VMEM] * 5,
            out_specs=[VMEM] * 2,
            compiler_params=PARAMS,
            cost_estimate=pl.CostEstimate(flops=2_500_000_000, bytes_accessed=6_000_000, transcendentals=0),
            name="receive",
        )(extended, turned, first_mats, edge_w, biases)
        outs = [rows_of(rows_total)] + ([] if last else [rows_of(ghosts)] * len(all_links))
        extra = [] if last else [wanted]
        extended, *sends = pl.pallas_call(
            functools.partial(layer_kernel, layer, last, all_links),
            out_shape=outs,
            in_specs=[VMEM] * 3 + [SMEM] + [VMEM] * (5 + len(all_links) + len(extra)),
            out_specs=[VMEM] * len(outs),
            scratch_shapes=[
                pltpu.VMEM((table_rows, width), F32),
                pltpu.VMEM((rows_total, 2 * width), BF16),
                pltpu.VMEM((rows_total, width), F32),
            ],
            compiler_params=PARAMS,
            name="layer",
        )(extended, base, own, tile_links, edge_w, node_w, second_mats, biases, gains, *landed, *extra)
    return extended[None, None]


def solution(mesh):
    block = lambda rank: P("gx", "gy", *[None] * rank)
    return jax.shard_map(
        body,
        mesh=mesh,
        in_specs=(block(2), block(2), block(1), block(2), block(1), block(2), block(3), P(), P(), P(), P(), P()),
        out_specs=block(2),
        check_vma=False,
    )
```

time: 60.5 us -> 52.6 us (0.87)
  waiting for transfers between devices: 10.3 us -> 2.3 us
  Pallas kernels: 23 us -> 21.1 us
  starting transfers between devices: 22.2 us -> 23.6 us
  local copies, waits for them, and re-layouts: 3.73 us -> 4.92 us
    ppermute x13, waiting for transfers between devices: 10.3 us -> 2.3 us  [swap(): return lax.ppermute(value, ('gx', 'gy'), pairs)]
    pallas_call x2, Pallas kernels: 20 us -> 13.2 us  [body(): pl.pallas_call(functools.partial(layer_kernel, layer, last, all_links), o...]
    pallas_call x2 -> x5, Pallas kernels: 1.85 us -> 5.59 us  [the longest x2 3.35 us: body(): pl.pallas_call(functools.partial(receive_kernel, layer), out_shape=[jax.S...]
    ppermute x13, starting transfers between devices: 22.2 us -> 23.6 us  [swap(): return lax.ppermute(value, ('gx', 'gy'), pairs)]
    unnamed x24 -> x22, local copies, waits for them, and re-layouts: 3.73 us -> 4.92 us
    pallas_call x1, Pallas kernels: 1.18 us -> 2.29 us  [body(): pl.pallas_call(functools.partial(pack_kernel, sides), out_shape=[rows_of(...]
  transfers between devices with their start and end apart: 13 -> 13, of which waited for: 3 -> 3; matrix products, arithmetic and copies ran while one was open for 0% -> 0% of each run, Pallas kernels for 0% -> 9%
where the time goes in v2:
time: 52.6 us; the launch traced here: 52.2 us
  starting transfers between devices  23.6 us (45%)
  Pallas kernels  21.1 us (40%)
  local copies, waits for them, and re-layouts  4.92 us (9%)
  waiting for transfers between devices  2.3 us (4%)
    ppermute x13, starting transfers between devices, swap(): return lax.ppermute(value, ('gx', 'gy'), pairs)  23.6 us
    pallas_call x2, Pallas kernels, body(): pl.pallas_call(functools.partial(layer_kernel, layer, last, all_links), o...  13.2 us
    unnamed x22, local copies, waits for them, and re-layouts  4.92 us
    pallas_call x2, Pallas kernels, body(): pl.pallas_call(functools.partial(receive_kernel, layer), out_shape=[jax.S...  3.35 us
    ppermute x13, waiting for transfers between devices, swap(): return lax.ppermute(value, ('gx', 'gy'), pairs)  2.3 us
    pallas_call x1, Pallas kernels, body(): pl.pallas_call(functools.partial(pack_kernel, sides), out_shape=[rows_of(...  2.29 us
  transfers between devices with their start and end apart: 13, of which 3 were waited for; matrix products, arithmetic and copies ran while one was open for 0% of the time, Pallas kernels for 9%

profile of v2, /device:TPU:8, one launch (start us, length us, event | category | flops | bytes accessed | tf_op | source)
XLA Modules:
  0.0 52.2 jit_solution(2679727603974988435)
XLA Ops:
  0.0 2.3 %pack.1 = (bf16[1024,128]{1,0:T(8,128)(2,1)}, bf16[64,128]{1,0:T(8,128)(2,1)}, bf16[64,128]{1,0:T(8,128)(2,1)}, bf16[64,128]{1,0:T(8,128)(2,1)}) custom-call(bf16[1024,128]{1,0:T(8,128)(2,1)} %bitcast.13, s32[4,64]{1,0:T(4,128)} %bitcast.14, s32[4]{0:T(128)} %bitcast.15), custom_call_target="tpu_custom_call" | custom-call | tf_op jit(solution)/shard_map/pack/pallas_call | solution.py:265
  2.3 2.9 %collective-permute-start = (bf16[64,128]{1,0:T(8,128)(2,1)}, bf16[64,128]{1,0:T(8,128)(2,1)S(1)}, u32[]{:S(2)}, u32[]{:S(2)}) collective-permute-start(bf16[64,128]{1,0:T(8,128)(2,1)} %get-tuple-element.29), channel_id=1, source_target_pairs={{2,4},{3,5},{4,2},{5,3},{6,8},{7,9},{8,6},{9,7},{10,12},{11,13},{1... | collective-permute-start | bytes 49160 | tf_op jit(solution)/shard_map/ppermute | solution.py:44
  5.2 0.9 %collective-permute-start.1 = (bf16[64,128]{1,0:T(8,128)(2,1)}, bf16[64,128]{1,0:T(8,128)(2,1)S(1)}, u32[]{:S(2)}, u32[]{:S(2)}) collective-permute-start(bf16[64,128]{1,0:T(8,128)(2,1)} %get-tuple-element.30), channel_id=1, source_target_pairs={{0,2},{1,3},{2,0},{3,1},{4,6},{5,7},{6,4},{7,5},{8,10},{9,11},{10,... | collective-permute-start | bytes 49160 | tf_op jit(solution)/shard_map/ppermute | solution.py:44
  6.1 1.5 %collective-permute-start.2 = (bf16[64,128]{1,0:T(8,128)(2,1)}, bf16[64,128]{1,0:T(8,128)(2,1)S(1)}, u32[]{:S(2)}, u32[]{:S(2)}) collective-permute-start(bf16[64,128]{1,0:T(8,128)(2,1)} %get-tuple-element.31), channel_id=1, source_target_pairs={{0,1},{1,0},{2,3},{3,2},{4,5},{5,4},{6,7},{7,6},{8,9},{9,8},{10,11... | collective-permute-start | bytes 49160 | tf_op jit(solution)/shard_map/ppermute | solution.py:44
  7.6 0.7 %copy-done.8 = s32[1,1,8,256]{3,2,1,0:T(8,128)S(1)} copy-done((s32[1,1,8,256]{3,2,1,0:T(8,128)S(1)}, s32[1,1,8,256]{3,2,1,0:T(8,128)}, u32[]{:S(2)}) %copy-start.8) | copy-done | bytes 8216
  8.3 0.7 %copy-done.10 = s32[1,1,8]{2,1,0:T(1,128)S(1)} copy-done((s32[1,1,8]{2,1,0:T(1,128)S(1)}, s32[1,1,8]{2,1,0:T(1,128)}, u32[]{:S(2)}) %copy-start.10) | copy-done | bytes 56
  8.9 0.8 %want.1.refs_3_.refs_5_ = f32[5,256,128]{2,1,0:T(8,128)S(1)} custom-call(s32[8,256]{1,0:T(8,128)S(1)} %bitcast.11, s32[8]{0:T(128)S(1)} %bitcast.12), custom_call_target="tpu_custom_call" | custom-call | flops 500000000 | bytes 1000000 | tf_op jit(solution)/shard_map/want/pallas_call | solution.py:279
  10.0 0.9 %copy-done.3 = bf16[1024,128]{1,0:T(8,128)(2,1)S(1)} copy-done((bf16[1024,128]{1,0:T(8,128)(2,1)S(1)}, bf16[1024,128]{1,0:T(8,128)(2,1)}, u32[]{:S(2)}) %copy-start.3) | copy-done | bytes 262168
  11.0 1.0 %build.1 = (bf16[1280,128]{1,0:T(8,128)(2,1)S(1)}, bf16[256,128]{1,0:T(8,128)(2,1)S(1)}, bf16[256,128]{1,0:T(8,128)(2,1)S(1)}, bf16[256,128]{1,0:T(8,128)(2,1)S(...) custom-call(bf16[1024,128]{1,0:T(8,128)(2,1)S(1)} %copy-done.3, ...), custom_call_target="tpu_custom_call" | custom-call | tf_op jit(solution)/shard_map/build/pallas_call | solution.py:288
  12.0 2.8 %collective-permute-start.3 = (bf16[256,128]{1,0:T(8,128)(2,1)S(1)}, bf16[256,128]{1,0:T(8,128)(2,1)S(1)}, u32[]{:S(2)}, u32[]{:S(2)}) collective-permute-start(bf16[256,128]{1,0:T(8,128)(2,1)S(1)} %get-tuple-element.38), channel_id=1, source_target_pairs={{2,5},{3,4},{4,3},{5,2},{6,9},{7,8},{8,7},{9,6},{10,13},{11,12},{1... | collective-permute-start | bytes 196616 | tf_op jit(solution)/shard_map/ppermute | solution.py:44
  14.8 4.6 %collective-permute-start.4 = (bf16[256,128]{1,0:T(8,128)(2,1)S(1)}, bf16[256,128]{1,0:T(8,128)(2,1)S(1)}, u32[]{:S(2)}, u32[]{:S(2)}) collective-permute-start(bf16[256,128]{1,0:T(8,128)(2,1)S(1)} %get-tuple-element.39), channel_id=1, source_target_pairs={{2,4},{3,5},{4,2},{5,3},{6,8},{7,9},{8,6},{9,7},{10,12},{11,13},{1... | collective-permute-start | bytes 196616 | tf_op jit(solution)/shard_map/ppermute | solution.py:44
  19.5 0.6 %collective-permute-start.6 = (bf16[256,128]{1,0:T(8,128)(2,1)S(1)}, bf16[256,128]{1,0:T(8,128)(2,1)S(1)}, u32[]{:S(2)}, u32[]{:S(2)}) collective-permute-start(bf16[256,128]{1,0:T(8,128)(2,1)S(1)} %get-tuple-element.41), channel_id=1, source_target_pairs={{0,2},{1,3},{2,0},{3,1},{4,6},{5,7},{6,4},{7,5},{8,10},{9,11},{10,... | collective-permute-start | bytes 196616 | tf_op jit(solution)/shard_map/ppermute | solution.py:44
  20.1 1.5 %collective-permute-start.7 = (bf16[256,128]{1,0:T(8,128)(2,1)S(1)}, bf16[256,128]{1,0:T(8,128)(2,1)S(1)}, u32[]{:S(2)}, u32[]{:S(2)}) collective-permute-start(bf16[256,128]{1,0:T(8,128)(2,1)S(1)} %get-tuple-element.42), channel_id=1, source_target_pairs={{0,1},{1,0},{2,3},{3,2},{4,5},{5,4},{6,7},{7,6},{8,9},{9,8},{10,11... | collective-permute-start | bytes 196616 | tf_op jit(solution)/shard_map/ppermute | solution.py:44
  21.6 0.9 %copy-done = bf16[2,3,128,128]{3,2,1,0:T(8,128)(2,1)S(1)} copy-done((bf16[2,3,128,128]{3,2,1,0:T(8,128)(2,1)S(1)}, bf16[2,3,128,128]{3,2,1,0:T(8,128)(2,1)}, u32[]{:S(2)}) %copy-start) | copy-done | bytes 196632
  22.6 1.0 %copy-done.7 = f32[1,1,4,16,1280]{4,3,2,1,0:T(8,128)S(1)} copy-done((f32[1,1,4,16,1280]{4,3,2,1,0:T(8,128)S(1)}, f32[1,1,4,16,1280]{4,3,2,1,0:T(8,128)}, u32[]{:S(2)}) %copy-start.7) | copy-done | bytes 327704
  23.5 0.7 %copy-done.9 = f32[2,4,128]{2,1,0:T(4,128)S(1)} copy-done((f32[2,4,128]{2,1,0:T(4,128)S(1)}, f32[2,4,128]{2,1,0:T(4,128)}, u32[]{:S(2)}) %copy-start.9) | copy-done | bytes 4120
  24.7 1.6 %receive.2 = (bf16[1280,2048]{1,0:T(8,128)(2,1)S(1)}, f32[1280,128]{1,0:T(8,128)S(1)}) custom-call(bf16[1280,128]{1,0:T(8,128)(2,1)S(1)} %get-tuple-element.32.extended_ref, bf16[1280,128]{1,0:T(8,128)(2,1)S(1)} %get-tuple-element.33.turned_ref, bf16[2,256,2048]{2,1,0:T(8,128)(2,1)S(1)} %get-tuple-element.34.first_ref, ...), custom_call_target="tpu_custom_call" | custom-call | flops 2500000000 | bytes 6000000 | tf_op jit(solution)/shard_map/receive/pallas_call | solution.py:314
  26.4 6.6 %layer.2 = (bf16[1280,128]{1,0:T(8,128)(2,1)S(1)}, bf16[256,128]{1,0:T(8,128)(2,1)S(1)}, bf16[256,128]{1,0:T(8,128)(2,1)S(1)}, bf16[256,128]{1,0:T(8,128)(2,1)S(...) custom-call(bf16[1280,128]{1,0:T(8,128)(2,1)S(1)} %get-tuple-element.32.extended_ref, ...), custom_call_target="tpu_custom_call" | custom-call | tf_op jit(solution)/shard_map/layer/pallas_call | solution.py:328
  33.0 2.2 %collective-permute-start.8 = (bf16[256,128]{1,0:T(8,128)(2,1)S(1)}, bf16[256,128]{1,0:T(8,128)(2,1)S(1)}, u32[]{:S(2)}, u32[]{:S(2)}) collective-permute-start(bf16[256,128]{1,0:T(8,128)(2,1)S(1)} %get-tuple-element.46), channel_id=1, source_target_pairs={{2,5},{3,4},{4,3},{5,2},{6,9},{7,8},{8,7},{9,6},{10,13},{11,12},{1... | collective-permute-start | bytes 196616 | tf_op jit(solution)/shard_map/ppermute | solution.py:44
  35.2 4.4 %collective-permute-start.9 = (bf16[256,128]{1,0:T(8,128)(2,1)S(1)}, bf16[256,128]{1,0:T(8,128)(2,1)S(1)}, u32[]{:S(2)}, u32[]{:S(2)}) collective-permute-start(bf16[256,128]{1,0:T(8,128)(2,1)S(1)} %get-tuple-element.47), channel_id=1, source_target_pairs={{2,4},{3,5},{4,2},{5,3},{6,8},{7,9},{8,6},{9,7},{10,12},{11,13},{1... | collective-permute-start | bytes 196616 | tf_op jit(solution)/shard_map/ppermute | solution.py:44
  39.7 1.6 %collective-permute-start.11 = (bf16[256,128]{1,0:T(8,128)(2,1)S(1)}, bf16[256,128]{1,0:T(8,128)(2,1)S(1)}, u32[]{:S(2)}, u32[]{:S(2)}) collective-permute-start(bf16[256,128]{1,0:T(8,128)(2,1)S(1)} %get-tuple-element.49), channel_id=1, source_target_pairs={{0,2},{1,3},{2,0},{3,1},{4,6},{5,7},{6,4},{7,5},{8,10},{9,11},{10,... | collective-permute-start | bytes 196616 | tf_op jit(solution)/shard_map/ppermute | solution.py:44
  41.9 1.7 %receive.3 = (bf16[1280,2048]{1,0:T(8,128)(2,1)S(1)}, f32[1280,128]{1,0:T(8,128)S(1)}) custom-call(bf16[1280,128]{1,0:T(8,128)(2,1)S(1)} %get-tuple-element.43.extended_ref, bf16[1280,128]{1,0:T(8,128)(2,1)S(1)} %get-tuple-element.33.turned_ref, bf16[2,256,2048]{2,1,0:T(8,128)(2,1)S(1)} %get-tuple-element.34.first_ref, ...), custom_call_target="tpu_custom_call" | custom-call | flops 2500000000 | bytes 6000000 | tf_op jit(solution)/shard_map/receive/pallas_call | solution.py:314
  44.0 1.6 %collective-permute-done.12.refs_4_ = bf16[256,128]{1,0:T(8,128)(2,1)S(1)} collective-permute-done((bf16[256,128]{1,0:T(8,128)(2,1)S(1)}, bf16[256,128]{1,0:T(8,128)(2,1)S(1)}, u32[]{:S(2)}, u32[]{:S(2)}) %collective-permute-start.12) | collective-permute-done | bytes 65568 | tf_op jit(solution)/shard_map/ppermute | solution.py:44
  45.6 6.6 %layer.3 = bf16[1280,128]{1,0:T(8,128)(2,1)} custom-call(bf16[1280,128]{1,0:T(8,128)(2,1)S(1)} %get-tuple-element.43.extended_ref, bf16[1280,2048]{1,0:T(8,128)(2,1)S(1)} %get-tuple-element.44.base_ref, f32[1280,128]{1,0:T(8,128)S(1)} %get-tuple-element.45.own_ref, s32[16,80]{1,0:T(8,128)S(1)} %bitcast.9, bf16[2,3,128,128]{3,2,1,0:T(8,128)(2,1)S(1)} %copy-done.1, ...), custom_call_target="tpu_custom_call" | custom-call | tf_op jit(solution)/shard_map/layer/pallas_call | solution.py:328
  (32 shorter events, 1.9 us)
Async XLA Ops:
  2.3 22.4 %copy-start.1 = (bf16[2,3,128,128]{3,2,1,0:T(8,128)(2,1)S(1)}, bf16[2,3,128,128]{3,2,1,0:T(8,128)(2,1)}, u32[]{:S(2)}) copy-start(bf16[2,3,128,128]{3,2,1,0:T(8,128)(2,1)} %edge_ref.9) | copy-start | bytes 589828
  2.3 22.4 %copy-start.5 = (f32[2,4,128]{2,1,0:T(4,128)S(1)}, f32[2,4,128]{2,1,0:T(4,128)}, u32[]{:S(2)}) copy-start(f32[2,4,128]{2,1,0:T(4,128)} %bias_ref.7) | copy-start | bytes 12292
  2.3 7.4 %collective-permute-start = (bf16[64,128]{1,0:T(8,128)(2,1)}, bf16[64,128]{1,0:T(8,128)(2,1)S(1)}, u32[]{:S(2)}, u32[]{:S(2)}) collective-permute-start(bf16[64,128]{1,0:T(8,128)(2,1)} %get-tuple-element.29), channel_id=1, source_target_pairs={{2,4},{3,5},{4,2},{5,3},{6,8},{7,9},{8,6},{9,7},{10,12},{11,13},{1... | collective-permute-start | bytes 49160 | tf_op jit(solution)/shard_map/ppermute | solution.py:44
  5.2 4.5 %collective-permute-start.1 = (bf16[64,128]{1,0:T(8,128)(2,1)}, bf16[64,128]{1,0:T(8,128)(2,1)S(1)}, u32[]{:S(2)}, u32[]{:S(2)}) collective-permute-start(bf16[64,128]{1,0:T(8,128)(2,1)} %get-tuple-element.30), channel_id=1, source_target_pairs={{0,2},{1,3},{2,0},{3,1},{4,6},{5,7},{6,4},{7,5},{8,10},{9,11},{10,... | collective-permute-start | bytes 49160 | tf_op jit(solution)/shard_map/ppermute | solution.py:44
  6.1 3.9 %collective-permute-start.2 = (bf16[64,128]{1,0:T(8,128)(2,1)}, bf16[64,128]{1,0:T(8,128)(2,1)S(1)}, u32[]{:S(2)}, u32[]{:S(2)}) collective-permute-start(bf16[64,128]{1,0:T(8,128)(2,1)} %get-tuple-element.31), channel_id=1, source_target_pairs={{0,1},{1,0},{2,3},{3,2},{4,5},{5,4},{6,7},{7,6},{8,9},{9,8},{10,11... | collective-permute-start | bytes 49160 | tf_op jit(solution)/shard_map/ppermute | solution.py:44
  7.6 0.7 %copy-start.8 = (s32[1,1,8,256]{3,2,1,0:T(8,128)S(1)}, s32[1,1,8,256]{3,2,1,0:T(8,128)}, u32[]{:S(2)}) copy-start(s32[1,1,8,256]{3,2,1,0:T(8,128)} %param.15) | copy-start | bytes 24580
  8.3 0.7 %copy-start.10 = (s32[1,1,8]{2,1,0:T(1,128)S(1)}, s32[1,1,8]{2,1,0:T(1,128)}, u32[]{:S(2)}) copy-start(s32[1,1,8]{2,1,0:T(1,128)} %param.16) | copy-start | bytes 100
  10.0 1.0 %copy-start.3 = (bf16[1024,128]{1,0:T(8,128)(2,1)S(1)}, bf16[1024,128]{1,0:T(8,128)(2,1)}, u32[]{:S(2)}) copy-start(bf16[1024,128]{1,0:T(8,128)(2,1)} %get-tuple-element.28.retained_ref) | copy-start | bytes 786436
  12.0 14.3 %collective-permute-start.3 = (bf16[256,128]{1,0:T(8,128)(2,1)S(1)}, bf16[256,128]{1,0:T(8,128)(2,1)S(1)}, u32[]{:S(2)}, u32[]{:S(2)}) collective-permute-start(bf16[256,128]{1,0:T(8,128)(2,1)S(1)} %get-tuple-element.38), channel_id=1, source_target_pairs={{2,5},{3,4},{4,3},{5,2},{6,9},{7,8},{8,7},{9,6},{10,13},{11,12},{1... | collective-permute-start | bytes 196616 | tf_op jit(solution)/shard_map/ppermute | solution.py:44
  14.8 11.5 %collective-permute-start.4 = (bf16[256,128]{1,0:T(8,128)(2,1)S(1)}, bf16[256,128]{1,0:T(8,128)(2,1)S(1)}, u32[]{:S(2)}, u32[]{:S(2)}) collective-permute-start(bf16[256,128]{1,0:T(8,128)(2,1)S(1)} %get-tuple-element.39), channel_id=1, source_target_pairs={{2,4},{3,5},{4,2},{5,3},{6,8},{7,9},{8,6},{9,7},{10,12},{11,13},{1... | collective-permute-start | bytes 196616 | tf_op jit(solution)/shard_map/ppermute | solution.py:44
  19.4 6.9 %collective-permute-start.5 = (bf16[256,128]{1,0:T(8,128)(2,1)S(1)}, bf16[256,128]{1,0:T(8,128)(2,1)S(1)}, u32[]{:S(2)}, u32[]{:S(2)}) collective-permute-start(bf16[256,128]{1,0:T(8,128)(2,1)S(1)} %get-tuple-element.40), channel_id=1, source_target_pairs={{0,3},{1,2},{2,1},{3,0},{4,7},{5,6},{6,5},{7,4},{8,11},{9,10},{10,... | collective-permute-start | bytes 196616 | tf_op jit(solution)/shard_map/ppermute | solution.py:44
  19.5 6.9 %collective-permute-start.6 = (bf16[256,128]{1,0:T(8,128)(2,1)S(1)}, bf16[256,128]{1,0:T(8,128)(2,1)S(1)}, u32[]{:S(2)}, u32[]{:S(2)}) collective-permute-start(bf16[256,128]{1,0:T(8,128)(2,1)S(1)} %get-tuple-element.41), channel_id=1, source_target_pairs={{0,2},{1,3},{2,0},{3,1},{4,6},{5,7},{6,4},{7,5},{8,10},{9,11},{10,... | collective-permute-start | bytes 196616 | tf_op jit(solution)/shard_map/ppermute | solution.py:44
  20.1 6.2 %collective-permute-start.7 = (bf16[256,128]{1,0:T(8,128)(2,1)S(1)}, bf16[256,128]{1,0:T(8,128)(2,1)S(1)}, u32[]{:S(2)}, u32[]{:S(2)}) collective-permute-start(bf16[256,128]{1,0:T(8,128)(2,1)S(1)} %get-tuple-element.42), channel_id=1, source_target_pairs={{0,1},{1,0},{2,3},{3,2},{4,5},{5,4},{6,7},{7,6},{8,9},{9,8},{10,11... | collective-permute-start | bytes 196616 | tf_op jit(solution)/shard_map/ppermute | solution.py:44
  21.6 0.9 %copy-start = (bf16[2,3,128,128]{3,2,1,0:T(8,128)(2,1)S(1)}, bf16[2,3,128,128]{3,2,1,0:T(8,128)(2,1)}, u32[]{:S(2)}) copy-start(bf16[2,3,128,128]{3,2,1,0:T(8,128)(2,1)} %edge_ref.9) | copy-start | bytes 589828
  22.6 1.0 %copy-start.7 = (f32[1,1,4,16,1280]{4,3,2,1,0:T(8,128)S(1)}, f32[1,1,4,16,1280]{4,3,2,1,0:T(8,128)}, u32[]{:S(2)}) copy-start(f32[1,1,4,16,1280]{4,3,2,1,0:T(8,128)} %param.18) | copy-start | bytes 983044
  23.5 0.7 %copy-start.9 = (f32[2,4,128]{2,1,0:T(4,128)S(1)}, f32[2,4,128]{2,1,0:T(4,128)}, u32[]{:S(2)}) copy-start(f32[2,4,128]{2,1,0:T(4,128)} %geo_ref.1) | copy-start | bytes 12292
  24.6 1.7 %copy-start.2 = (bf16[2,3,128,128]{3,2,1,0:T(8,128)(2,1)S(1)}, bf16[2,3,128,128]{3,2,1,0:T(8,128)(2,1)}, u32[]{:S(2)}) copy-start(bf16[2,3,128,128]{3,2,1,0:T(8,128)(2,1)} %node_ref.3) | copy-start | bytes 589828
  24.7 1.7 %copy-start.4 = (s32[1,1,16,80]{3,2,1,0:T(8,128)S(1)}, s32[1,1,16,80]{3,2,1,0:T(8,128)}, u32[]{:S(2)}) copy-start(s32[1,1,16,80]{3,2,1,0:T(8,128)} %param.17) | copy-start | bytes 15364
  24.7 1.7 %copy-start.6 = (f32[2,2,128]{2,1,0:T(2,128)S(1)}, f32[2,2,128]{2,1,0:T(2,128)}, u32[]{:S(2)}) copy-start(f32[2,2,128]{2,1,0:T(2,128)} %gain_ref.3) | copy-start | bytes 6148
  33.0 10.6 %collective-permute-start.8 = (bf16[256,128]{1,0:T(8,128)(2,1)S(1)}, bf16[256,128]{1,0:T(8,128)(2,1)S(1)}, u32[]{:S(2)}, u32[]{:S(2)}) collective-permute-start(bf16[256,128]{1,0:T(8,128)(2,1)S(1)} %get-tuple-element.46), channel_id=1, source_target_pairs={{2,5},{3,4},{4,3},{5,2},{6,9},{7,8},{8,7},{9,6},{10,13},{11,12},{1... | collective-permute-start | bytes 196616 | tf_op jit(solution)/shard_map/ppermute | solution.py:44
  35.2 8.4 %collective-permute-start.9 = (bf16[256,128]{1,0:T(8,128)(2,1)S(1)}, bf16[256,128]{1,0:T(8,128)(2,1)S(1)}, u32[]{:S(2)}, u32[]{:S(2)}) collective-permute-start(bf16[256,128]{1,0:T(8,128)(2,1)S(1)} %get-tuple-element.47), channel_id=1, source_target_pairs={{2,4},{3,5},{4,2},{5,3},{6,8},{7,9},{8,6},{9,7},{10,12},{11,13},{1... | collective-permute-start | bytes 196616 | tf_op jit(solution)/shard_map/ppermute | solution.py:44
  39.7 4.4 %collective-permute-start.10 = (bf16[256,128]{1,0:T(8,128)(2,1)S(1)}, bf16[256,128]{1,0:T(8,128)(2,1)S(1)}, u32[]{:S(2)}, u32[]{:S(2)}) collective-permute-start(bf16[256,128]{1,0:T(8,128)(2,1)S(1)} %get-tuple-element.48), channel_id=1, source_target_pairs={{0,3},{1,2},{2,1},{3,0},{4,7},{5,6},{6,5},{7,4},{8,11},{9,10},{10,... | collective-permute-start | bytes 196616 | tf_op jit(solution)/shard_map/ppermute | solution.py:44
  39.7 4.3 %collective-permute-start.11 = (bf16[256,128]{1,0:T(8,128)(2,1)S(1)}, bf16[256,128]{1,0:T(8,128)(2,1)S(1)}, u32[]{:S(2)}, u32[]{:S(2)}) collective-permute-start(bf16[256,128]{1,0:T(8,128)(2,1)S(1)} %get-tuple-element.49), channel_id=1, source_target_pairs={{0,2},{1,3},{2,0},{3,1},{4,6},{5,7},{6,4},{7,5},{8,10},{9,11},{10,... | collective-permute-start | bytes 196616 | tf_op jit(solution)/shard_map/ppermute | solution.py:44
  41.3 4.3 %collective-permute-start.12 = (bf16[256,128]{1,0:T(8,128)(2,1)S(1)}, bf16[256,128]{1,0:T(8,128)(2,1)S(1)}, u32[]{:S(2)}, u32[]{:S(2)}) collective-permute-start(bf16[256,128]{1,0:T(8,128)(2,1)S(1)} %get-tuple-element.50), channel_id=1, source_target_pairs={{0,1},{1,0},{2,3},{3,2},{4,5},{5,4},{6,7},{7,6},{8,9},{9,8},{10,11... | collective-permute-start | bytes 196616 | tf_op jit(solution)/shard_map/ppermute | solution.py:44

commit v3 on v2

--- a/solution.py
+++ b/solution.py
@@ -31,6 +31,25 @@
 def links(count_x, count_y):
     both = itertools.product(kinds(count_x)[::-1] + [None], kinds(count_y)[::-1] + [None])
     return [pair for pair in both if pair != (None, None)]
+
+
+def messages(all_links):
+    along_y = [link for link in all_links if link[0] is None]
+    groups = [[(1, None)] + [(1, kind) for _, kind in along_y]] if (1, None) in all_links else []
+    groups += [[link, (0, link[1])] for link in along_y]
+    return groups + [[(0, None)]]
+
+
+def exchange(sends, all_links, ghosts):
+    landed = {}
+    for group, send in zip(messages(all_links), sends):
+        arrived = swap(send, group[0])
+        for place, link in enumerate(group):
+            landed[link] = arrived if place == 0 else arrived[place * ghosts : (place + 1) * ghosts]
+    for link in all_links:
+        if None not in link:
+            landed[link] = swap(landed[link], (None, link[1]) if link[0] == 1 else (0, None))
+    return [landed[link] for link in all_links]
 
 
 def swap(value, link):
@@ -78,41 +97,45 @@
 
 
 def pack_kernel(sides, latents_hbm, rows_hbm, count_hbm, retained_ref, *refs):
-    packet_refs, (latents_ref, rows_ref, count_ref, sems) = refs[: len(sides)], refs[len(sides) :]
+    packet_refs, (chosen_ref, latents_ref, rows_ref, count_ref, sems) = refs[: len(sides)], refs[len(sides) :]
     fetch((latents_hbm, rows_hbm, count_hbm), (latents_ref, rows_ref, count_ref), sems)
     total = latents_ref.shape[0]
     slots = rows_ref.shape[1]
     owned = latents_ref[...]
-    row_id = lax.broadcasted_iota(jnp.int32, (total, slots), 0)
+    directions = rows_ref.shape[0]
     lane = lax.broadcasted_iota(jnp.int32, (1, slots), 1)
-
-    def picker(direction):
-        wanted = rows_ref[pl.ds(direction, 1), :]
-        wanted = jnp.where(lane < count_ref[direction], wanted, -1)
-        return (row_id == wanted).astype(F32)
-
-    marks = picker(0)
-    for direction in range(1, 4):
-        marks = marks + picker(direction)
-    marks = jnp.dot(marks.astype(BF16), jnp.ones((slots, owned.shape[1]), BF16), preferred_element_type=F32)
+    wanted = jnp.concatenate(
+        [jnp.where(lane < count_ref[side_at], rows_ref[pl.ds(side_at, 1), :], -1) for side_at in range(directions)], axis=1
+    )
+    row_id = lax.broadcasted_iota(jnp.int32, (total, directions * slots), 0)
+    picker = (row_id == wanted).astype(F32).astype(BF16)
+    chosen = lax.dot_general(picker, owned, (((0,), (0,)), ((), ())), preferred_element_type=F32)
+    chosen_ref[...] = chosen.astype(BF16)
+    for link, packet_ref in zip(sides, packet_refs):
+        packet_ref[...] = chosen_ref[pl.ds(pl.multiple_of(side(link) * slots, 16), slots), :]
+    marks = jnp.dot(picker, jnp.ones((directions * slots, owned.shape[1]), BF16), preferred_element_type=F32)
     retained_ref[...] = jnp.where(marks > 0.0, 0.0, owned.astype(F32)).astype(BF16)
-    for link, packet_ref in zip(sides, packet_refs):
-        chosen = lax.dot_general(
-            picker(side(link)).astype(BF16), owned, (((0,), (0,)), ((), ())), preferred_element_type=F32
-        )
-        packet_ref[...] = chosen.astype(BF16)
 
 
 def gather_ghosts(extended_ref, wanted_ref, send_refs):
     total = extended_ref.shape[0]
+    ghosts = wanted_ref.shape[1]
+    spots = [(ref, start) for ref in send_refs for start in range(0, ref.shape[0], ghosts)]
     column = lax.broadcasted_iota(jnp.int32, wanted_ref.shape[1:], 1).astype(F32)
-    for place, send_ref in enumerate(send_refs):
+    parts = 2 if total % 256 == 0 else 1
+    part = total // parts
+    source = jnp.concatenate([extended_ref[pl.ds(start, part), :] for start in range(0, total, part)], axis=1)
+    for place, (send_ref, start_row) in enumerate(spots):
         wanted = wanted_ref[place]
+        upper = wanted >= float(part)
+        within = jnp.where(upper, wanted - float(part), wanted) if parts > 1 else wanted
         picker = jnp.concatenate(
-            [jnp.where(wanted == column + float(start), 1.0, 0.0).astype(BF16) for start in range(0, total, 128)],
-            axis=1,
+            [jnp.where(within == column + float(start), 1.0, 0.0).astype(BF16) for start in range(0, part, 128)], axis=1
         )
-        send_ref[...] = jnp.dot(picker, extended_ref[...], preferred_element_type=F32).astype(BF16)
+        chosen = jnp.dot(picker, source, preferred_element_type=F32)
+        if parts > 1:
+            chosen = jnp.where(upper, chosen[:, column.shape[1] :], chosen[:, : column.shape[1]])
+        send_ref[pl.ds(start_row, ghosts), :] = chosen.astype(BF16)
 
 
 def build_kernel(sides, retained_ref, *refs):
@@ -129,10 +152,10 @@
     gather_ghosts(extended_ref, wanted_ref, send_refs)
 
 
-def want_kernel(all_links, rows_ref, count_ref, wanted_ref):
+def want_kernel(order, rows_ref, count_ref, wanted_ref):
     ghosts = rows_ref.shape[1]
     lane = lax.broadcasted_iota(jnp.int32, (1, ghosts), 1)
-    for place, link in enumerate(all_links):
+    for place, link in enumerate(order):
         target = section(step("gx", link[0]), step("gy", link[1]))
         wanted = rows_ref[pl.ds(target, 1), :]
         wanted = jnp.where(lane < count_ref[target], wanted, -1).astype(F32)
@@ -182,7 +205,7 @@
 
 
 def layer_kernel(
-    layer, last, all_links, extended_ref, base_ref, own_ref, links_ref, edge_ref, node_ref, second_ref, bias_ref, gain_ref, *refs
+    layer, last, ghosts, all_links, extended_ref, base_ref, own_ref, links_ref, edge_ref, node_ref, second_ref, bias_ref, gain_ref, *refs
 ):
     landed, refs = refs[: len(all_links)], refs[len(all_links) :]
     if not last:
@@ -191,7 +214,6 @@
     rows_total, width = extended_ref.shape
     slots, tiles = links_ref.shape
     rows = rows_total // tiles
-    ghosts = landed[0].shape[0]
 
     sender_mat = edge_ref[layer, 1]
     table_ref[pl.ds(0, rows_total), :] = own_ref[...]
@@ -200,9 +222,24 @@
     for link, landed_ref in zip(all_links, landed):
         source = section(-step("gx", link[0]), -step("gy", link[1]))
         start = pl.multiple_of(rows_total + ghosts * source, 16)
-        table_ref[pl.ds(start, ghosts), :] = jnp.dot(landed_ref[...], sender_mat, preferred_element_type=F32)
+        table_ref[pl.ds(start, ghosts), :] = jnp.dot(landed_ref[pl.ds(0, ghosts), :], sender_mat, preferred_element_type=F32)
     bias_second = bias_ref[layer, pl.ds(1, 1), :]
     bias_second = bias_second - jnp.mean(bias_second, axis=-1, keepdims=True)
+
+    gain_first = gain_ref[layer, pl.ds(0, 1), :] * math.sqrt(width)
+    node_mat = jnp.concatenate([node_ref[layer, 0], node_ref[layer, 1]], axis=0)
+
+    def update(start, total):
+        extended = extended_ref[pl.ds(start, total.shape[0]), :]
+        gathered = (total * gain_first).astype(BF16)
+        node_first = jnp.dot(jnp.concatenate([extended, gathered], axis=1), node_mat, preferred_element_type=F32)
+        node_hidden = jnp.maximum(node_first + bias_ref[layer, pl.ds(2, 1), :], 0.0).astype(BF16)
+        node_out = jnp.dot(node_hidden, node_ref[layer, 2], preferred_element_type=F32)
+        node_out = node_out + bias_ref[layer, pl.ds(3, 1), :]
+        center = node_out - jnp.mean(node_out, axis=-1, keepdims=True)
+        scale = lax.rsqrt(spread_of(center) / width + 1e-5)
+        updated = extended.astype(F32) + center * scale * gain_ref[layer, pl.ds(1, 1), :]
+        updated_ref[pl.ds(start, total.shape[0]), :] = updated.astype(BF16)
 
     chunk_rows = math.gcd(rows_total, CHUNK)
     chunk_tiles = chunk_rows // rows
@@ -214,11 +251,10 @@
                 senders = []
                 for tile in range(start // rows, start // rows + chunk_tiles):
                     picked = table_ref[pl.ds(jnp.maximum(links_ref[slot, tile], 0), 1), :]
-                    senders.append(jnp.broadcast_to(picked, (rows, width)))
+                    senders.append(jnp.broadcast_to(picked, (rows, width)).astype(BF16))
                 halves.append(jnp.concatenate(senders, axis=0))
-            base = base_ref[pl.ds(start, chunk_rows), pl.ds(pair * width, 2 * width)].astype(F32)
-            hidden = jnp.maximum(base + jnp.concatenate(halves, axis=1), 0.0)
-            hidden_ref[pl.ds(start, chunk_rows), :] = hidden.astype(BF16)
+            base = base_ref[pl.ds(start, chunk_rows), pl.ds(pair * width, 2 * width)]
+            hidden_ref[pl.ds(start, chunk_rows), :] = jnp.maximum(base + jnp.concatenate(halves, axis=1), 0)
         for start in chunks:
             second = jnp.dot(hidden_ref[pl.ds(start, chunk_rows), :], second_ref[layer], preferred_element_type=F32)
             for place in range(0, chunk_rows, rows):
@@ -229,19 +265,8 @@
                     limit = jnp.where(links_ref[pair + half, tile] >= 0, width * 1e-5, jnp.inf)
                     total = total + center * lax.rsqrt(spread_of(center) + limit)
                 total_ref[pl.ds(start + place, rows), :] = total
-
-    gathered = (total_ref[...] * (gain_ref[layer, pl.ds(0, 1), :] * math.sqrt(width))).astype(BF16)
-    extended = extended_ref[...]
-    node_first = jnp.dot(
-        jnp.concatenate([extended, gathered], axis=1),
-        jnp.concatenate([node_ref[layer, 0], node_ref[layer, 1]], axis=0),
-        preferred_element_type=F32,
-    )
-    node_hidden = jnp.maximum(node_first + bias_ref[layer, pl.ds(2, 1), :], 0.0).astype(BF16)
-    node_out = jnp.dot(node_hidden, node_ref[layer, 2], preferred_element_type=F32) + bias_ref[layer, pl.ds(3, 1), :]
-    center = node_out - jnp.mean(node_out, axis=-1, keepdims=True)
-    scale = lax.rsqrt(spread_of(center) / width + 1e-5)
-    updated_ref[...] = (extended.astype(F32) + center * scale * gain_ref[layer, pl.ds(1, 1), :]).astype(BF16)
+    for start in range(0, rows_total, 256):
+        update(start, total_ref[pl.ds(start, 256), :])
     if not last:
         gather_ghosts(updated_ref, wanted_ref, send_refs)
 
@@ -260,6 +285,7 @@
     table_rows = rows_total + 8 * ghosts
     all_links = links(lax.axis_size("gx"), lax.axis_size("gy"))
     sides = [link for link in all_links if None in link]
+    groups = messages(all_links)
     rows_of = lambda count: jax.ShapeDtypeStruct((count, width), BF16)
 
     retained, *packets = pl.pallas_call(
@@ -267,7 +293,7 @@
         out_shape=[rows_of(owned.shape[0])] + [rows_of(leave_rows.shape[1])] * len(sides),
         in_specs=[HBM] * 3,
         out_specs=[VMEM] * (1 + len(sides)),
-        scratch_shapes=fetched(owned, leave_rows, leave_count, smem=(2,)),
+        scratch_shapes=[pltpu.VMEM((leave_rows.size, width), BF16)] + fetched(owned, leave_rows, leave_count, smem=(2,)),
         compiler_params=WHOLE,
         name="pack",
     )(owned, leave_rows, leave_count)
@@ -277,7 +303,7 @@
     layers = edge_w.shape[0]
     deep = 2 * feats.shape[0] + width
     wanted = pl.pallas_call(
-        functools.partial(want_kernel, all_links),
+        functools.partial(want_kernel, sum(groups, [])),
         out_shape=jax.ShapeDtypeStruct((len(all_links), ghosts, 128), F32),
         in_specs=[VMEM, SMEM],
         out_specs=VMEM,
@@ -287,9 +313,9 @@
     )(ghost_list, ghost_total)
     extended, *sends = pl.pallas_call(
         functools.partial(build_kernel, sides),
-        out_shape=[rows_of(rows_total)] + [rows_of(ghosts)] * len(all_links),
+        out_shape=[rows_of(rows_total)] + [rows_of(ghosts * len(group)) for group in groups],
         in_specs=[VMEM] * (2 + len(sides)),
-        out_specs=[VMEM] * (1 + len(all_links)),
+        out_specs=[VMEM] * (1 + len(groups)),
         compiler_params=PARAMS,
         name="build",
     )(retained, *arrivals, wanted)
@@ -310,7 +336,7 @@
 
     for layer in range(layers):
         last = layer == layers - 1
-        landed = [swap(send, link) for send, link in zip(sends, all_links)]
+        landed = exchange(sends, all_links, ghosts)
         base, own = pl.pallas_call(
             functools.partial(receive_kernel, layer),
             out_shape=[
@@ -323,10 +349,10 @@
             cost_estimate=pl.CostEstimate(flops=2_500_000_000, bytes_accessed=6_000_000, transcendentals=0),
             name="receive",
         )(extended, turned, first_mats, edge_w, biases)
-        outs = [rows_of(rows_total)] + ([] if last else [rows_of(ghosts)] * len(all_links))
+        outs = [rows_of(rows_total)] + ([] if last else [rows_of(ghosts * len(group)) for group in groups])
         extra = [] if last else [wanted]
         extended, *sends = pl.pallas_call(
-            functools.partial(layer_kernel, layer, last, all_links),
+            functools.partial(layer_kernel, layer, last, ghosts, all_links),
             out_shape=outs,
             in_specs=[VMEM] * 3 + [SMEM] + [VMEM] * (5 + len(all_links) + len(extra)),
             out_specs=[VMEM] * len(outs),

time: 52.6 us -> 49.1 us (0.933)
  starting transfers between devices: 23.6 us -> 17.6 us
  waiting for transfers between devices: 2.3 us -> 5.63 us
  Pallas kernels: 21.1 us -> 20.2 us
    ppermute x13, starting transfers between devices: 23.6 us -> 17.6 us  [swap(): return lax.ppermute(value, ('gx', 'gy'), pairs)]
    ppermute x13, waiting for transfers between devices: 2.3 us -> 5.63 us  [swap(): return lax.ppermute(value, ('gx', 'gy'), pairs)]
  transfers between devices with their start and end apart: 13 -> 13, of which waited for: 3 -> 4; matrix products, arithmetic and copies ran while one was open for 0% -> 0% of each run, Pallas kernels for 9% -> 9%
where the time goes in v3:
time: 49.1 us; the launch traced here: 48.6 us
  Pallas kernels  20.2 us (41%)
  starting transfers between devices  17.6 us (36%)
  waiting for transfers between devices  5.63 us (11%)
  local copies, waits for them, and re-layouts  4.94 us (10%)
    ppermute x13, starting transfers between devices, swap(): return lax.ppermute(value, ('gx', 'gy'), pairs)  17.6 us
    pallas_call x2, Pallas kernels, body(): pl.pallas_call(functools.partial(layer_kernel, layer, last, ghosts, all_l...  12.7 us
    ppermute x13, waiting for transfers between devices, swap(): return lax.ppermute(value, ('gx', 'gy'), pairs)  5.63 us
    unnamed x22, local copies, waits for them, and re-layouts  4.92 us
    pallas_call x2, Pallas kernels, body(): pl.pallas_call(functools.partial(receive_kernel, layer), out_shape=[jax.S...  3.25 us
    pallas_call x1, Pallas kernels, body(): pl.pallas_call(functools.partial(pack_kernel, sides), out_shape=[rows_of(...  2.32 us
  transfers between devices with their start and end apart: 13, of which 4 were waited for; matrix products, arithmetic and copies ran while one was open for 0% of the time, Pallas kernels for 9%

profile of v3, /device:TPU:8, one launch (start us, length us, event | category | flops | bytes accessed | tf_op | source)
XLA Modules:
  0.0 48.6 jit_solution(9042968351387880955)
XLA Ops:
  0.0 2.3 %pack.1 = (bf16[1024,128]{1,0:T(8,128)(2,1)}, bf16[64,128]{1,0:T(8,128)(2,1)}, bf16[64,128]{1,0:T(8,128)(2,1)}, bf16[64,128]{1,0:T(8,128)(2,1)}) custom-call(bf16[1024,128]{1,0:T(8,128)(2,1)} %bitcast.13, s32[4,64]{1,0:T(4,128)} %bitcast.14, s32[4]{0:T(128)} %bitcast.15), custom_call_target="tpu_custom_call" | custom-call | tf_op jit(solution)/shard_map/pack/pallas_call | solution.py:291
  2.4 2.9 %collective-permute-start = (bf16[64,128]{1,0:T(8,128)(2,1)}, bf16[64,128]{1,0:T(8,128)(2,1)S(1)}, u32[]{:S(2)}, u32[]{:S(2)}) collective-permute-start(bf16[64,128]{1,0:T(8,128)(2,1)} %get-tuple-element.25), channel_id=1, source_target_pairs={{2,4},{3,5},{4,2},{5,3},{6,8},{7,9},{8,6},{9,7},{10,12},{11,13},{1... | collective-permute-start | bytes 49160 | tf_op jit(solution)/shard_map/ppermute | solution.py:63
  5.2 0.9 %collective-permute-start.1 = (bf16[64,128]{1,0:T(8,128)(2,1)}, bf16[64,128]{1,0:T(8,128)(2,1)S(1)}, u32[]{:S(2)}, u32[]{:S(2)}) collective-permute-start(bf16[64,128]{1,0:T(8,128)(2,1)} %get-tuple-element.26), channel_id=1, source_target_pairs={{0,2},{1,3},{2,0},{3,1},{4,6},{5,7},{6,4},{7,5},{8,10},{9,11},{10,... | collective-permute-start | bytes 49160 | tf_op jit(solution)/shard_map/ppermute | solution.py:63
  6.1 1.5 %collective-permute-start.2 = (bf16[64,128]{1,0:T(8,128)(2,1)}, bf16[64,128]{1,0:T(8,128)(2,1)S(1)}, u32[]{:S(2)}, u32[]{:S(2)}) collective-permute-start(bf16[64,128]{1,0:T(8,128)(2,1)} %get-tuple-element.27), channel_id=1, source_target_pairs={{0,1},{1,0},{2,3},{3,2},{4,5},{5,4},{6,7},{7,6},{8,9},{9,8},{10,11... | collective-permute-start | bytes 49160 | tf_op jit(solution)/shard_map/ppermute | solution.py:63
  8.9 0.8 %want.1.refs_3_.refs_5_ = f32[5,256,128]{2,1,0:T(8,128)S(1)} custom-call(s32[8,256]{1,0:T(8,128)S(1)} %bitcast.11, s32[8]{0:T(128)S(1)} %bitcast.12), custom_call_target="tpu_custom_call" | custom-call | flops 500000000 | bytes 1000000 | tf_op jit(solution)/shard_map/want/pallas_call | solution.py:305
  10.1 0.9 %copy-done.3 = bf16[1024,128]{1,0:T(8,128)(2,1)S(1)} copy-done((bf16[1024,128]{1,0:T(8,128)(2,1)S(1)}, bf16[1024,128]{1,0:T(8,128)(2,1)}, u32[]{:S(2)}) %copy-start.3) | copy-done | bytes 262168
  11.0 0.7 %build.1 = (bf16[1280,128]{1,0:T(8,128)(2,1)S(1)}, bf16[512,128]{1,0:T(8,128)(2,1)S(1)}, bf16[512,128]{1,0:T(8,128)(2,1)S(1)}, bf16[256,128]{1,0:T(8,128)(2,1)S(1)}) custom-call(bf16[1024,128]{1,0:T(8,128)(2,1)S(1)} %copy-done.3, bf16[64,128]{1,0:T(8,128)(2,1)S(1)} %collective-permute-done.refs_0_, bf16[64,128]{1,0:T(8,128)(2,1)S(1)} %collective-permute-done.1.refs_1_, ...), custom_call_target="tpu_custom_call" | custom-call | tf_op jit(solution)/shard_map/build/pallas_call | solution.py:314
  11.7 2.4 %collective-permute-start.3 = (bf16[512,128]{1,0:T(8,128)(2,1)S(1)}, bf16[512,128]{1,0:T(8,128)(2,1)S(1)}, u32[]{:S(2)}, u32[]{:S(2)}) collective-permute-start(bf16[512,128]{1,0:T(8,128)(2,1)S(1)} %get-tuple-element.34), channel_id=1, source_target_pairs={{2,4},{3,5},{4,2},{5,3},{6,8},{7,9},{8,6},{9,7},{10,12},{11,13},{1... | collective-permute-start | bytes 393224 | tf_op jit(solution)/shard_map/ppermute | solution.py:63
  14.2 1.0 %collective-permute-start.5 = (bf16[512,128]{1,0:T(8,128)(2,1)S(1)}, bf16[512,128]{1,0:T(8,128)(2,1)S(1)}, u32[]{:S(2)}, u32[]{:S(2)}) collective-permute-start(bf16[512,128]{1,0:T(8,128)(2,1)S(1)} %get-tuple-element.35), channel_id=1, source_target_pairs={{0,1},{1,0},{2,3},{3,2},{4,5},{5,4},{6,7},{7,6},{8,9},{9,8},{10,11... | collective-permute-start | bytes 393224 | tf_op jit(solution)/shard_map/ppermute | solution.py:63
  15.2 1.3 %collective-permute-start.7 = (bf16[256,128]{1,0:T(8,128)(2,1)S(1)}, bf16[256,128]{1,0:T(8,128)(2,1)S(1)}, u32[]{:S(2)}, u32[]{:S(2)}) collective-permute-start(bf16[256,128]{1,0:T(8,128)(2,1)S(1)} %get-tuple-element.36), channel_id=1, source_target_pairs={{0,2},{1,3},{2,0},{3,1},{4,6},{5,7},{6,4},{7,5},{8,10},{9,11},{10,... | collective-permute-start | bytes 196616 | tf_op jit(solution)/shard_map/ppermute | solution.py:63
  16.6 0.9 %copy-done = bf16[2,3,128,128]{3,2,1,0:T(8,128)(2,1)S(1)} copy-done((bf16[2,3,128,128]{3,2,1,0:T(8,128)(2,1)S(1)}, bf16[2,3,128,128]{3,2,1,0:T(8,128)(2,1)}, u32[]{:S(2)}) %copy-start) | copy-done | bytes 196632
  17.5 1.0 %copy-done.7 = f32[1,1,4,16,1280]{4,3,2,1,0:T(8,128)S(1)} copy-done((f32[1,1,4,16,1280]{4,3,2,1,0:T(8,128)S(1)}, f32[1,1,4,16,1280]{4,3,2,1,0:T(8,128)}, u32[]{:S(2)}) %copy-start.7) | copy-done | bytes 327704
  19.6 0.9 %collective-permute-start.4 = (bf16[256,128]{1,0:T(8,128)(2,1)S(1)}, bf16[256,128]{1,0:T(8,128)(2,1)S(1)}, u32[]{:S(2)}, u32[]{:S(2)}) collective-permute-start(bf16[256,128]{1,0:T(8,128)(2,1)S(1)} %slice.16), channel_id=1, source_target_pairs={{0,1},{1,0},{2,3},{3,2},{4,5},{5,4},{6,7},{7,6},{8,9},{9,8},{10,11... | collective-permute-start | bytes 196616 | tf_op jit(solution)/shard_map/ppermute | solution.py:63
  20.9 1.6 %receive.2 = (bf16[1280,2048]{1,0:T(8,128)(2,1)S(1)}, f32[1280,128]{1,0:T(8,128)S(1)}) custom-call(bf16[1280,128]{1,0:T(8,128)(2,1)S(1)} %get-tuple-element.28.extended_ref, bf16[1280,128]{1,0:T(8,128)(2,1)S(1)} %get-tuple-element.29.turned_ref, bf16[2,256,2048]{2,1,0:T(8,128)(2,1)S(1)} %get-tuple-element.30.first_ref, ...), custom_call_target="tpu_custom_call" | custom-call | flops 2500000000 | bytes 6000000 | tf_op jit(solution)/shard_map/receive/pallas_call | solution.py:340
  22.6 1.4 %collective-permute-done.4.refs_0_ = bf16[256,128]{1,0:T(8,128)(2,1)S(1)} collective-permute-done((bf16[256,128]{1,0:T(8,128)(2,1)S(1)}, bf16[256,128]{1,0:T(8,128)(2,1)S(1)}, u32[]{:S(2)}, u32[]{:S(2)}) %collective-permute-start.4) | collective-permute-done | bytes 65568 | tf_op jit(solution)/shard_map/ppermute | solution.py:63
  24.0 6.2 %layer.2 = (bf16[1280,128]{1,0:T(8,128)(2,1)S(1)}, bf16[512,128]{1,0:T(8,128)(2,1)S(1)}, bf16[512,128]{1,0:T(8,128)(2,1)S(1)}, bf16[256,128]{1,0:T(8,128)(2,1)S(1)}) custom-call(bf16[1280,128]{1,0:T(8,128)(2,1)S(1)} %get-tuple-element.28.extended_ref, bf16[1280,2048]{1,0:T(8,128)(2,1)S(1)} %get-tuple-element.31.base_ref, ...), custom_call_target="tpu_custom_call" | custom-call | tf_op jit(solution)/shard_map/layer/pallas_call | solution.py:354
  30.3 2.3 %collective-permute-start.8 = (bf16[512,128]{1,0:T(8,128)(2,1)S(1)}, bf16[512,128]{1,0:T(8,128)(2,1)S(1)}, u32[]{:S(2)}, u32[]{:S(2)}) collective-permute-start(bf16[512,128]{1,0:T(8,128)(2,1)S(1)} %get-tuple-element.40), channel_id=1, source_target_pairs={{2,4},{3,5},{4,2},{5,3},{6,8},{7,9},{8,6},{9,7},{10,12},{11,13},{1... | collective-permute-start | bytes 393224 | tf_op jit(solution)/shard_map/ppermute | solution.py:63
  32.6 1.0 %collective-permute-start.10 = (bf16[512,128]{1,0:T(8,128)(2,1)S(1)}, bf16[512,128]{1,0:T(8,128)(2,1)S(1)}, u32[]{:S(2)}, u32[]{:S(2)}) collective-permute-start(bf16[512,128]{1,0:T(8,128)(2,1)S(1)} %get-tuple-element.41), channel_id=1, source_target_pairs={{0,1},{1,0},{2,3},{3,2},{4,5},{5,4},{6,7},{7,6},{8,9},{9,8},{10,11... | collective-permute-start | bytes 393224 | tf_op jit(solution)/shard_map/ppermute | solution.py:63
  33.6 1.4 %collective-permute-start.12 = (bf16[256,128]{1,0:T(8,128)(2,1)S(1)}, bf16[256,128]{1,0:T(8,128)(2,1)S(1)}, u32[]{:S(2)}, u32[]{:S(2)}) collective-permute-start(bf16[256,128]{1,0:T(8,128)(2,1)S(1)} %get-tuple-element.42), channel_id=1, source_target_pairs={{0,2},{1,3},{2,0},{3,1},{4,6},{5,7},{6,4},{7,5},{8,10},{9,11},{10,... | collective-permute-start | bytes 196616 | tf_op jit(solution)/shard_map/ppermute | solution.py:63
  35.0 2.5 %collective-permute-done.8.refs_1_ = bf16[512,128]{1,0:T(8,128)(2,1)S(1)} collective-permute-done((bf16[512,128]{1,0:T(8,128)(2,1)S(1)}, bf16[512,128]{1,0:T(8,128)(2,1)S(1)}, u32[]{:S(2)}, u32[]{:S(2)}) %collective-permute-start.8) | collective-permute-done | bytes 131104 | tf_op jit(solution)/shard_map/ppermute | solution.py:63
  37.6 1.1 %collective-permute-start.9 = (bf16[256,128]{1,0:T(8,128)(2,1)S(1)}, bf16[256,128]{1,0:T(8,128)(2,1)S(1)}, u32[]{:S(2)}, u32[]{:S(2)}) collective-permute-start(bf16[256,128]{1,0:T(8,128)(2,1)S(1)} %slice.18), channel_id=1, source_target_pairs={{0,1},{1,0},{2,3},{3,2},{4,5},{5,4},{6,7},{7,6},{8,9},{9,8},{10,11... | collective-permute-start | bytes 196616 | tf_op jit(solution)/shard_map/ppermute | solution.py:63
  39.2 1.6 %receive.3 = (bf16[1280,2048]{1,0:T(8,128)(2,1)S(1)}, f32[1280,128]{1,0:T(8,128)S(1)}) custom-call(bf16[1280,128]{1,0:T(8,128)(2,1)S(1)} %get-tuple-element.37.extended_ref, bf16[1280,128]{1,0:T(8,128)(2,1)S(1)} %get-tuple-element.29.turned_ref, bf16[2,256,2048]{2,1,0:T(8,128)(2,1)S(1)} %get-tuple-element.30.first_ref, ...), custom_call_target="tpu_custom_call" | custom-call | flops 2500000000 | bytes 6000000 | tf_op jit(solution)/shard_map/receive/pallas_call | solution.py:340
  40.8 1.4 %collective-permute-done.9.refs_0_ = bf16[256,128]{1,0:T(8,128)(2,1)S(1)} collective-permute-done((bf16[256,128]{1,0:T(8,128)(2,1)S(1)}, bf16[256,128]{1,0:T(8,128)(2,1)S(1)}, u32[]{:S(2)}, u32[]{:S(2)}) %collective-permute-start.9) | collective-permute-done | bytes 65568 | tf_op jit(solution)/shard_map/ppermute | solution.py:63
  42.2 6.5 %layer.3 = bf16[1280,128]{1,0:T(8,128)(2,1)} custom-call(bf16[1280,128]{1,0:T(8,128)(2,1)S(1)} %get-tuple-element.37.extended_ref, bf16[1280,2048]{1,0:T(8,128)(2,1)S(1)} %get-tuple-element.38.base_ref, f32[1280,128]{1,0:T(8,128)S(1)} %get-tuple-element.39.own_ref, s32[16,80]{1,0:T(8,128)S(1)} %bitcast.9, bf16[2,3,128,128]{3,2,1,0:T(8,128)(2,1)S(1)} %copy-done.1, ...), custom_call_target="tpu_custom_call" | custom-call | tf_op jit(solution)/shard_map/layer/pallas_call | solution.py:354
  (36 shorter events, 3.7 us)
Async XLA Ops:
  2.3 18.6 %copy-start.1 = (bf16[2,3,128,128]{3,2,1,0:T(8,128)(2,1)S(1)}, bf16[2,3,128,128]{3,2,1,0:T(8,128)(2,1)}, u32[]{:S(2)}) copy-start(bf16[2,3,128,128]{3,2,1,0:T(8,128)(2,1)} %edge_ref.9) | copy-start | bytes 589828
  2.3 18.6 %copy-start.5 = (f32[2,4,128]{2,1,0:T(4,128)S(1)}, f32[2,4,128]{2,1,0:T(4,128)}, u32[]{:S(2)}) copy-start(f32[2,4,128]{2,1,0:T(4,128)} %bias_ref.7) | copy-start | bytes 12292
  2.4 7.4 %collective-permute-start = (bf16[64,128]{1,0:T(8,128)(2,1)}, bf16[64,128]{1,0:T(8,128)(2,1)S(1)}, u32[]{:S(2)}, u32[]{:S(2)}) collective-permute-start(bf16[64,128]{1,0:T(8,128)(2,1)} %get-tuple-element.25), channel_id=1, source_target_pairs={{2,4},{3,5},{4,2},{5,3},{6,8},{7,9},{8,6},{9,7},{10,12},{11,13},{1... | collective-permute-start | bytes 49160 | tf_op jit(solution)/shard_map/ppermute | solution.py:63
  5.2 4.5 %collective-permute-start.1 = (bf16[64,128]{1,0:T(8,128)(2,1)}, bf16[64,128]{1,0:T(8,128)(2,1)S(1)}, u32[]{:S(2)}, u32[]{:S(2)}) collective-permute-start(bf16[64,128]{1,0:T(8,128)(2,1)} %get-tuple-element.26), channel_id=1, source_target_pairs={{0,2},{1,3},{2,0},{3,1},{4,6},{5,7},{6,4},{7,5},{8,10},{9,11},{10,... | collective-permute-start | bytes 49160 | tf_op jit(solution)/shard_map/ppermute | solution.py:63
  6.1 3.9 %collective-permute-start.2 = (bf16[64,128]{1,0:T(8,128)(2,1)}, bf16[64,128]{1,0:T(8,128)(2,1)S(1)}, u32[]{:S(2)}, u32[]{:S(2)}) collective-permute-start(bf16[64,128]{1,0:T(8,128)(2,1)} %get-tuple-element.27), channel_id=1, source_target_pairs={{0,1},{1,0},{2,3},{3,2},{4,5},{5,4},{6,7},{7,6},{8,9},{9,8},{10,11... | collective-permute-start | bytes 49160 | tf_op jit(solution)/shard_map/ppermute | solution.py:63
  7.6 0.7 %copy-start.8 = (s32[1,1,8,256]{3,2,1,0:T(8,128)S(1)}, s32[1,1,8,256]{3,2,1,0:T(8,128)}, u32[]{:S(2)}) copy-start(s32[1,1,8,256]{3,2,1,0:T(8,128)} %param.15) | copy-start | bytes 24580
  8.3 0.7 %copy-start.10 = (s32[1,1,8]{2,1,0:T(1,128)S(1)}, s32[1,1,8]{2,1,0:T(1,128)}, u32[]{:S(2)}) copy-start(s32[1,1,8]{2,1,0:T(1,128)} %param.16) | copy-start | bytes 100
  10.1 1.0 %copy-start.3 = (bf16[1024,128]{1,0:T(8,128)(2,1)S(1)}, bf16[1024,128]{1,0:T(8,128)(2,1)}, u32[]{:S(2)}) copy-start(bf16[1024,128]{1,0:T(8,128)(2,1)} %get-tuple-element.24.retained_ref) | copy-start | bytes 786436
  11.7 7.9 %collective-permute-start.3 = (bf16[512,128]{1,0:T(8,128)(2,1)S(1)}, bf16[512,128]{1,0:T(8,128)(2,1)S(1)}, u32[]{:S(2)}, u32[]{:S(2)}) collective-permute-start(bf16[512,128]{1,0:T(8,128)(2,1)S(1)} %get-tuple-element.34), channel_id=1, source_target_pairs={{2,4},{3,5},{4,2},{5,3},{6,8},{7,9},{8,6},{9,7},{10,12},{11,13},{1... | collective-permute-start | bytes 393224 | tf_op jit(solution)/shard_map/ppermute | solution.py:63
  14.2 6.3 %collective-permute-start.5 = (bf16[512,128]{1,0:T(8,128)(2,1)S(1)}, bf16[512,128]{1,0:T(8,128)(2,1)S(1)}, u32[]{:S(2)}, u32[]{:S(2)}) collective-permute-start(bf16[512,128]{1,0:T(8,128)(2,1)S(1)} %get-tuple-element.35), channel_id=1, source_target_pairs={{0,1},{1,0},{2,3},{3,2},{4,5},{5,4},{6,7},{7,6},{8,9},{9,8},{10,11... | collective-permute-start | bytes 393224 | tf_op jit(solution)/shard_map/ppermute | solution.py:63
  15.2 7.3 %collective-permute-start.7 = (bf16[256,128]{1,0:T(8,128)(2,1)S(1)}, bf16[256,128]{1,0:T(8,128)(2,1)S(1)}, u32[]{:S(2)}, u32[]{:S(2)}) collective-permute-start(bf16[256,128]{1,0:T(8,128)(2,1)S(1)} %get-tuple-element.36), channel_id=1, source_target_pairs={{0,2},{1,3},{2,0},{3,1},{4,6},{5,7},{6,4},{7,5},{8,10},{9,11},{10,... | collective-permute-start | bytes 196616 | tf_op jit(solution)/shard_map/ppermute | solution.py:63
  16.6 0.9 %copy-start = (bf16[2,3,128,128]{3,2,1,0:T(8,128)(2,1)S(1)}, bf16[2,3,128,128]{3,2,1,0:T(8,128)(2,1)}, u32[]{:S(2)}) copy-start(bf16[2,3,128,128]{3,2,1,0:T(8,128)(2,1)} %edge_ref.9) | copy-start | bytes 589828
  17.5 1.0 %copy-start.7 = (f32[1,1,4,16,1280]{4,3,2,1,0:T(8,128)S(1)}, f32[1,1,4,16,1280]{4,3,2,1,0:T(8,128)}, u32[]{:S(2)}) copy-start(f32[1,1,4,16,1280]{4,3,2,1,0:T(8,128)} %param.18) | copy-start | bytes 983044
  18.5 0.7 %copy-start.9 = (f32[2,4,128]{2,1,0:T(4,128)S(1)}, f32[2,4,128]{2,1,0:T(4,128)}, u32[]{:S(2)}) copy-start(f32[2,4,128]{2,1,0:T(4,128)} %geo_ref.1) | copy-start | bytes 12292
  19.6 4.4 %copy-start.2 = (bf16[2,3,128,128]{3,2,1,0:T(8,128)(2,1)S(1)}, bf16[2,3,128,128]{3,2,1,0:T(8,128)(2,1)}, u32[]{:S(2)}) copy-start(bf16[2,3,128,128]{3,2,1,0:T(8,128)(2,1)} %node_ref.3) | copy-start | bytes 589828
  19.6 4.4 %copy-start.4 = (s32[1,1,16,80]{3,2,1,0:T(8,128)S(1)}, s32[1,1,16,80]{3,2,1,0:T(8,128)}, u32[]{:S(2)}) copy-start(s32[1,1,16,80]{3,2,1,0:T(8,128)} %param.17) | copy-start | bytes 15364
  19.6 4.4 %copy-start.6 = (f32[2,2,128]{2,1,0:T(2,128)S(1)}, f32[2,2,128]{2,1,0:T(2,128)}, u32[]{:S(2)}) copy-start(f32[2,2,128]{2,1,0:T(2,128)} %gain_ref.3) | copy-start | bytes 6148
  19.6 4.3 %collective-permute-start.4 = (bf16[256,128]{1,0:T(8,128)(2,1)S(1)}, bf16[256,128]{1,0:T(8,128)(2,1)S(1)}, u32[]{:S(2)}, u32[]{:S(2)}) collective-permute-start(bf16[256,128]{1,0:T(8,128)(2,1)S(1)} %slice.16), channel_id=1, source_target_pairs={{0,1},{1,0},{2,3},{3,2},{4,5},{5,4},{6,7},{7,6},{8,9},{9,8},{10,11... | collective-permute-start | bytes 196616 | tf_op jit(solution)/shard_map/ppermute | solution.py:63
  20.5 3.4 %collective-permute-start.6 = (bf16[256,128]{1,0:T(8,128)(2,1)S(1)}, bf16[256,128]{1,0:T(8,128)(2,1)S(1)}, u32[]{:S(2)}, u32[]{:S(2)}) collective-permute-start(bf16[256,128]{1,0:T(8,128)(2,1)S(1)} %slice.17), channel_id=1, source_target_pairs={{0,2},{1,3},{2,0},{3,1},{4,6},{5,7},{6,4},{7,5},{8,10},{9,11},{10,... | collective-permute-start | bytes 196616 | tf_op jit(solution)/shard_map/ppermute | solution.py:63
  30.3 7.3 %collective-permute-start.8 = (bf16[512,128]{1,0:T(8,128)(2,1)S(1)}, bf16[512,128]{1,0:T(8,128)(2,1)S(1)}, u32[]{:S(2)}, u32[]{:S(2)}) collective-permute-start(bf16[512,128]{1,0:T(8,128)(2,1)S(1)} %get-tuple-element.40), channel_id=1, source_target_pairs={{2,4},{3,5},{4,2},{5,3},{6,8},{7,9},{8,6},{9,7},{10,12},{11,13},{1... | collective-permute-start | bytes 393224 | tf_op jit(solution)/shard_map/ppermute | solution.py:63
  32.6 6.1 %collective-permute-start.10 = (bf16[512,128]{1,0:T(8,128)(2,1)S(1)}, bf16[512,128]{1,0:T(8,128)(2,1)S(1)}, u32[]{:S(2)}, u32[]{:S(2)}) collective-permute-start(bf16[512,128]{1,0:T(8,128)(2,1)S(1)} %get-tuple-element.41), channel_id=1, source_target_pairs={{0,1},{1,0},{2,3},{3,2},{4,5},{5,4},{6,7},{7,6},{8,9},{9,8},{10,11... | collective-permute-start | bytes 393224 | tf_op jit(solution)/shard_map/ppermute | solution.py:63
  33.6 7.2 %collective-permute-start.12 = (bf16[256,128]{1,0:T(8,128)(2,1)S(1)}, bf16[256,128]{1,0:T(8,128)(2,1)S(1)}, u32[]{:S(2)}, u32[]{:S(2)}) collective-permute-start(bf16[256,128]{1,0:T(8,128)(2,1)S(1)} %get-tuple-element.42), channel_id=1, source_target_pairs={{0,2},{1,3},{2,0},{3,1},{4,6},{5,7},{6,4},{7,5},{8,10},{9,11},{10,... | collective-permute-start | bytes 196616 | tf_op jit(solution)/shard_map/ppermute | solution.py:63
  37.6 4.6 %collective-permute-start.9 = (bf16[256,128]{1,0:T(8,128)(2,1)S(1)}, bf16[256,128]{1,0:T(8,128)(2,1)S(1)}, u32[]{:S(2)}, u32[]{:S(2)}) collective-permute-start(bf16[256,128]{1,0:T(8,128)(2,1)S(1)} %slice.18), channel_id=1, source_target_pairs={{0,1},{1,0},{2,3},{3,2},{4,5},{5,4},{6,7},{7,6},{8,9},{9,8},{10,11... | collective-permute-start | bytes 196616 | tf_op jit(solution)/shard_map/ppermute | solution.py:63
  38.7 3.5 %collective-permute-start.11 = (bf16[256,128]{1,0:T(8,128)(2,1)S(1)}, bf16[256,128]{1,0:T(8,128)(2,1)S(1)}, u32[]{:S(2)}, u32[]{:S(2)}) collective-permute-start(bf16[256,128]{1,0:T(8,128)(2,1)S(1)} %slice.19), channel_id=1, source_target_pairs={{0,2},{1,3},{2,0},{3,1},{4,6},{5,7},{6,4},{7,5},{8,10},{9,11},{10,... | collective-permute-start | bytes 196616 | tf_op jit(solution)/shard_map/ppermute | solution.py:63

commit v4 on v3

--- a/solution.py
+++ b/solution.py
@@ -152,13 +152,12 @@
     gather_ghosts(extended_ref, wanted_ref, send_refs)
 
 
-def want_kernel(order, rows_ref, count_ref, wanted_ref):
+def want_kernel(order, rows_ref, retained_ref, wanted_ref, kept_ref):
     ghosts = rows_ref.shape[1]
-    lane = lax.broadcasted_iota(jnp.int32, (1, ghosts), 1)
+    kept_ref[...] = retained_ref[...]
     for place, link in enumerate(order):
         target = section(step("gx", link[0]), step("gy", link[1]))
-        wanted = rows_ref[pl.ds(target, 1), :]
-        wanted = jnp.where(lane < count_ref[target], wanted, -1).astype(F32)
+        wanted = rows_ref[pl.ds(target, 1), :].astype(F32)
         wanted_ref[place] = jnp.transpose(jnp.broadcast_to(wanted, (128, ghosts)))
 
 
@@ -302,15 +301,17 @@
     feats = geometry.reshape(-1, rows_total)
     layers = edge_w.shape[0]
     deep = 2 * feats.shape[0] + width
-    wanted = pl.pallas_call(
+    valid_ghosts = jnp.where(jnp.arange(ghosts)[None, :] < ghost_total[:, None], ghost_list, -1)
+    wanted, kept = pl.pallas_call(
         functools.partial(want_kernel, sum(groups, [])),
-        out_shape=jax.ShapeDtypeStruct((len(all_links), ghosts, 128), F32),
-        in_specs=[VMEM, SMEM],
-        out_specs=VMEM,
+        out_shape=[jax.ShapeDtypeStruct((len(all_links), ghosts, 128), F32), rows_of(owned.shape[0])],
+        in_specs=[VMEM] * 2,
+        out_specs=[VMEM] * 2,
         compiler_params=PARAMS,
         cost_estimate=pl.CostEstimate(flops=500_000_000, bytes_accessed=1_000_000, transcendentals=0),
         name="want",
-    )(ghost_list, ghost_total)
+    )(valid_ghosts, retained)
+
     extended, *sends = pl.pallas_call(
         functools.partial(build_kernel, sides),
         out_shape=[rows_of(rows_total)] + [rows_of(ghosts * len(group)) for group in groups],
@@ -318,7 +319,7 @@
         out_specs=[VMEM] * (1 + len(groups)),
         compiler_params=PARAMS,
         name="build",
-    )(retained, *arrivals, wanted)
+    )(kept, *arrivals, wanted)
 
     turned, first_mats, second_mats = pl.pallas_call(
         static_kernel,

time: 49.1 us -> 48.1 us (0.980)
  local copies, waits for them, and re-layouts: 4.94 us -> 3.59 us
  other arithmetic: 0 us -> 0.77 us
  Pallas kernels: 20.2 us -> 19.7 us
    unnamed x22 -> x18, local copies, waits for them, and re-layouts: 4.92 us -> 3.57 us
    select_n x0 -> x1, other arithmetic: none -> 0.77 us  [body(): jnp.where(jnp.arange(ghosts)[None, :] < ghost_total[:, None], ghost_list,...]
    pallas_call x1, Pallas kernels: 0.78 us -> 0.23 us  [body(): pl.pallas_call(functools.partial(want_kernel, sum(groups, [])), out_shape...]
  transfers between devices with their start and end apart: 13 -> 13, of which waited for: 4 -> 4; matrix products, arithmetic and copies ran while one was open for 0% -> 2% of each run, Pallas kernels for 9% -> 8%
where the time goes in v4:
time: 48.1 us; the launch traced here: 47.7 us
  Pallas kernels  19.7 us (41%)
  starting transfers between devices  17.6 us (37%)
  waiting for transfers between devices  5.82 us (12%)
  local copies, waits for them, and re-layouts  3.59 us (7%)
  other arithmetic  0.77 us (2%)
    ppermute x13, starting transfers between devices, swap(): return lax.ppermute(value, ('gx', 'gy'), pairs)  17.6 us
    pallas_call x2, Pallas kernels, body(): pl.pallas_call(functools.partial(layer_kernel, layer, last, ghosts, all_l...  12.7 us
    ppermute x13, waiting for transfers between devices, swap(): return lax.ppermute(value, ('gx', 'gy'), pairs)  5.82 us
    unnamed x18, local copies, waits for them, and re-layouts  3.57 us
    pallas_call x2, Pallas kernels, body(): pl.pallas_call(functools.partial(receive_kernel, layer), out_shape=[jax.S...  3.25 us
    pallas_call x1, Pallas kernels, body(): pl.pallas_call(functools.partial(pack_kernel, sides), out_shape=[rows_of(...  2.32 us
  transfers between devices with their start and end apart: 13, of which 4 were waited for; matrix products, arithmetic and copies ran while one was open for 2% of the time, Pallas kernels for 8%

profile of v4, /device:TPU:8, one launch (start us, length us, event | category | flops | bytes accessed | tf_op | source)
XLA Modules:
  0.0 47.7 jit_solution(16331497918975566362)
XLA Ops:
  0.0 2.3 %pack.1 = (bf16[1024,128]{1,0:T(8,128)(2,1)}, bf16[64,128]{1,0:T(8,128)(2,1)}, bf16[64,128]{1,0:T(8,128)(2,1)}, bf16[64,128]{1,0:T(8,128)(2,1)}) custom-call(bf16[1024,128]{1,0:T(8,128)(2,1)} %bitcast.12, s32[4,64]{1,0:T(4,128)} %bitcast.13, s32[4]{0:T(128)} %bitcast.14), custom_call_target="tpu_custom_call" | custom-call | tf_op jit(solution)/shard_map/pack/pallas_call | solution.py:290
  2.4 2.9 %collective-permute-start = (bf16[64,128]{1,0:T(8,128)(2,1)}, bf16[64,128]{1,0:T(8,128)(2,1)S(1)}, u32[]{:S(2)}, u32[]{:S(2)}) collective-permute-start(bf16[64,128]{1,0:T(8,128)(2,1)} %get-tuple-element.28), channel_id=1, source_target_pairs={{2,4},{3,5},{4,2},{5,3},{6,8},{7,9},{8,6},{9,7},{10,12},{11,13},{1... | collective-permute-start | bytes 49160 | tf_op jit(solution)/shard_map/ppermute | solution.py:63
  5.2 0.9 %collective-permute-start.1 = (bf16[64,128]{1,0:T(8,128)(2,1)}, bf16[64,128]{1,0:T(8,128)(2,1)S(1)}, u32[]{:S(2)}, u32[]{:S(2)}) collective-permute-start(bf16[64,128]{1,0:T(8,128)(2,1)} %get-tuple-element.29), channel_id=1, source_target_pairs={{0,2},{1,3},{2,0},{3,1},{4,6},{5,7},{6,4},{7,5},{8,10},{9,11},{10,... | collective-permute-start | bytes 49160 | tf_op jit(solution)/shard_map/ppermute | solution.py:63
  6.1 1.5 %collective-permute-start.2 = (bf16[64,128]{1,0:T(8,128)(2,1)}, bf16[64,128]{1,0:T(8,128)(2,1)S(1)}, u32[]{:S(2)}, u32[]{:S(2)}) collective-permute-start(bf16[64,128]{1,0:T(8,128)(2,1)} %get-tuple-element.30), channel_id=1, source_target_pairs={{0,1},{1,0},{2,3},{3,2},{4,5},{5,4},{6,7},{7,6},{8,9},{9,8},{10,11... | collective-permute-start | bytes 49160 | tf_op jit(solution)/shard_map/ppermute | solution.py:63
  7.6 0.8 %bitcast_select_fusion.rows_ref = s32[8,256]{1,0:T(8,128)S(1)} fusion(s32[1,1,8,256]{3,2,1,0:T(8,128)} %param.15, s32[8]{0:T(128)} %bitcast.15), kind=kLoop, calls=%fused_computation | loop fusion | flops 4096 | bytes 16416 | tf_op jit(solution)/shard_map/jit(_where)/select_n | solution.py:304
  8.4 0.9 %copy-done.7 = bf16[1024,128]{1,0:T(8,128)(2,1)S(1)} copy-done((bf16[1024,128]{1,0:T(8,128)(2,1)S(1)}, bf16[1024,128]{1,0:T(8,128)(2,1)}, u32[]{:S(2)}) %copy-start.7) | copy-done | bytes 262168
  10.1 0.7 %build.1 = (bf16[1280,128]{1,0:T(8,128)(2,1)S(1)}, bf16[512,128]{1,0:T(8,128)(2,1)S(1)}, bf16[512,128]{1,0:T(8,128)(2,1)S(1)}, bf16[256,128]{1,0:T(8,128)(2,1)S(1)}) custom-call(bf16[1024,128]{1,0:T(8,128)(2,1)S(1)} %get-tuple-element.27.retained_ref, bf16[64,128]{1,0:T(8,128)(2,1)S(1)} %collective-permute-done.refs_0_, ...), custom_call_target="tpu_custom_call" | custom-call | tf_op jit(solution)/shard_map/build/pallas_call | solution.py:315
  10.8 2.2 %collective-permute-start.3 = (bf16[512,128]{1,0:T(8,128)(2,1)S(1)}, bf16[512,128]{1,0:T(8,128)(2,1)S(1)}, u32[]{:S(2)}, u32[]{:S(2)}) collective-permute-start(bf16[512,128]{1,0:T(8,128)(2,1)S(1)} %get-tuple-element.38), channel_id=1, source_target_pairs={{2,4},{3,5},{4,2},{5,3},{6,8},{7,9},{8,6},{9,7},{10,12},{11,13},{1... | collective-permute-start | bytes 393224 | tf_op jit(solution)/shard_map/ppermute | solution.py:63
  13.0 1.2 %collective-permute-start.5 = (bf16[512,128]{1,0:T(8,128)(2,1)S(1)}, bf16[512,128]{1,0:T(8,128)(2,1)S(1)}, u32[]{:S(2)}, u32[]{:S(2)}) collective-permute-start(bf16[512,128]{1,0:T(8,128)(2,1)S(1)} %get-tuple-element.39), channel_id=1, source_target_pairs={{0,1},{1,0},{2,3},{3,2},{4,5},{5,4},{6,7},{7,6},{8,9},{9,8},{10,11... | collective-permute-start | bytes 393224 | tf_op jit(solution)/shard_map/ppermute | solution.py:63
  14.3 1.3 %collective-permute-start.7 = (bf16[256,128]{1,0:T(8,128)(2,1)S(1)}, bf16[256,128]{1,0:T(8,128)(2,1)S(1)}, u32[]{:S(2)}, u32[]{:S(2)}) collective-permute-start(bf16[256,128]{1,0:T(8,128)(2,1)S(1)} %get-tuple-element.40), channel_id=1, source_target_pairs={{0,2},{1,3},{2,0},{3,1},{4,6},{5,7},{6,4},{7,5},{8,10},{9,11},{10,... | collective-permute-start | bytes 196616 | tf_op jit(solution)/shard_map/ppermute | solution.py:63
  15.6 0.9 %copy-done = bf16[2,3,128,128]{3,2,1,0:T(8,128)(2,1)S(1)} copy-done((bf16[2,3,128,128]{3,2,1,0:T(8,128)(2,1)S(1)}, bf16[2,3,128,128]{3,2,1,0:T(8,128)(2,1)}, u32[]{:S(2)}) %copy-start) | copy-done | bytes 196632
  16.6 1.0 %copy-done.6 = f32[1,1,4,16,1280]{4,3,2,1,0:T(8,128)S(1)} copy-done((f32[1,1,4,16,1280]{4,3,2,1,0:T(8,128)S(1)}, f32[1,1,4,16,1280]{4,3,2,1,0:T(8,128)}, u32[]{:S(2)}) %copy-start.6) | copy-done | bytes 327704
  18.7 0.9 %collective-permute-start.4 = (bf16[256,128]{1,0:T(8,128)(2,1)S(1)}, bf16[256,128]{1,0:T(8,128)(2,1)S(1)}, u32[]{:S(2)}, u32[]{:S(2)}) collective-permute-start(bf16[256,128]{1,0:T(8,128)(2,1)S(1)} %slice.16), channel_id=1, source_target_pairs={{0,1},{1,0},{2,3},{3,2},{4,5},{5,4},{6,7},{7,6},{8,9},{9,8},{10,11... | collective-permute-start | bytes 196616 | tf_op jit(solution)/shard_map/ppermute | solution.py:63
  20.0 1.6 %receive.2 = (bf16[1280,2048]{1,0:T(8,128)(2,1)S(1)}, f32[1280,128]{1,0:T(8,128)S(1)}) custom-call(bf16[1280,128]{1,0:T(8,128)(2,1)S(1)} %get-tuple-element.32.extended_ref, bf16[1280,128]{1,0:T(8,128)(2,1)S(1)} %get-tuple-element.33.turned_ref, bf16[2,256,2048]{2,1,0:T(8,128)(2,1)S(1)} %get-tuple-element.34.first_ref, ...), custom_call_target="tpu_custom_call" | custom-call | flops 2500000000 | bytes 6000000 | tf_op jit(solution)/shard_map/receive/pallas_call | solution.py:341
  21.6 1.4 %collective-permute-done.4.refs_0_ = bf16[256,128]{1,0:T(8,128)(2,1)S(1)} collective-permute-done((bf16[256,128]{1,0:T(8,128)(2,1)S(1)}, bf16[256,128]{1,0:T(8,128)(2,1)S(1)}, u32[]{:S(2)}, u32[]{:S(2)}) %collective-permute-start.4) | collective-permute-done | bytes 65568 | tf_op jit(solution)/shard_map/ppermute | solution.py:63
  23.0 6.2 %layer.2 = (bf16[1280,128]{1,0:T(8,128)(2,1)S(1)}, bf16[512,128]{1,0:T(8,128)(2,1)S(1)}, bf16[512,128]{1,0:T(8,128)(2,1)S(1)}, bf16[256,128]{1,0:T(8,128)(2,1)S(1)}) custom-call(bf16[1280,128]{1,0:T(8,128)(2,1)S(1)} %get-tuple-element.32.extended_ref, bf16[1280,2048]{1,0:T(8,128)(2,1)S(1)} %get-tuple-element.35.base_ref, ...), custom_call_target="tpu_custom_call" | custom-call | tf_op jit(solution)/shard_map/layer/pallas_call | solution.py:355
  29.3 2.3 %collective-permute-start.8 = (bf16[512,128]{1,0:T(8,128)(2,1)S(1)}, bf16[512,128]{1,0:T(8,128)(2,1)S(1)}, u32[]{:S(2)}, u32[]{:S(2)}) collective-permute-start(bf16[512,128]{1,0:T(8,128)(2,1)S(1)} %get-tuple-element.44), channel_id=1, source_target_pairs={{2,4},{3,5},{4,2},{5,3},{6,8},{7,9},{8,6},{9,7},{10,12},{11,13},{1... | collective-permute-start | bytes 393224 | tf_op jit(solution)/shard_map/ppermute | solution.py:63
  31.6 1.0 %collective-permute-start.10 = (bf16[512,128]{1,0:T(8,128)(2,1)S(1)}, bf16[512,128]{1,0:T(8,128)(2,1)S(1)}, u32[]{:S(2)}, u32[]{:S(2)}) collective-permute-start(bf16[512,128]{1,0:T(8,128)(2,1)S(1)} %get-tuple-element.45), channel_id=1, source_target_pairs={{0,1},{1,0},{2,3},{3,2},{4,5},{5,4},{6,7},{7,6},{8,9},{9,8},{10,11... | collective-permute-start | bytes 393224 | tf_op jit(solution)/shard_map/ppermute | solution.py:63
  32.6 1.4 %collective-permute-start.12 = (bf16[256,128]{1,0:T(8,128)(2,1)S(1)}, bf16[256,128]{1,0:T(8,128)(2,1)S(1)}, u32[]{:S(2)}, u32[]{:S(2)}) collective-permute-start(bf16[256,128]{1,0:T(8,128)(2,1)S(1)} %get-tuple-element.46), channel_id=1, source_target_pairs={{0,2},{1,3},{2,0},{3,1},{4,6},{5,7},{6,4},{7,5},{8,10},{9,11},{10,... | collective-permute-start | bytes 196616 | tf_op jit(solution)/shard_map/ppermute | solution.py:63
  34.1 2.5 %collective-permute-done.8.refs_1_ = bf16[512,128]{1,0:T(8,128)(2,1)S(1)} collective-permute-done((bf16[512,128]{1,0:T(8,128)(2,1)S(1)}, bf16[512,128]{1,0:T(8,128)(2,1)S(1)}, u32[]{:S(2)}, u32[]{:S(2)}) %collective-permute-start.8) | collective-permute-done | bytes 131104 | tf_op jit(solution)/shard_map/ppermute | solution.py:63
  36.6 1.1 %collective-permute-start.9 = (bf16[256,128]{1,0:T(8,128)(2,1)S(1)}, bf16[256,128]{1,0:T(8,128)(2,1)S(1)}, u32[]{:S(2)}, u32[]{:S(2)}) collective-permute-start(bf16[256,128]{1,0:T(8,128)(2,1)S(1)} %slice.18), channel_id=1, source_target_pairs={{0,1},{1,0},{2,3},{3,2},{4,5},{5,4},{6,7},{7,6},{8,9},{9,8},{10,11... | collective-permute-start | bytes 196616 | tf_op jit(solution)/shard_map/ppermute | solution.py:63
  38.2 1.6 %receive.3 = (bf16[1280,2048]{1,0:T(8,128)(2,1)S(1)}, f32[1280,128]{1,0:T(8,128)S(1)}) custom-call(bf16[1280,128]{1,0:T(8,128)(2,1)S(1)} %get-tuple-element.41.extended_ref, bf16[1280,128]{1,0:T(8,128)(2,1)S(1)} %get-tuple-element.33.turned_ref, bf16[2,256,2048]{2,1,0:T(8,128)(2,1)S(1)} %get-tuple-element.34.first_ref, ...), custom_call_target="tpu_custom_call" | custom-call | flops 2500000000 | bytes 6000000 | tf_op jit(solution)/shard_map/receive/pallas_call | solution.py:341
  39.8 1.3 %collective-permute-done.9.refs_0_ = bf16[256,128]{1,0:T(8,128)(2,1)S(1)} collective-permute-done((bf16[256,128]{1,0:T(8,128)(2,1)S(1)}, bf16[256,128]{1,0:T(8,128)(2,1)S(1)}, u32[]{:S(2)}, u32[]{:S(2)}) %collective-permute-start.9) | collective-permute-done | bytes 65568 | tf_op jit(solution)/shard_map/ppermute | solution.py:63
  41.2 6.5 %layer.3 = bf16[1280,128]{1,0:T(8,128)(2,1)} custom-call(bf16[1280,128]{1,0:T(8,128)(2,1)S(1)} %get-tuple-element.41.extended_ref, bf16[1280,2048]{1,0:T(8,128)(2,1)S(1)} %get-tuple-element.42.base_ref, f32[1280,128]{1,0:T(8,128)S(1)} %get-tuple-element.43.own_ref, s32[16,80]{1,0:T(8,128)S(1)} %bitcast.10, bf16[2,3,128,128]{3,2,1,0:T(8,128)(2,1)S(1)} %copy-done.1, ...), custom_call_target="tpu_custom_call" | custom-call | tf_op jit(solution)/shard_map/layer/pallas_call | solution.py:355
  (33 shorter events, 2.7 us)
Async XLA Ops:
  2.3 17.6 %copy-start.1 = (bf16[2,3,128,128]{3,2,1,0:T(8,128)(2,1)S(1)}, bf16[2,3,128,128]{3,2,1,0:T(8,128)(2,1)}, u32[]{:S(2)}) copy-start(bf16[2,3,128,128]{3,2,1,0:T(8,128)(2,1)} %edge_ref.9) | copy-start | bytes 589828
  2.3 17.6 %copy-start.4 = (f32[2,4,128]{2,1,0:T(4,128)S(1)}, f32[2,4,128]{2,1,0:T(4,128)}, u32[]{:S(2)}) copy-start(f32[2,4,128]{2,1,0:T(4,128)} %bias_ref.7) | copy-start | bytes 12292
  2.4 7.2 %collective-permute-start = (bf16[64,128]{1,0:T(8,128)(2,1)}, bf16[64,128]{1,0:T(8,128)(2,1)S(1)}, u32[]{:S(2)}, u32[]{:S(2)}) collective-permute-start(bf16[64,128]{1,0:T(8,128)(2,1)} %get-tuple-element.28), channel_id=1, source_target_pairs={{2,4},{3,5},{4,2},{5,3},{6,8},{7,9},{8,6},{9,7},{10,12},{11,13},{1... | collective-permute-start | bytes 49160 | tf_op jit(solution)/shard_map/ppermute | solution.py:63
  5.2 4.3 %collective-permute-start.1 = (bf16[64,128]{1,0:T(8,128)(2,1)}, bf16[64,128]{1,0:T(8,128)(2,1)S(1)}, u32[]{:S(2)}, u32[]{:S(2)}) collective-permute-start(bf16[64,128]{1,0:T(8,128)(2,1)} %get-tuple-element.29), channel_id=1, source_target_pairs={{0,2},{1,3},{2,0},{3,1},{4,6},{5,7},{6,4},{7,5},{8,10},{9,11},{10,... | collective-permute-start | bytes 49160 | tf_op jit(solution)/shard_map/ppermute | solution.py:63
  6.1 3.9 %collective-permute-start.2 = (bf16[64,128]{1,0:T(8,128)(2,1)}, bf16[64,128]{1,0:T(8,128)(2,1)S(1)}, u32[]{:S(2)}, u32[]{:S(2)}) collective-permute-start(bf16[64,128]{1,0:T(8,128)(2,1)} %get-tuple-element.30), channel_id=1, source_target_pairs={{0,1},{1,0},{2,3},{3,2},{4,5},{5,4},{6,7},{7,6},{8,9},{9,8},{10,11... | collective-permute-start | bytes 49160 | tf_op jit(solution)/shard_map/ppermute | solution.py:63
  8.4 1.0 %copy-start.7 = (bf16[1024,128]{1,0:T(8,128)(2,1)S(1)}, bf16[1024,128]{1,0:T(8,128)(2,1)}, u32[]{:S(2)}) copy-start(bf16[1024,128]{1,0:T(8,128)(2,1)} %get-tuple-element.26.retained_ref) | copy-start | bytes 786436
  10.8 7.9 %collective-permute-start.3 = (bf16[512,128]{1,0:T(8,128)(2,1)S(1)}, bf16[512,128]{1,0:T(8,128)(2,1)S(1)}, u32[]{:S(2)}, u32[]{:S(2)}) collective-permute-start(bf16[512,128]{1,0:T(8,128)(2,1)S(1)} %get-tuple-element.38), channel_id=1, source_target_pairs={{2,4},{3,5},{4,2},{5,3},{6,8},{7,9},{8,6},{9,7},{10,12},{11,13},{1... | collective-permute-start | bytes 393224 | tf_op jit(solution)/shard_map/ppermute | solution.py:63
  13.0 6.5 %collective-permute-start.5 = (bf16[512,128]{1,0:T(8,128)(2,1)S(1)}, bf16[512,128]{1,0:T(8,128)(2,1)S(1)}, u32[]{:S(2)}, u32[]{:S(2)}) collective-permute-start(bf16[512,128]{1,0:T(8,128)(2,1)S(1)} %get-tuple-element.39), channel_id=1, source_target_pairs={{0,1},{1,0},{2,3},{3,2},{4,5},{5,4},{6,7},{7,6},{8,9},{9,8},{10,11... | collective-permute-start | bytes 393224 | tf_op jit(solution)/shard_map/ppermute | solution.py:63
  14.3 7.3 %collective-permute-start.7 = (bf16[256,128]{1,0:T(8,128)(2,1)S(1)}, bf16[256,128]{1,0:T(8,128)(2,1)S(1)}, u32[]{:S(2)}, u32[]{:S(2)}) collective-permute-start(bf16[256,128]{1,0:T(8,128)(2,1)S(1)} %get-tuple-element.40), channel_id=1, source_target_pairs={{0,2},{1,3},{2,0},{3,1},{4,6},{5,7},{6,4},{7,5},{8,10},{9,11},{10,... | collective-permute-start | bytes 196616 | tf_op jit(solution)/shard_map/ppermute | solution.py:63
  15.6 0.9 %copy-start = (bf16[2,3,128,128]{3,2,1,0:T(8,128)(2,1)S(1)}, bf16[2,3,128,128]{3,2,1,0:T(8,128)(2,1)}, u32[]{:S(2)}) copy-start(bf16[2,3,128,128]{3,2,1,0:T(8,128)(2,1)} %edge_ref.9) | copy-start | bytes 589828
  16.6 1.0 %copy-start.6 = (f32[1,1,4,16,1280]{4,3,2,1,0:T(8,128)S(1)}, f32[1,1,4,16,1280]{4,3,2,1,0:T(8,128)}, u32[]{:S(2)}) copy-start(f32[1,1,4,16,1280]{4,3,2,1,0:T(8,128)} %param.18) | copy-start | bytes 983044
  17.5 0.7 %copy-start.8 = (f32[2,4,128]{2,1,0:T(4,128)S(1)}, f32[2,4,128]{2,1,0:T(4,128)}, u32[]{:S(2)}) copy-start(f32[2,4,128]{2,1,0:T(4,128)} %geo_ref.1) | copy-start | bytes 12292
  18.6 4.4 %copy-start.2 = (bf16[2,3,128,128]{3,2,1,0:T(8,128)(2,1)S(1)}, bf16[2,3,128,128]{3,2,1,0:T(8,128)(2,1)}, u32[]{:S(2)}) copy-start(bf16[2,3,128,128]{3,2,1,0:T(8,128)(2,1)} %node_ref.3) | copy-start | bytes 589828
  18.6 4.4 %copy-start.3 = (s32[1,1,16,80]{3,2,1,0:T(8,128)S(1)}, s32[1,1,16,80]{3,2,1,0:T(8,128)}, u32[]{:S(2)}) copy-start(s32[1,1,16,80]{3,2,1,0:T(8,128)} %param.17) | copy-start | bytes 15364
  18.7 4.4 %copy-start.5 = (f32[2,2,128]{2,1,0:T(2,128)S(1)}, f32[2,2,128]{2,1,0:T(2,128)}, u32[]{:S(2)}) copy-start(f32[2,2,128]{2,1,0:T(2,128)} %gain_ref.3) | copy-start | bytes 6148
  18.7 4.3 %collective-permute-start.4 = (bf16[256,128]{1,0:T(8,128)(2,1)S(1)}, bf16[256,128]{1,0:T(8,128)(2,1)S(1)}, u32[]{:S(2)}, u32[]{:S(2)}) collective-permute-start(bf16[256,128]{1,0:T(8,128)(2,1)S(1)} %slice.16), channel_id=1, source_target_pairs={{0,1},{1,0},{2,3},{3,2},{4,5},{5,4},{6,7},{7,6},{8,9},{9,8},{10,11... | collective-permute-start | bytes 196616 | tf_op jit(solution)/shard_map/ppermute | solution.py:63
  19.6 3.4 %collective-permute-start.6 = (bf16[256,128]{1,0:T(8,128)(2,1)S(1)}, bf16[256,128]{1,0:T(8,128)(2,1)S(1)}, u32[]{:S(2)}, u32[]{:S(2)}) collective-permute-start(bf16[256,128]{1,0:T(8,128)(2,1)S(1)} %slice.17), channel_id=1, source_target_pairs={{0,2},{1,3},{2,0},{3,1},{4,6},{5,7},{6,4},{7,5},{8,10},{9,11},{10,... | collective-permute-start | bytes 196616 | tf_op jit(solution)/shard_map/ppermute | solution.py:63
  29.3 7.3 %collective-permute-start.8 = (bf16[512,128]{1,0:T(8,128)(2,1)S(1)}, bf16[512,128]{1,0:T(8,128)(2,1)S(1)}, u32[]{:S(2)}, u32[]{:S(2)}) collective-permute-start(bf16[512,128]{1,0:T(8,128)(2,1)S(1)} %get-tuple-element.44), channel_id=1, source_target_pairs={{2,4},{3,5},{4,2},{5,3},{6,8},{7,9},{8,6},{9,7},{10,12},{11,13},{1... | collective-permute-start | bytes 393224 | tf_op jit(solution)/shard_map/ppermute | solution.py:63
  31.6 6.1 %collective-permute-start.10 = (bf16[512,128]{1,0:T(8,128)(2,1)S(1)}, bf16[512,128]{1,0:T(8,128)(2,1)S(1)}, u32[]{:S(2)}, u32[]{:S(2)}) collective-permute-start(bf16[512,128]{1,0:T(8,128)(2,1)S(1)} %get-tuple-element.45), channel_id=1, source_target_pairs={{0,1},{1,0},{2,3},{3,2},{4,5},{5,4},{6,7},{7,6},{8,9},{9,8},{10,11... | collective-permute-start | bytes 393224 | tf_op jit(solution)/shard_map/ppermute | solution.py:63
  32.6 7.2 %collective-permute-start.12 = (bf16[256,128]{1,0:T(8,128)(2,1)S(1)}, bf16[256,128]{1,0:T(8,128)(2,1)S(1)}, u32[]{:S(2)}, u32[]{:S(2)}) collective-permute-start(bf16[256,128]{1,0:T(8,128)(2,1)S(1)} %get-tuple-element.46), channel_id=1, source_target_pairs={{0,2},{1,3},{2,0},{3,1},{4,6},{5,7},{6,4},{7,5},{8,10},{9,11},{10,... | collective-permute-start | bytes 196616 | tf_op jit(solution)/shard_map/ppermute | solution.py:63
  36.6 4.6 %collective-permute-start.9 = (bf16[256,128]{1,0:T(8,128)(2,1)S(1)}, bf16[256,128]{1,0:T(8,128)(2,1)S(1)}, u32[]{:S(2)}, u32[]{:S(2)}) collective-permute-start(bf16[256,128]{1,0:T(8,128)(2,1)S(1)} %slice.18), channel_id=1, source_target_pairs={{0,1},{1,0},{2,3},{3,2},{4,5},{5,4},{6,7},{7,6},{8,9},{9,8},{10,11... | collective-permute-start | bytes 196616 | tf_op jit(solution)/shard_map/ppermute | solution.py:63
  37.8 3.4 %collective-permute-start.11 = (bf16[256,128]{1,0:T(8,128)(2,1)S(1)}, bf16[256,128]{1,0:T(8,128)(2,1)S(1)}, u32[]{:S(2)}, u32[]{:S(2)}) collective-permute-start(bf16[256,128]{1,0:T(8,128)(2,1)S(1)} %slice.19), channel_id=1, source_target_pairs={{0,2},{1,3},{2,0},{3,1},{4,6},{5,7},{6,4},{7,5},{8,10},{9,11},{10,... | collective-permute-start | bytes 196616 | tf_op jit(solution)/shard_map/ppermute | solution.py:63

commit v5 on v4

--- a/solution.py
+++ b/solution.py
@@ -11,7 +11,8 @@
 
 F32 = jnp.float32
 BF16 = jnp.bfloat16
-CHUNK = 256
+CHUNK = 1280
+NOTHING = -1e30
 VMEM = pl.BlockSpec(memory_space=pltpu.VMEM)
 SMEM = pl.BlockSpec(memory_space=pltpu.SMEM)
 HBM = pl.BlockSpec(memory_space=pltpu.HBM)
@@ -188,7 +189,7 @@
         second_ref[layer, pl.ds(width, width), pl.ds(width, width)] = edge_second
 
 
-def receive_kernel(layer, extended_ref, turned_ref, first_ref, edge_ref, bias_ref, base_ref, table_ref):
+def receive_kernel(layer, extended_ref, turned_ref, first_ref, edge_ref, bias_ref, links_ref, base_ref, table_ref, empty_ref):
     own = jnp.concatenate([turned_ref[...], extended_ref[...]], axis=1)
     width = extended_ref.shape[1]
     bias = bias_ref[layer, pl.ds(0, 1), :]
@@ -197,6 +198,15 @@
         columns = pl.ds(start, 2 * width)
         base_ref[:, columns] = (jnp.dot(own, first_ref[layer, :, columns], preferred_element_type=F32) + bias).astype(BF16)
     table_ref[...] = jnp.dot(extended_ref[...], edge_ref[layer, 1], preferred_element_type=F32)
+    slots, tiles = links_ref.shape
+    rows_total = extended_ref.shape[0]
+    vacant = jnp.where(links_ref[...] < 0, 1.0, 0.0).astype(BF16)
+    counts = lax.dot_general(
+        vacant, jnp.ones((slots, width), BF16), (((0,), (0,)), ((), ())), preferred_element_type=F32
+    ).astype(BF16)
+    tile_of = lax.div(lax.broadcasted_iota(jnp.int32, (rows_total, tiles), 0), rows_total // tiles)
+    spread = (tile_of == lax.broadcasted_iota(jnp.int32, (rows_total, tiles), 1)).astype(F32).astype(BF16)
+    empty_ref[...] = jnp.dot(spread, counts, preferred_element_type=F32)
 
 
 def spread_of(center):
@@ -204,7 +214,7 @@
 
 
 def layer_kernel(
-    layer, last, ghosts, all_links, extended_ref, base_ref, own_ref, links_ref, edge_ref, node_ref, second_ref, bias_ref, gain_ref, *refs
+    layer, last, ghosts, all_links, extended_ref, base_ref, own_ref, empty_ref, links_ref, edge_ref, node_ref, second_ref, bias_ref, gain_ref, *refs
 ):
     landed, refs = refs[: len(all_links)], refs[len(all_links) :]
     if not last:
@@ -215,6 +225,8 @@
     rows = rows_total // tiles
 
     sender_mat = edge_ref[layer, 1]
+    table_rows = rows_total + 8 * ghosts
+    table_ref[pl.ds(table_rows, 8), :] = jnp.full((8, width), NOTHING, F32)
     table_ref[pl.ds(0, rows_total), :] = own_ref[...]
     if len(all_links) < 8:
         table_ref[pl.ds(rows_total, 8 * ghosts), :] = jnp.zeros((8 * ghosts, width), F32)
@@ -225,6 +237,7 @@
     bias_second = bias_ref[layer, pl.ds(1, 1), :]
     bias_second = bias_second - jnp.mean(bias_second, axis=-1, keepdims=True)
 
+    empty_message = -bias_second * lax.rsqrt(spread_of(bias_second) + width * 1e-5)
     gain_first = gain_ref[layer, pl.ds(0, 1), :] * math.sqrt(width)
     node_mat = jnp.concatenate([node_ref[layer, 0], node_ref[layer, 1]], axis=0)
 
@@ -249,7 +262,8 @@
             for slot in (pair, pair + 1):
                 senders = []
                 for tile in range(start // rows, start // rows + chunk_tiles):
-                    picked = table_ref[pl.ds(jnp.maximum(links_ref[slot, tile], 0), 1), :]
+                    row = links_ref[slot, tile]
+                    picked = table_ref[pl.ds(jnp.where(row >= 0, row, table_rows), 1), :]
                     senders.append(jnp.broadcast_to(picked, (rows, width)).astype(BF16))
                 halves.append(jnp.concatenate(senders, axis=0))
             base = base_ref[pl.ds(start, chunk_rows), pl.ds(pair * width, 2 * width)]
@@ -257,13 +271,12 @@
         for start in chunks:
             second = jnp.dot(hidden_ref[pl.ds(start, chunk_rows), :], second_ref[layer], preferred_element_type=F32)
             for place in range(0, chunk_rows, rows):
-                tile = (start + place) // rows
-                total = 0.0 if pair == 0 else total_ref[pl.ds(start + place, rows), :]
+                spot = pl.ds(start + place, rows)
+                total = empty_ref[spot, :] * empty_message if pair == 0 else total_ref[spot, :]
                 for half in range(2):
                     center = second[place : place + rows, half * width : (half + 1) * width] + bias_second
-                    limit = jnp.where(links_ref[pair + half, tile] >= 0, width * 1e-5, jnp.inf)
-                    total = total + center * lax.rsqrt(spread_of(center) + limit)
-                total_ref[pl.ds(start + place, rows), :] = total
+                    total = total + center * lax.rsqrt(spread_of(center) + width * 1e-5)
+                total_ref[spot, :] = total
     for start in range(0, rows_total, 256):
         update(start, total_ref[pl.ds(start, 256), :])
     if not last:
@@ -338,33 +351,34 @@
     for layer in range(layers):
         last = layer == layers - 1
         landed = exchange(sends, all_links, ghosts)
-        base, own = pl.pallas_call(
+        base, own, empty = pl.pallas_call(
             functools.partial(receive_kernel, layer),
             out_shape=[
                 jax.ShapeDtypeStruct((rows_total, slots * width), BF16),
                 jax.ShapeDtypeStruct((rows_total, width), F32),
+                jax.ShapeDtypeStruct((rows_total, width), F32),
             ],
-            in_specs=[VMEM] * 5,
-            out_specs=[VMEM] * 2,
+            in_specs=[VMEM] * 6,
+            out_specs=[VMEM] * 3,
             compiler_params=PARAMS,
             cost_estimate=pl.CostEstimate(flops=2_500_000_000, bytes_accessed=6_000_000, transcendentals=0),
             name="receive",
-        )(extended, turned, first_mats, edge_w, biases)
+        )(extended, turned, first_mats, edge_w, biases, tile_links)
         outs = [rows_of(rows_total)] + ([] if last else [rows_of(ghosts * len(group)) for group in groups])
         extra = [] if last else [wanted]
         extended, *sends = pl.pallas_call(
             functools.partial(layer_kernel, layer, last, ghosts, all_links),
             out_shape=outs,
-            in_specs=[VMEM] * 3 + [SMEM] + [VMEM] * (5 + len(all_links) + len(extra)),
+            in_specs=[VMEM] * 4 + [SMEM] + [VMEM] * (5 + len(all_links) + len(extra)),
             out_specs=[VMEM] * len(outs),
             scratch_shapes=[
-                pltpu.VMEM((table_rows, width), F32),
+                pltpu.VMEM((table_rows + 8, width), F32),
                 pltpu.VMEM((rows_total, 2 * width), BF16),
                 pltpu.VMEM((rows_total, width), F32),
             ],
             compiler_params=PARAMS,
             name="layer",
-        )(extended, base, own, tile_links, edge_w, node_w, second_mats, biases, gains, *landed, *extra)
+        )(extended, base, own, empty, tile_links, edge_w, node_w, second_mats, biases, gains, *landed, *extra)
     return extended[None, None]
 
 

time: 48.1 us -> 47.5 us (0.988)
  waiting for transfers between devices: 5.82 us -> 5.33 us
    pallas_call x2, Pallas kernels: 3.25 us -> 4.06 us  [body(): pl.pallas_call(functools.partial(receive_kernel, layer), out_shape=[jax.S...]
    pallas_call x2, Pallas kernels: 12.7 us -> 12.2 us  [body(): pl.pallas_call(functools.partial(layer_kernel, layer, last, ghosts, all_l...]
    ppermute x13, waiting for transfers between devices: 5.82 us -> 5.33 us  [swap(): return lax.ppermute(value, ('gx', 'gy'), pairs)]
  transfers between devices with their start and end apart: 13 -> 13, of which waited for: 4 -> 5; matrix products, arithmetic and copies ran while one was open for 2% -> 2% of each run, Pallas kernels for 8% -> 10%
where the time goes in v5:
time: 47.5 us; the launch traced here: 47.1 us
  Pallas kernels  19.9 us (42%)
  starting transfers between devices  17.3 us (36%)
  waiting for transfers between devices  5.33 us (11%)
  local copies, waits for them, and re-layouts  3.59 us (8%)
  other arithmetic  0.77 us (2%)
    ppermute x13, starting transfers between devices, swap(): return lax.ppermute(value, ('gx', 'gy'), pairs)  17.3 us
    pallas_call x2, Pallas kernels, body(): pl.pallas_call(functools.partial(layer_kernel, layer, last, ghosts, all_l...  12.2 us
    ppermute x13, waiting for transfers between devices, swap(): return lax.ppermute(value, ('gx', 'gy'), pairs)  5.33 us
    pallas_call x2, Pallas kernels, body(): pl.pallas_call(functools.partial(receive_kernel, layer), out_shape=[jax.S...  4.06 us
    unnamed x18, local copies, waits for them, and re-layouts  3.57 us
    pallas_call x1, Pallas kernels, body(): pl.pallas_call(functools.partial(pack_kernel, sides), out_shape=[rows_of(...  2.32 us
  transfers between devices with their start and end apart: 13, of which 5 were waited for; matrix products, arithmetic and copies ran while one was open for 2% of the time, Pallas kernels for 10%

profile of v5, /device:TPU:8, one launch (start us, length us, event | category | flops | bytes accessed | tf_op | source)
XLA Modules:
  0.0 47.1 jit_solution(1457397572931051558)
XLA Ops:
  0.0 2.3 %pack.1 = (bf16[1024,128]{1,0:T(8,128)(2,1)}, bf16[64,128]{1,0:T(8,128)(2,1)}, bf16[64,128]{1,0:T(8,128)(2,1)}, bf16[64,128]{1,0:T(8,128)(2,1)}) custom-call(bf16[1024,128]{1,0:T(8,128)(2,1)} %bitcast.14, s32[4,64]{1,0:T(4,128)} %bitcast.15, s32[4]{0:T(128)} %bitcast.16), custom_call_target="tpu_custom_call" | custom-call | tf_op jit(solution)/shard_map/pack/pallas_call | solution.py:303
  2.4 2.9 %collective-permute-start = (bf16[64,128]{1,0:T(8,128)(2,1)}, bf16[64,128]{1,0:T(8,128)(2,1)S(1)}, u32[]{:S(2)}, u32[]{:S(2)}) collective-permute-start(bf16[64,128]{1,0:T(8,128)(2,1)} %get-tuple-element.30), channel_id=1, source_target_pairs={{2,4},{3,5},{4,2},{5,3},{6,8},{7,9},{8,6},{9,7},{10,12},{11,13},{1... | collective-permute-start | bytes 49160 | tf_op jit(solution)/shard_map/ppermute | solution.py:64
  5.3 0.9 %collective-permute-start.1 = (bf16[64,128]{1,0:T(8,128)(2,1)}, bf16[64,128]{1,0:T(8,128)(2,1)S(1)}, u32[]{:S(2)}, u32[]{:S(2)}) collective-permute-start(bf16[64,128]{1,0:T(8,128)(2,1)} %get-tuple-element.31), channel_id=1, source_target_pairs={{0,2},{1,3},{2,0},{3,1},{4,6},{5,7},{6,4},{7,5},{8,10},{9,11},{10,... | collective-permute-start | bytes 49160 | tf_op jit(solution)/shard_map/ppermute | solution.py:64
  6.1 1.5 %collective-permute-start.2 = (bf16[64,128]{1,0:T(8,128)(2,1)}, bf16[64,128]{1,0:T(8,128)(2,1)S(1)}, u32[]{:S(2)}, u32[]{:S(2)}) collective-permute-start(bf16[64,128]{1,0:T(8,128)(2,1)} %get-tuple-element.32), channel_id=1, source_target_pairs={{0,1},{1,0},{2,3},{3,2},{4,5},{5,4},{6,7},{7,6},{8,9},{9,8},{10,11... | collective-permute-start | bytes 49160 | tf_op jit(solution)/shard_map/ppermute | solution.py:64
  7.6 0.8 %bitcast_select_fusion.rows_ref = s32[8,256]{1,0:T(8,128)S(1)} fusion(s32[1,1,8,256]{3,2,1,0:T(8,128)} %param.15, s32[8]{0:T(128)} %bitcast.17), kind=kLoop, calls=%fused_computation | loop fusion | flops 4096 | bytes 16416 | tf_op jit(solution)/shard_map/jit(_where)/select_n | solution.py:317
  8.4 0.9 %copy-done.7 = bf16[1024,128]{1,0:T(8,128)(2,1)S(1)} copy-done((bf16[1024,128]{1,0:T(8,128)(2,1)S(1)}, bf16[1024,128]{1,0:T(8,128)(2,1)}, u32[]{:S(2)}) %copy-start.7) | copy-done | bytes 262168
  10.1 0.7 %build.1 = (bf16[1280,128]{1,0:T(8,128)(2,1)S(1)}, bf16[512,128]{1,0:T(8,128)(2,1)S(1)}, bf16[512,128]{1,0:T(8,128)(2,1)S(1)}, bf16[256,128]{1,0:T(8,128)(2,1)S(1)}) custom-call(bf16[1024,128]{1,0:T(8,128)(2,1)S(1)} %get-tuple-element.29.retained_ref, bf16[64,128]{1,0:T(8,128)(2,1)S(1)} %collective-permute-done.refs_0_, ...), custom_call_target="tpu_custom_call" | custom-call | tf_op jit(solution)/shard_map/build/pallas_call | solution.py:328
  10.8 2.2 %collective-permute-start.3 = (bf16[512,128]{1,0:T(8,128)(2,1)S(1)}, bf16[512,128]{1,0:T(8,128)(2,1)S(1)}, u32[]{:S(2)}, u32[]{:S(2)}) collective-permute-start(bf16[512,128]{1,0:T(8,128)(2,1)S(1)} %get-tuple-element.41), channel_id=1, source_target_pairs={{2,4},{3,5},{4,2},{5,3},{6,8},{7,9},{8,6},{9,7},{10,12},{11,13},{1... | collective-permute-start | bytes 393224 | tf_op jit(solution)/shard_map/ppermute | solution.py:64
  13.1 1.2 %collective-permute-start.5 = (bf16[512,128]{1,0:T(8,128)(2,1)S(1)}, bf16[512,128]{1,0:T(8,128)(2,1)S(1)}, u32[]{:S(2)}, u32[]{:S(2)}) collective-permute-start(bf16[512,128]{1,0:T(8,128)(2,1)S(1)} %get-tuple-element.42), channel_id=1, source_target_pairs={{0,1},{1,0},{2,3},{3,2},{4,5},{5,4},{6,7},{7,6},{8,9},{9,8},{10,11... | collective-permute-start | bytes 393224 | tf_op jit(solution)/shard_map/ppermute | solution.py:64
  14.3 1.3 %collective-permute-start.7 = (bf16[256,128]{1,0:T(8,128)(2,1)S(1)}, bf16[256,128]{1,0:T(8,128)(2,1)S(1)}, u32[]{:S(2)}, u32[]{:S(2)}) collective-permute-start(bf16[256,128]{1,0:T(8,128)(2,1)S(1)} %get-tuple-element.43), channel_id=1, source_target_pairs={{0,2},{1,3},{2,0},{3,1},{4,6},{5,7},{6,4},{7,5},{8,10},{9,11},{10,... | collective-permute-start | bytes 196616 | tf_op jit(solution)/shard_map/ppermute | solution.py:64
  15.6 0.9 %copy-done = bf16[2,3,128,128]{3,2,1,0:T(8,128)(2,1)S(1)} copy-done((bf16[2,3,128,128]{3,2,1,0:T(8,128)(2,1)S(1)}, bf16[2,3,128,128]{3,2,1,0:T(8,128)(2,1)}, u32[]{:S(2)}) %copy-start) | copy-done | bytes 196632
  16.6 1.0 %copy-done.6 = f32[1,1,4,16,1280]{4,3,2,1,0:T(8,128)S(1)} copy-done((f32[1,1,4,16,1280]{4,3,2,1,0:T(8,128)S(1)}, f32[1,1,4,16,1280]{4,3,2,1,0:T(8,128)}, u32[]{:S(2)}) %copy-start.6) | copy-done | bytes 327704
  17.5 0.7 %copy-done.8 = f32[2,4,128]{2,1,0:T(4,128)S(1)} copy-done((f32[2,4,128]{2,1,0:T(4,128)S(1)}, f32[2,4,128]{2,1,0:T(4,128)}, u32[]{:S(2)}) %copy-start.8) | copy-done | bytes 4120
  18.7 0.9 %collective-permute-start.4 = (bf16[256,128]{1,0:T(8,128)(2,1)S(1)}, bf16[256,128]{1,0:T(8,128)(2,1)S(1)}, u32[]{:S(2)}, u32[]{:S(2)}) collective-permute-start(bf16[256,128]{1,0:T(8,128)(2,1)S(1)} %slice.16), channel_id=1, source_target_pairs={{0,1},{1,0},{2,3},{3,2},{4,5},{5,4},{6,7},{7,6},{8,9},{9,8},{10,11... | collective-permute-start | bytes 196616 | tf_op jit(solution)/shard_map/ppermute | solution.py:64
  20.0 2.0 %receive.2 = (bf16[1280,2048]{1,0:T(8,128)(2,1)S(1)}, f32[1280,128]{1,0:T(8,128)S(1)}, f32[1280,128]{1,0:T(8,128)S(1)}) custom-call(bf16[1280,128]{1,0:T(8,128)(2,1)S(1)} %get-tuple-element.34.extended_ref, bf16[1280,128]{1,0:T(8,128)(2,1)S(1)} %get-tuple-element.35.turned_ref, bf16[2,256,2048]{2,1,0:T(8,128)(2,1)S(1)} %get-tuple-element.36.first_ref, ...), custom_call_target="tpu_custom_call" | custom-call | flops 2500000000 | bytes 6000000 | tf_op jit(solution)/shard_map/receive/pallas_call | solution.py:354
  22.0 1.0 %collective-permute-done.4.refs_0_ = bf16[256,128]{1,0:T(8,128)(2,1)S(1)} collective-permute-done((bf16[256,128]{1,0:T(8,128)(2,1)S(1)}, bf16[256,128]{1,0:T(8,128)(2,1)S(1)}, u32[]{:S(2)}, u32[]{:S(2)}) %collective-permute-start.4) | collective-permute-done | bytes 65568 | tf_op jit(solution)/shard_map/ppermute | solution.py:64
  23.0 6.0 %layer.2 = (bf16[1280,128]{1,0:T(8,128)(2,1)S(1)}, bf16[512,128]{1,0:T(8,128)(2,1)S(1)}, bf16[512,128]{1,0:T(8,128)(2,1)S(1)}, bf16[256,128]{1,0:T(8,128)(2,1)S(1)}) custom-call(bf16[1280,128]{1,0:T(8,128)(2,1)S(1)} %get-tuple-element.34.extended_ref, bf16[1280,2048]{1,0:T(8,128)(2,1)S(1)} %get-tuple-element.37.base_ref, ...), custom_call_target="tpu_custom_call" | custom-call | tf_op jit(solution)/shard_map/layer/pallas_call | solution.py:369
  29.0 2.7 %collective-permute-start.8 = (bf16[512,128]{1,0:T(8,128)(2,1)S(1)}, bf16[512,128]{1,0:T(8,128)(2,1)S(1)}, u32[]{:S(2)}, u32[]{:S(2)}) collective-permute-start(bf16[512,128]{1,0:T(8,128)(2,1)S(1)} %get-tuple-element.48), channel_id=1, source_target_pairs={{2,4},{3,5},{4,2},{5,3},{6,8},{7,9},{8,6},{9,7},{10,12},{11,13},{1... | collective-permute-start | bytes 393224 | tf_op jit(solution)/shard_map/ppermute | solution.py:64
  31.8 0.8 %collective-permute-start.10 = (bf16[512,128]{1,0:T(8,128)(2,1)S(1)}, bf16[512,128]{1,0:T(8,128)(2,1)S(1)}, u32[]{:S(2)}, u32[]{:S(2)}) collective-permute-start(bf16[512,128]{1,0:T(8,128)(2,1)S(1)} %get-tuple-element.49), channel_id=1, source_target_pairs={{0,1},{1,0},{2,3},{3,2},{4,5},{5,4},{6,7},{7,6},{8,9},{9,8},{10,11... | collective-permute-start | bytes 393224 | tf_op jit(solution)/shard_map/ppermute | solution.py:64
  32.6 1.2 %collective-permute-start.12 = (bf16[256,128]{1,0:T(8,128)(2,1)S(1)}, bf16[256,128]{1,0:T(8,128)(2,1)S(1)}, u32[]{:S(2)}, u32[]{:S(2)}) collective-permute-start(bf16[256,128]{1,0:T(8,128)(2,1)S(1)} %get-tuple-element.50), channel_id=1, source_target_pairs={{0,2},{1,3},{2,0},{3,1},{4,6},{5,7},{6,4},{7,5},{8,10},{9,11},{10,... | collective-permute-start | bytes 196616 | tf_op jit(solution)/shard_map/ppermute | solution.py:64
  33.8 2.5 %collective-permute-done.8.refs_1_ = bf16[512,128]{1,0:T(8,128)(2,1)S(1)} collective-permute-done((bf16[512,128]{1,0:T(8,128)(2,1)S(1)}, bf16[512,128]{1,0:T(8,128)(2,1)S(1)}, u32[]{:S(2)}, u32[]{:S(2)}) %collective-permute-start.8) | collective-permute-done | bytes 131104 | tf_op jit(solution)/shard_map/ppermute | solution.py:64
  36.3 1.2 %collective-permute-start.9 = (bf16[256,128]{1,0:T(8,128)(2,1)S(1)}, bf16[256,128]{1,0:T(8,128)(2,1)S(1)}, u32[]{:S(2)}, u32[]{:S(2)}) collective-permute-start(bf16[256,128]{1,0:T(8,128)(2,1)S(1)} %slice.18), channel_id=1, source_target_pairs={{0,1},{1,0},{2,3},{3,2},{4,5},{5,4},{6,7},{7,6},{8,9},{9,8},{10,11... | collective-permute-start | bytes 196616 | tf_op jit(solution)/shard_map/ppermute | solution.py:64
  38.3 2.0 %receive.3 = (bf16[1280,2048]{1,0:T(8,128)(2,1)S(1)}, f32[1280,128]{1,0:T(8,128)S(1)}, f32[1280,128]{1,0:T(8,128)S(1)}) custom-call(bf16[1280,128]{1,0:T(8,128)(2,1)S(1)} %get-tuple-element.44.extended_ref, bf16[1280,128]{1,0:T(8,128)(2,1)S(1)} %get-tuple-element.35.turned_ref, bf16[2,256,2048]{2,1,0:T(8,128)(2,1)S(1)} %get-tuple-element.36.first_ref, ...), custom_call_target="tpu_custom_call" | custom-call | flops 2500000000 | bytes 6000000 | tf_op jit(solution)/shard_map/receive/pallas_call | solution.py:354
  40.9 6.2 %layer.3 = bf16[1280,128]{1,0:T(8,128)(2,1)} custom-call(bf16[1280,128]{1,0:T(8,128)(2,1)S(1)} %get-tuple-element.44.extended_ref, bf16[1280,2048]{1,0:T(8,128)(2,1)S(1)} %get-tuple-element.45.base_ref, f32[1280,128]{1,0:T(8,128)S(1)} %get-tuple-element.46.own_ref, f32[1280,128]{1,0:T(8,128)S(1)} %get-tuple-element.47.empty_ref, s32[16,80]{1,0:T(8,128)S(1)} %bitcast.12, ...), custom_call_target="tpu_custom_call" | custom-call | tf_op jit(solution)/shard_map/layer/pallas_call | solution.py:369
  (33 shorter events, 3.0 us)
Async XLA Ops:
  2.3 17.7 %copy-start.1 = (bf16[2,3,128,128]{3,2,1,0:T(8,128)(2,1)S(1)}, bf16[2,3,128,128]{3,2,1,0:T(8,128)(2,1)}, u32[]{:S(2)}) copy-start(bf16[2,3,128,128]{3,2,1,0:T(8,128)(2,1)} %edge_ref.9) | copy-start | bytes 589828
  2.3 17.6 %copy-start.3 = (s32[1,1,16,80]{3,2,1,0:T(8,128)S(1)}, s32[1,1,16,80]{3,2,1,0:T(8,128)}, u32[]{:S(2)}) copy-start(s32[1,1,16,80]{3,2,1,0:T(8,128)} %param.17) | copy-start | bytes 15364
  2.4 17.6 %copy-start.4 = (f32[2,4,128]{2,1,0:T(4,128)S(1)}, f32[2,4,128]{2,1,0:T(4,128)}, u32[]{:S(2)}) copy-start(f32[2,4,128]{2,1,0:T(4,128)} %bias_ref.7) | copy-start | bytes 12292
  2.4 7.2 %collective-permute-start = (bf16[64,128]{1,0:T(8,128)(2,1)}, bf16[64,128]{1,0:T(8,128)(2,1)S(1)}, u32[]{:S(2)}, u32[]{:S(2)}) collective-permute-start(bf16[64,128]{1,0:T(8,128)(2,1)} %get-tuple-element.30), channel_id=1, source_target_pairs={{2,4},{3,5},{4,2},{5,3},{6,8},{7,9},{8,6},{9,7},{10,12},{11,13},{1... | collective-permute-start | bytes 49160 | tf_op jit(solution)/shard_map/ppermute | solution.py:64
  5.3 4.3 %collective-permute-start.1 = (bf16[64,128]{1,0:T(8,128)(2,1)}, bf16[64,128]{1,0:T(8,128)(2,1)S(1)}, u32[]{:S(2)}, u32[]{:S(2)}) collective-permute-start(bf16[64,128]{1,0:T(8,128)(2,1)} %get-tuple-element.31), channel_id=1, source_target_pairs={{0,2},{1,3},{2,0},{3,1},{4,6},{5,7},{6,4},{7,5},{8,10},{9,11},{10,... | collective-permute-start | bytes 49160 | tf_op jit(solution)/shard_map/ppermute | solution.py:64
  6.1 3.9 %collective-permute-start.2 = (bf16[64,128]{1,0:T(8,128)(2,1)}, bf16[64,128]{1,0:T(8,128)(2,1)S(1)}, u32[]{:S(2)}, u32[]{:S(2)}) collective-permute-start(bf16[64,128]{1,0:T(8,128)(2,1)} %get-tuple-element.32), channel_id=1, source_target_pairs={{0,1},{1,0},{2,3},{3,2},{4,5},{5,4},{6,7},{7,6},{8,9},{9,8},{10,11... | collective-permute-start | bytes 49160 | tf_op jit(solution)/shard_map/ppermute | solution.py:64
  8.4 1.0 %copy-start.7 = (bf16[1024,128]{1,0:T(8,128)(2,1)S(1)}, bf16[1024,128]{1,0:T(8,128)(2,1)}, u32[]{:S(2)}) copy-start(bf16[1024,128]{1,0:T(8,128)(2,1)} %get-tuple-element.28.retained_ref) | copy-start | bytes 786436
  10.8 7.9 %collective-permute-start.3 = (bf16[512,128]{1,0:T(8,128)(2,1)S(1)}, bf16[512,128]{1,0:T(8,128)(2,1)S(1)}, u32[]{:S(2)}, u32[]{:S(2)}) collective-permute-start(bf16[512,128]{1,0:T(8,128)(2,1)S(1)} %get-tuple-element.41), channel_id=1, source_target_pairs={{2,4},{3,5},{4,2},{5,3},{6,8},{7,9},{8,6},{9,7},{10,12},{11,13},{1... | collective-permute-start | bytes 393224 | tf_op jit(solution)/shard_map/ppermute | solution.py:64
  13.1 6.5 %collective-permute-start.5 = (bf16[512,128]{1,0:T(8,128)(2,1)S(1)}, bf16[512,128]{1,0:T(8,128)(2,1)S(1)}, u32[]{:S(2)}, u32[]{:S(2)}) collective-permute-start(bf16[512,128]{1,0:T(8,128)(2,1)S(1)} %get-tuple-element.42), channel_id=1, source_target_pairs={{0,1},{1,0},{2,3},{3,2},{4,5},{5,4},{6,7},{7,6},{8,9},{9,8},{10,11... | collective-permute-start | bytes 393224 | tf_op jit(solution)/shard_map/ppermute | solution.py:64
  14.3 7.7 %collective-permute-start.7 = (bf16[256,128]{1,0:T(8,128)(2,1)S(1)}, bf16[256,128]{1,0:T(8,128)(2,1)S(1)}, u32[]{:S(2)}, u32[]{:S(2)}) collective-permute-start(bf16[256,128]{1,0:T(8,128)(2,1)S(1)} %get-tuple-element.43), channel_id=1, source_target_pairs={{0,2},{1,3},{2,0},{3,1},{4,6},{5,7},{6,4},{7,5},{8,10},{9,11},{10,... | collective-permute-start | bytes 196616 | tf_op jit(solution)/shard_map/ppermute | solution.py:64
  15.6 0.9 %copy-start = (bf16[2,3,128,128]{3,2,1,0:T(8,128)(2,1)S(1)}, bf16[2,3,128,128]{3,2,1,0:T(8,128)(2,1)}, u32[]{:S(2)}) copy-start(bf16[2,3,128,128]{3,2,1,0:T(8,128)(2,1)} %edge_ref.9) | copy-start | bytes 589828
  16.6 1.0 %copy-start.6 = (f32[1,1,4,16,1280]{4,3,2,1,0:T(8,128)S(1)}, f32[1,1,4,16,1280]{4,3,2,1,0:T(8,128)}, u32[]{:S(2)}) copy-start(f32[1,1,4,16,1280]{4,3,2,1,0:T(8,128)} %param.18) | copy-start | bytes 983044
  17.5 0.7 %copy-start.8 = (f32[2,4,128]{2,1,0:T(4,128)S(1)}, f32[2,4,128]{2,1,0:T(4,128)}, u32[]{:S(2)}) copy-start(f32[2,4,128]{2,1,0:T(4,128)} %geo_ref.1) | copy-start | bytes 12292
  18.6 4.4 %copy-start.2 = (bf16[2,3,128,128]{3,2,1,0:T(8,128)(2,1)S(1)}, bf16[2,3,128,128]{3,2,1,0:T(8,128)(2,1)}, u32[]{:S(2)}) copy-start(bf16[2,3,128,128]{3,2,1,0:T(8,128)(2,1)} %node_ref.3) | copy-start | bytes 589828
  18.7 4.4 %copy-start.5 = (f32[2,2,128]{2,1,0:T(2,128)S(1)}, f32[2,2,128]{2,1,0:T(2,128)}, u32[]{:S(2)}) copy-start(f32[2,2,128]{2,1,0:T(2,128)} %gain_ref.3) | copy-start | bytes 6148
  18.7 4.3 %collective-permute-start.4 = (bf16[256,128]{1,0:T(8,128)(2,1)S(1)}, bf16[256,128]{1,0:T(8,128)(2,1)S(1)}, u32[]{:S(2)}, u32[]{:S(2)}) collective-permute-start(bf16[256,128]{1,0:T(8,128)(2,1)S(1)} %slice.16), channel_id=1, source_target_pairs={{0,1},{1,0},{2,3},{3,2},{4,5},{5,4},{6,7},{7,6},{8,9},{9,8},{10,11... | collective-permute-start | bytes 196616 | tf_op jit(solution)/shard_map/ppermute | solution.py:64
  19.6 3.4 %collective-permute-start.6 = (bf16[256,128]{1,0:T(8,128)(2,1)S(1)}, bf16[256,128]{1,0:T(8,128)(2,1)S(1)}, u32[]{:S(2)}, u32[]{:S(2)}) collective-permute-start(bf16[256,128]{1,0:T(8,128)(2,1)S(1)} %slice.17), channel_id=1, source_target_pairs={{0,2},{1,3},{2,0},{3,1},{4,6},{5,7},{6,4},{7,5},{8,10},{9,11},{10,... | collective-permute-start | bytes 196616 | tf_op jit(solution)/shard_map/ppermute | solution.py:64
  29.0 7.3 %collective-permute-start.8 = (bf16[512,128]{1,0:T(8,128)(2,1)S(1)}, bf16[512,128]{1,0:T(8,128)(2,1)S(1)}, u32[]{:S(2)}, u32[]{:S(2)}) collective-permute-start(bf16[512,128]{1,0:T(8,128)(2,1)S(1)} %get-tuple-element.48), channel_id=1, source_target_pairs={{2,4},{3,5},{4,2},{5,3},{6,8},{7,9},{8,6},{9,7},{10,12},{11,13},{1... | collective-permute-start | bytes 393224 | tf_op jit(solution)/shard_map/ppermute | solution.py:64
  31.8 6.4 %collective-permute-start.10 = (bf16[512,128]{1,0:T(8,128)(2,1)S(1)}, bf16[512,128]{1,0:T(8,128)(2,1)S(1)}, u32[]{:S(2)}, u32[]{:S(2)}) collective-permute-start(bf16[512,128]{1,0:T(8,128)(2,1)S(1)} %get-tuple-element.49), channel_id=1, source_target_pairs={{0,1},{1,0},{2,3},{3,2},{4,5},{5,4},{6,7},{7,6},{8,9},{9,8},{10,11... | collective-permute-start | bytes 393224 | tf_op jit(solution)/shard_map/ppermute | solution.py:64
  32.6 7.7 %collective-permute-start.12 = (bf16[256,128]{1,0:T(8,128)(2,1)S(1)}, bf16[256,128]{1,0:T(8,128)(2,1)S(1)}, u32[]{:S(2)}, u32[]{:S(2)}) collective-permute-start(bf16[256,128]{1,0:T(8,128)(2,1)S(1)} %get-tuple-element.50), channel_id=1, source_target_pairs={{0,2},{1,3},{2,0},{3,1},{4,6},{5,7},{6,4},{7,5},{8,10},{9,11},{10,... | collective-permute-start | bytes 196616 | tf_op jit(solution)/shard_map/ppermute | solution.py:64
  36.3 4.6 %collective-permute-start.9 = (bf16[256,128]{1,0:T(8,128)(2,1)S(1)}, bf16[256,128]{1,0:T(8,128)(2,1)S(1)}, u32[]{:S(2)}, u32[]{:S(2)}) collective-permute-start(bf16[256,128]{1,0:T(8,128)(2,1)S(1)} %slice.18), channel_id=1, source_target_pairs={{0,1},{1,0},{2,3},{3,2},{4,5},{5,4},{6,7},{7,6},{8,9},{9,8},{10,11... | collective-permute-start | bytes 196616 | tf_op jit(solution)/shard_map/ppermute | solution.py:64
  38.2 2.8 %collective-permute-start.11 = (bf16[256,128]{1,0:T(8,128)(2,1)S(1)}, bf16[256,128]{1,0:T(8,128)(2,1)S(1)}, u32[]{:S(2)}, u32[]{:S(2)}) collective-permute-start(bf16[256,128]{1,0:T(8,128)(2,1)S(1)} %slice.19), channel_id=1, source_target_pairs={{0,2},{1,3},{2,0},{3,1},{4,6},{5,7},{6,4},{7,5},{8,10},{9,11},{10,... | collective-permute-start | bytes 196616 | tf_op jit(solution)/shard_map/ppermute | solution.py:64
